TPU v7x, 128 devices: a whole 4x4x4 slice. The times are simulated.
128 devices in a mesh: dp: 8 (over z_lo, x), tensor: 16 (over y, z_hi, core).
Axes of the slice: x: 4, y: 4, z: 4 (z_hi: 2, z_lo: 2; z = z_hi * 2 + z_lo), core: 2. Of those that a mesh axis runs over, the one named last changes fastest.
Arguments:
- cotangent: bfloat16 [16384, 4096], P(('dp', 'tensor')), may hold values from -4 to 4
- mixer_out: bfloat16 [16384, 8192], P('dp', 'tensor'), may hold values from -60 to 60, as said below
- gate: bfloat16 [16384, 8192], P('dp', 'tensor'), may hold values from -6 to 6
- norm_gain: float32 [8192], P('tensor'), may hold values from 0.5 to 1.5
- out_weight: bfloat16 [8192, 4096], P('tensor'), may hold values from -0.0625 to 0.0625
- old_master: float32 [16, 768, 4096], P('tensor', 'dp'), may hold values from -0.3125 to 0.3125
- old_first: float32 [16, 768, 4096], P('tensor', 'dp'), may hold values from -6 to 6
- old_second: float32 [16, 768, 4096], P('tensor', 'dp'), may hold values from 0.5 to 20
- old_bounds: int32 [16, 9], P('tensor'), may hold values from 0 to 512, as said below
- new_bounds: int32 [16, 9], P('tensor'), may hold values from 0 to 512, as said below
Outputs:
- new_master: float32 [16, 768, 4096], P('tensor', 'dp')
- new_first: float32 [16, 768, 4096], P('tensor', 'dp')
- new_second: float32 [16, 768, 4096], P('tensor', 'dp')
- input_grad: bfloat16 [16384, 8192], P('dp', 'tensor')
- gate_grad: bfloat16 [16384, 8192], P('dp', 'tensor')
Inputs may be any that keep to these rules, and one draw needn't show every extreme that they name: `mixer_out`: the scan's channel values. `old_bounds`: row t starts at 0, ends at 512 and never falls; old_bounds[t, j] - j * 64 lies in -16 to 0; an old share holds at most 80 rows, and in every row of the table one share holds exactly that many. `new_bounds`: row t starts at 0, ends at 512 and never falls; new_bounds[t, j] - old_bounds[t, j] lies in 0 to 16 and equals 16 for some j in every row; new_bounds[t, j] - j * 64 lies in -16 to 16, both ends reached in every row; a new share holds at most 96 rows, exactly 96 for some j in every row.
All inputs are finite; a program needn't handle non-finite values.
Results may differ from a plain program's by a relative error of at most 0.001.
Values may be sent and summed in bfloat16 or wider, within the bound.
No kernel may reach another device: no remote copies, remote signals or barrier semaphores. Data moves between devices by JAX's collectives and lax.ppermute only.
A program may use at most 192 MiB of HBM per device.

v0:
```python
import jax
import jax.numpy as jnp
from jax import lax
from jax.sharding import PartitionSpec as P

GROUP = 2048


norm_eps = 1e-05
beta_one = 0.9
beta_two = 0.95
adam_eps = 1e-08
learn_rate = 0.0003
weight_decay = 0.1
adam_step = 1000.0


def partner(value, axis, stride):
    mask = 2**stride
    pairs = [(source, source ^ mask) for source in range(lax.axis_size(axis))]
    return lax.ppermute(value, axis, pairs)


def passed_along(shard, axis, by):
    length = lax.axis_size(axis)
    pairs = [(i, i + by) for i in range(length) if 0 <= i + by < length]
    return lax.ppermute(shard, axis, pairs)


def adam_update(master, first, second, grad):
    first_new = beta_one * first + (1.0 - beta_one) * grad
    second_new = beta_two * second + (1.0 - beta_two) * grad * grad
    corr_one = 1.0 - beta_one**adam_step
    corr_two = 1.0 - beta_two**adam_step
    update = first_new / corr_one / (jnp.sqrt(second_new / corr_two) + adam_eps)
    return (master - learn_rate * (update + weight_decay * master), first_new, second_new)


def local(
    cotangent,
    mixer_out,
    gate,
    norm_gain,
    out_weight,
    old_master,
    old_first,
    old_second,
    old_bounds,
    new_bounds,
):
    dp_count = lax.axis_size("dp")
    dp_index = lax.axis_index("dp")
    row_count = out_weight.shape[0]
    model_width = out_weight.shape[1]
    per_group = GROUP // row_count

    def group_mean(values):
        group_total = jnp.sum(values, axis=1)
        for bit_index in range(per_group.bit_length() - 1):
            group_total = group_total + partner(group_total, "tensor", bit_index)
        return (group_total / GROUP)[:, None]

    mixer_value = mixer_out.astype(jnp.float32)
    gate_value = gate.astype(jnp.float32)
    sigmoid_gate = jax.nn.sigmoid(gate_value)
    activated = gate_value * sigmoid_gate
    slope = sigmoid_gate * (1.0 + gate_value * (1.0 - sigmoid_gate))
    gated = mixer_value * activated
    inverse = lax.rsqrt(group_mean(gated * gated) + norm_eps)
    normed = gated * inverse
    hidden = (normed * norm_gain).astype(jnp.bfloat16)
    arrived = lax.all_gather(cotangent, "tensor", axis=0, tiled=True)
    grad_sum = lax.dot_general(
        hidden, arrived, (((0,), (0,)), ((), ())), preferred_element_type=jnp.float32
    )
    product = lax.dot_general(
        arrived, out_weight, (((1,), (1,)), ((), ())), preferred_element_type=jnp.float32
    )
    scaled = product * norm_gain
    centre = group_mean(scaled * normed)
    gated_back = inverse * (scaled - normed * centre)
    input_grad = (gated_back * activated).astype(jnp.bfloat16)
    gate_grad = (gated_back * mixer_value * slope).astype(jnp.bfloat16)
    capacity = old_master.shape[1]
    share_rows = row_count // dp_count
    spill_rows = share_rows // 4
    new_row = new_bounds[0]
    old_row = old_bounds[0]
    new_start = new_row[dp_index]
    new_count = new_row[dp_index + 1] - new_start
    zero_rows = jnp.zeros((capacity, model_width), jnp.float32)
    summed_grad = lax.psum(grad_sum, "dp")
    owned = lax.dynamic_slice_in_dim(
        jnp.concatenate([summed_grad, zero_rows], axis=0), new_start, capacity, 0
    )
    grad_rows = owned / dp_count
    old_start = old_row[dp_index]
    old_count = old_row[dp_index + 1] - old_start
    moved_rows = new_start - old_start
    kept_rows = old_count - moved_rows
    states = (old_master[0], old_first[0], old_second[0])
    arrived_state = passed_along(
        (states[0][:spill_rows], states[1][:spill_rows], states[2][:spill_rows]), "dp", -1
    )
    slot_index = jnp.arange(capacity, dtype=jnp.int32)
    source_row = jnp.where(
        slot_index < kept_rows, moved_rows + slot_index, capacity + slot_index - kept_rows
    )
    source_row = jnp.clip(source_row, 0, capacity + spill_rows - 1)
    placed = [
        jnp.take(jnp.concatenate([own_state, extra_rows], axis=0), source_row, axis=0)
        for own_state, extra_rows in zip(states, arrived_state)
    ]
    master_new, first_new, second_new = adam_update(placed[0], placed[1], placed[2], grad_rows)
    valid = (slot_index < new_count)[:, None]
    return (
        jnp.where(valid, master_new, 0.0)[None],
        jnp.where(valid, first_new, 0.0)[None],
        jnp.where(valid, second_new, 0.0)[None],
        input_grad,
        gate_grad,
    )


def solution(mesh):
    return jax.shard_map(
        local,
        mesh=mesh,
        in_specs=(
            P(("dp", "tensor"), None),
            P("dp", "tensor"),
            P("dp", "tensor"),
            P("tensor"),
            P("tensor", None),
            P("tensor", "dp", None),
            P("tensor", "dp", None),
            P("tensor", "dp", None),
            P("tensor", None),
            P("tensor", None),
        ),
        out_specs=(
            P("tensor", "dp", None),
            P("tensor", "dp", None),
            P("tensor", "dp", None),
            P("dp", "tensor"),
            P("dp", "tensor"),
        ),
        check_vma=False,
    )
```

profile of v0, /device:TPU:6, one launch (start us, length us, event | category | flops | bytes accessed | tf_op | source)
XLA Modules:
  0.0 347.0 jit_solution(8908622829589761948)
XLA Ops:
  7.2 0.0 all-gather.2.cloned.1.call-start
  7.2 0.7 all-gather.2.cloned.1.call-update
  7.9 0.0 all-reduce.3.cloned.1.call-start
  7.9 2.9 copy.15
  10.9 0.0 copy-start.1
  10.9 4.5 %copy.16 = bf16[2048,512]{0,1:T(8,128)(2,1)} copy(bf16[2048,512]{1,0:T(8,128)(2,1)} %param.14) | data formatting | bytes 4194304 | tf_op args[2]
  15.4 0.0 copy-start.8
  15.4 3.2 multiply_reduce_fusion.1
  18.6 0.1 collective-permute-start.2
  18.7 1.2 collective-permute-done.2
  19.9 3.9 %collective-permute-start.3 = (f32[2048]{0:T(1024)S(1)}, f32[2048]{0:T(1024)S(1)}, u32[]{:S(2)}, u32[]{:S(2)}) collective-permute-start(f32[2048]{0:T(1024)S(1)} %add.87), channel_id=1, source_target_pairs={{0,2},{1,3},{2,0},{3,1},{4,6},{5,7},{6,4},{7,5},{8,10},{9,11},{10,... | collective-permute-start | bytes 24584 | tf_op jit(solution)/shard_map/ppermute | solution.py:21
  23.8 1.6 collective-permute-done.3
  25.4 97.8 %all-gather.2.cloned.1.call-done = bf16[2048,4096]{1,0:T(8,128)(2,1)} async-done(((bf16[128,4096]{1,0:T(8,128)(2,1)}), bf16[2048,4096]{1,0:T(8,128)(2,1)}) %all-gather.2.cloned.1.call-update) | async-done | bytes 16777232 | tf_op jit(solution)/shard_map/all_gather | solution.py:72
  123.3 0.0 copy-done.1
  123.3 0.0 copy-done.8
  123.3 16.1 %fusion.7 = f32[512,4096]{1,0:T(8,128)} fusion(bf16[2048,4096]{1,0:T(8,128)(2,1)} %all-gather.2.cloned.1.call-done, f32[512]{0:T(512)S(1)} %copy-done.8, bf16[2048,512]{0,1:T(8,128)(2,1)S(1)} %copy.15, f32[2048]{0:T(1024)S(1)} %add_rsqrt_fusion, bf16[2048,512]{0,1:T(8,128)(2,1)} %copy.16), kind=kOutput, calls=%fused_computation.21 | convolution fusion | flops 8600420352 | bytes 29370368 | tf_op jit(solution)/shard_map/dot_general | solution.py:73
  139.4 0.0 copy-start.2
  139.4 0.0 copy-start.6
  139.4 0.0 copy-start.7
  139.4 0.0 all-reduce.3.cloned.1.call-update
  139.4 1.4 copy-done.2
  140.8 2.8 collective-permute-start.4
  143.6 1.7 slice_bitcast_fusion.1
  145.3 2.5 collective-permute-start.1
  147.7 1.7 slice_bitcast_fusion.2
  149.4 2.6 collective-permute-start
  152.0 0.0 copy-done.6
  152.1 0.0 copy-done.7
  152.1 0.7 constant_dynamic-slice_fusion.1
  158.5 0.5 collective-permute-done.4
  159.0 0.0 copy-start.5
  159.0 0.7 copy-done.5
  159.7 1.1 pad_maximum_fusion.2
  160.8 0.0 copy-start.3
  160.8 17.1 %multiply_reduce_fusion = (f32[2048]{0:T(1024)S(1)}, f32[2048,512]{0,1:T(8,128)}) fusion(f32[512]{0:T(512)S(1)} %copy-done.8, bf16[2048,512]{0,1:T(8,128)(2,1)} %copy-done.1, f32[2048]{0:T(1024)S(1)} %add_rsqrt_fusion, bf16[2048,512]{0,1:T(8,128)(2,1)} %copy.16, bf16[2048,4096]{1,0:T(8,128)(2,1)} %all-gather.2.cloned.1.call-done, bf16[512,4096]{1,0:T(8,128)(2,1)} %param.16), kind=kOutput, calls=%fused_computation.18 | convolution fusion | flops 8601466880 | bytes 29378560 | tf_op jit(solution)/shard_map/dot_general | solution.py:76
  178.0 0.0 copy-start.4
  178.0 0.0 collective-permute-start.5
  178.0 0.0 collective-permute-done.1
  178.0 0.0 copy-done.3
  178.0 2.5 pad_maximum_fusion.1
  180.5 0.0 collective-permute-done.5
  180.5 0.0 collective-permute-start.6
  180.5 1.1 collective-permute-done
  181.6 0.0 copy-done.4
  181.6 2.3 pad_maximum_fusion
  183.9 2.2 gather_fusion.2
  186.1 0.0 copy-start
  186.1 4.5 %gather_fusion.1 = f32[96,4096]{1,0:T(8,128)} fusion(f32[112,4096]{1,0:T(8,128)} %pad_maximum_fusion.1, s32[1024]{0:T(1024)S(1)} %pad_clamp_fusion), kind=kCustom, calls=%fused_computation.1.clone | custom fusion | bytes 3146112 | tf_op jit(solution)/shard_map/jit(_take)/gather | solution.py:111
  190.6 0.0 copy-done
  190.6 2.2 gather_fusion
  192.8 41.8 %collective-permute-done.6 = f32[2048]{0:T(1024)S(1)} collective-permute-done((f32[2048]{0:T(1024)S(1)}, f32[2048]{0:T(1024)S(1)}, u32[]{:S(2)}, u32[]{:S(2)}) %collective-permute-start.6) | collective-permute-done | bytes 8224 | tf_op jit(solution)/shard_map/ppermute | solution.py:21
  234.5 6.5 %fusion.1 = (bf16[2048,512]{0,1:T(8,128)(2,1)S(1)}, bf16[2048,512]{0,1:T(8,128)(2,1)}) fusion(bf16[2048,512]{0,1:T(8,128)(2,1)} %copy-done.1, bf16[2048,512]{0,1:T(8,128)(2,1)} %copy.16, f32[2048]{0:T(1024)S(1)} %add_multiply_fusion, f32[2048,512]{0,1:T(8,128)} %get-tuple-element.23, f32[512]{0:T(512)S(1)} %copy-done.8, f32[2048]{0:T(1024)S(1)} %add_rsqrt_fusion), kind=kLoop, calls=%fused_computation.10 | loop fusion | flops 22020096 | bytes 12601344 | tf_op jit(solution)/shard_map/convert_element_type | solution.py:83
  241.0 3.9 %copy.17 = bf16[2048,512]{1,0:T(8,128)(2,1)} copy(bf16[2048,512]{0,1:T(8,128)(2,1)} %get-tuple-element.17) | data formatting | bytes 4194304
  245.0 2.5 copy.18
  247.5 84.8 %all-reduce.3.cloned.1.call-done = f32[512,4096]{1,0:T(8,128)} async-done(((f32[512,4096]{1,0:T(8,128)}), f32[512,4096]{1,0:T(8,128)}) %all-reduce.3.cloned.1.call-update) | async-done | bytes 8388624 | tf_op jit(solution)/shard_map/psum | solution.py:92
  332.2 8.0 %select_bitcast_fusion = (f32[1,96,4096]{2,1,0:T(8,128)}, f32[1,96,4096]{2,1,0:T(8,128)}, f32[1,96,4096]{2,1,0:T(8,128)}) fusion(pred[96]{0:T(512)(128)(4,1)S(1)} %iota_compare_fusion, s32[]{:T(128)S(6)} %select_n.34, f32[512,4096]{1,0:T(8,128)} %all-reduce.3.cloned.1.call-done, f32[96,4096]{1,0:T(8,128)} %gather_fusion.2, ...), kind=kLoop, calls=%fused_computation.31 | loop fusion | flops 10223616 | bytes 17825988 | tf_op jit(solution)/shard_map/broadcast_in_dim | solution.py:119
  (8 shorter events, 0.1 us)
Async XLA Ops:
  7.2 116.1 %all-gather.2.cloned.1.call-start = ((), (), s32[]{:S(2)}) async-start(), calls=%async_computation | async-start | bytes 17825792 | tf_op jit(solution)/shard_map/all_gather | solution.py:72
  7.9 324.3 %all-reduce.3.cloned.1.call-start = ((), (), s32[]{:S(2)}) async-start(), calls=%async_computation.1 | async-start | bytes 16777216 | tf_op jit(solution)/shard_map/psum | solution.py:92
  10.9 112.4 %copy-start.1 = (bf16[2048,512]{0,1:T(8,128)(2,1)}, bf16[2048,512]{0,1:T(8,128)(2,1)S(1)}, u32[]{:S(2)}) copy-start(bf16[2048,512]{0,1:T(8,128)(2,1)S(1)} %copy.15) | copy-start | bytes 6291460
  15.4 107.8 %copy-start.8 = (f32[512]{0:T(512)S(1)}, f32[512]{0:T(512)}, u32[]{:S(2)}) copy-start(f32[512]{0:T(512)} %param.15) | copy-start | bytes 6148
  18.6 1.3 collective-permute-start.2
  19.9 5.5 %collective-permute-start.3 = (f32[2048]{0:T(1024)S(1)}, f32[2048]{0:T(1024)S(1)}, u32[]{:S(2)}, u32[]{:S(2)}) collective-permute-start(f32[2048]{0:T(1024)S(1)} %add.87), channel_id=1, source_target_pairs={{0,2},{1,3},{2,0},{3,1},{4,6},{5,7},{6,4},{7,5},{8,10},{9,11},{10,... | collective-permute-start | bytes 24584 | tf_op jit(solution)/shard_map/ppermute | solution.py:21
  139.4 1.4 copy-start.2
  139.4 12.7 %copy-start.6 = (s32[1,9]{1,0:T(1,128)S(1)}, s32[1,9]{1,0:T(1,128)}, u32[]{:S(2)}) copy-start(s32[1,9]{1,0:T(1,128)} %param.20) | copy-start | bytes 112
  139.4 12.7 %copy-start.7 = (s32[1,9]{1,0:T(1,128)S(1)}, s32[1,9]{1,0:T(1,128)}, u32[]{:S(2)}) copy-start(s32[1,9]{1,0:T(1,128)} %param.21) | copy-start | bytes 112
  140.8 18.2 %collective-permute-start.4 = (f32[16,4096]{1,0:T(8,128)S(1)}, f32[16,4096]{1,0:T(8,128)S(1)}, u32[]{:S(2)}, u32[]{:S(2)}) collective-permute-start(f32[16,4096]{1,0:T(8,128)S(1)} %slice_bitcast_fusion), channel_id=1, source_target_pairs={{16,0},{32,16},{48,32},{64,48},{80,64},{96,80},{112,96},{17,1},{33... | collective-permute-start | bytes 786440 | tf_op jit(solution)/shard_map/ppermute | solution.py:27
  145.3 32.7 %collective-permute-start.1 = (f32[16,4096]{1,0:T(8,128)}, f32[16,4096]{1,0:T(8,128)}, u32[]{:S(2)}, u32[]{:S(2)}) collective-permute-start(f32[16,4096]{1,0:T(8,128)} %slice_bitcast_fusion.1), channel_id=1, source_target_pairs={{16,0},{32,16},{48,32},{64,48},{80,64},{96,80},{112,96},{17,1},{33... | collective-permute-start | bytes 786440 | tf_op jit(solution)/shard_map/ppermute | solution.py:27
  149.4 32.2 %collective-permute-start = (f32[16,4096]{1,0:T(8,128)}, f32[16,4096]{1,0:T(8,128)}, u32[]{:S(2)}, u32[]{:S(2)}) collective-permute-start(f32[16,4096]{1,0:T(8,128)} %slice_bitcast_fusion.2), channel_id=1, source_target_pairs={{16,0},{32,16},{48,32},{64,48},{80,64},{96,80},{112,96},{17,1},{33... | collective-permute-start | bytes 786440 | tf_op jit(solution)/shard_map/ppermute | solution.py:27
  159.0 0.7 copy-start.5
  160.8 17.1 %copy-start.3 = (f32[1,96,4096]{2,1,0:T(8,128)S(1)}, f32[1,96,4096]{2,1,0:T(8,128)}, u32[]{:S(2)}) copy-start(f32[1,96,4096]{2,1,0:T(8,128)} %param.18) | copy-start | bytes 4718596
  178.0 3.6 %copy-start.4 = (f32[1,96,4096]{2,1,0:T(8,128)S(1)}, f32[1,96,4096]{2,1,0:T(8,128)}, u32[]{:S(2)}) copy-start(f32[1,96,4096]{2,1,0:T(8,128)} %param.17) | copy-start | bytes 4718596
  178.0 2.5 collective-permute-start.5
  180.5 54.0 %collective-permute-start.6 = (f32[2048]{0:T(1024)S(1)}, f32[2048]{0:T(1024)S(1)}, u32[]{:S(2)}, u32[]{:S(2)}) collective-permute-start(f32[2048]{0:T(1024)S(1)} %add.97), channel_id=1, source_target_pairs={{0,2},{1,3},{2,0},{3,1},{4,6},{5,7},{6,4},{7,5},{8,10},{9,11},{10,... | collective-permute-start | bytes 24584 | tf_op jit(solution)/shard_map/ppermute | solution.py:21
  186.1 4.5 %copy-start = (f32[112,4096]{1,0:T(8,128)S(1)}, f32[112,4096]{1,0:T(8,128)}, u32[]{:S(2)}) copy-start(f32[112,4096]{1,0:T(8,128)} %pad_maximum_fusion) | copy-start | bytes 5505028
Sparse Core Ops, SparseCore 0:
  10.4 112.8 all-gather.1
  139.5 192.6 all-reduce.2
where the time goes:
time: 351 us; the launch traced here: 347 us
  waiting for transfers between devices  229 us (65%)
  matrix products  33.2 us (9%)
  local copies, waits for them, and re-layouts  28.9 us (8%)
  other arithmetic  23.6 us (7%)
  between operations  20 us (6%)
  starting transfers between devices  11.9 us (3%)
    all_gather x1, waiting for transfers between devices, local(): arrived = lax.all_gather(cotangent, 'tensor', axis=0, tiled=True)  97.8 us
    psum x1, waiting for transfers between devices, local(): summed_grad = lax.psum(grad_sum, 'dp')  84.8 us
    ppermute x4, waiting for transfers between devices, partner(): return lax.ppermute(value, axis, pairs)  44.6 us
    dot_general x1, matrix products, local(): lax.dot_general(arrived, out_weight, (((1,), (1,)), ((), ())), preferred_...  17.1 us
    dot_general x1, matrix products, local(): lax.dot_general(hidden, arrived, (((0,), (0,)), ((), ())), preferred_elem...  16.1 us
    unnamed x22, local copies, waits for them, and re-layouts  16 us
    gather x3, local copies, waits for them, and re-layouts, local(): jnp.take(jnp.concatenate([own_state, extra_rows], axis=0), source_row, ax...  8.87 us
    broadcast_in_dim x1, other arithmetic, local(): jnp.where(valid, second_new, 0.0)[None]  7.95 us
  transfers between devices with their start and end apart: 9, of which 7 were waited for; matrix products, arithmetic and copies ran while one was open for 17% of the time, Pallas kernels for 0%

commit v1 on v0

v1 whole, which is shorter than its diff:
```python
import jax
import jax.numpy as jnp
from jax import lax
from jax.experimental import pallas as pl
from jax.experimental.pallas import tpu as pltpu
from jax.sharding import PartitionSpec as P

GROUP = 2048

norm_eps = 1e-05
beta_one = 0.9
beta_two = 0.95
adam_eps = 1e-08
learn_rate = 0.0003
weight_decay = 0.1
adam_step = 1000.0

N_X, N_Y = 4, 4
AXES = ("dp", "tensor")
TILE = 1024
TOP, FINE = 32700.0, 256.0
BLOCK = 128
HALO = 16
CAP = 96
OWNERS = ((2, 1), (1, 1), (3, 1), (0, 1), (2, 0), (1, 0), (3, 0), (0, 0))
EARLY = ((0, 0), (0, 1), (3, 0), (1, 0), (2, 0))
LATE = ((3, 1), (1, 1), (2, 1))
F32 = jnp.float32
BF16 = jnp.bfloat16


def position(flat):
    dp, tensor = flat // 16, flat % 16
    return dp % 4, tensor // 4, dp // 4, (tensor // 2) % 2, tensor % 2


def flat_of(x, y, zl, zh, c):
    return (zl * 4 + x) * 16 + (y * 2 + zh) * 2 + c


def pairs_of(move):
    return [(i, flat_of(*move(*position(i)))) for i in range(128)]


TO_CORE = pairs_of(lambda x, y, zl, zh, c: (x, y, zl, zh, 1 - c))
TO_ZHI = pairs_of(lambda x, y, zl, zh, c: (x, y, zl, 1 - zh, c))
TO_YP = pairs_of(lambda x, y, zl, zh, c: (x, (y + 1) % N_Y, zl, zh, c))
TO_YM = pairs_of(lambda x, y, zl, zh, c: (x, (y - 1) % N_Y, zl, zh, c))
TO_OWNER = [pairs_of(lambda x, y, zl, zh, c: ((x + dx) % N_X, y, (zl + dz) % 2, zh, c)) for dx, dz in OWNERS]
TO_NEXT = [(i, i + 16) for i in range(112)]
TO_LAST = [(i + 16, i) for i in range(112)]


def move(value, pairs):
    return lax.ppermute(value, AXES, pairs)


def params(mib):
    return pltpu.CompilerParams(vmem_limit_bytes=mib * 2**20)


SMALL = pl.CostEstimate(flops=1024, bytes_accessed=1024, transcendentals=0)


def eye():
    rows = lax.broadcasted_iota(jnp.int32, (BLOCK, BLOCK), 0)
    cols = lax.broadcasted_iota(jnp.int32, (BLOCK, BLOCK), 1)
    return rows == cols


def column_of(row):
    return jnp.sum(jnp.where(eye(), jnp.broadcast_to(row, (BLOCK, BLOCK)), 0.0), axis=1, keepdims=True)


def row_of(column):
    return jnp.sum(jnp.where(eye(), jnp.broadcast_to(column, (BLOCK, BLOCK)), 0.0), axis=0, keepdims=True)


def square_kernel(mixer_ref, gate_ref, out_ref):
    gate = gate_ref[...].astype(F32)
    gated = mixer_ref[...].astype(F32) * (gate * jax.nn.sigmoid(gate))
    out_ref[0] = row_of(jnp.sum(gated * gated, axis=1, keepdims=True))


def hidden_kernel(order_ref, mixer_ref, gate_ref, inverse_ref, gain_ref, out_ref, turned):
    gate = gate_ref[...].astype(F32)
    gated = mixer_ref[...].astype(F32) * (gate * jax.nn.sigmoid(gate))
    normed = gated * column_of(inverse_ref[0])
    hidden = normed * gain_ref[...]
    turned[...] = hidden.T
    x, zl = order_ref[16], order_ref[17]
    for k, (dx, dz) in enumerate(OWNERS):
        start = lax.rem(zl + dz, 2) * 256 + lax.rem(x + dx, N_X) * 64
        out_ref[k * 64 : (k + 1) * 64, :] = turned[pl.ds(pl.multiple_of(start, 64), 64), :].astype(BF16)


def centre_kernel(order_ref, back_ref, mixer_ref, gate_ref, inverse_ref, gain_ref, out_ref):
    gate = gate_ref[...].astype(F32)
    gated = mixer_ref[...].astype(F32) * (gate * jax.nn.sigmoid(gate))
    normed = gated * column_of(inverse_ref[0])
    scaled = back_ref[...] * gain_ref[...]
    out_ref[0] = row_of(jnp.sum(scaled * normed, axis=1, keepdims=True))


def grads_kernel(order_ref, back_ref, mixer_ref, gate_ref, inverse_ref, centre_ref, gain_ref, input_ref, gate_out_ref):
    gate = gate_ref[...].astype(F32)
    mixer = mixer_ref[...].astype(F32)
    sig = jax.nn.sigmoid(gate)
    activated = gate * sig
    slope = sig * (1.0 + gate * (1.0 - sig))
    inverse = column_of(inverse_ref[0])
    normed = mixer * activated * inverse
    scaled = back_ref[...] * gain_ref[...]
    gated_back = inverse * (scaled - normed * column_of(centre_ref[0]))
    input_ref[...] = (gated_back * activated).astype(BF16)
    gate_out_ref[...] = (gated_back * mixer * slope).astype(BF16)


def copies(sources, target, sems):
    start, made = 0, []
    for k, source in enumerate(sources):
        rows = source.shape[0]
        made.append(pltpu.make_async_copy(source, target.at[pl.ds(start, rows)], sems.at[k]))
        start += rows
    return made


def join_kernel(count, *refs):
    sources, out_ref, sems = refs[:count], refs[-2], refs[-1]
    made = copies(sources, out_ref, sems)
    for copy in made:
        copy.start()
    for copy in made:
        copy.wait()


def join(pieces, after, name):
    rows = sum(p.shape[0] for p in pieces)
    anywhere = pl.BlockSpec(memory_space=pl.ANY)
    return pl.pallas_call(
        lambda *refs: join_kernel(len(pieces), *refs),
        in_specs=[anywhere] * (len(pieces) + len(after)),
        out_specs=anywhere,
        out_shape=jax.ShapeDtypeStruct((rows, pieces[0].shape[1]), pieces[0].dtype),
        scratch_shapes=[pltpu.SemaphoreType.DMA((len(pieces),))],
        compiler_params=params(16),
        cost_estimate=SMALL,
        name=name,
    )(*pieces, *after)


def fetches(pieces, cot, sems, n):
    at, made = 0, []
    cols = pl.ds(n * TILE, TILE)
    for piece in pieces:
        rows = piece.shape[0]
        made.append(pltpu.make_async_copy(piece.at[:, cols], cot.at[pl.ds(at, rows), cols], sems.at[n, len(made)]))
        at += rows
    return made


def arrive(pieces, cot, sems, steps):
    n = pl.program_id(0)

    @pl.when(n == 0)
    def _():
        for k in range(steps):
            for copy in fetches(pieces, cot, sems, k):
                copy.start()

    for k in range(steps):

        @pl.when(n == k)
        def _():
            for copy in fetches(pieces, cot, sems, k):
                copy.wait()

    return cot[:, pl.ds(pl.multiple_of(n * TILE, TILE), TILE)]


def back_step(cot, weight_ref, sums, back_ref, start, sem, steps):
    n = pl.program_id(0)
    part = lax.dot_general(cot, weight_ref[...], (((1,), (1,)), ((), ())), preferred_element_type=F32)

    @pl.when(n == 0)
    def _():
        sums[...] = part

    @pl.when(n > 0)
    def _():
        sums[...] += part

    @pl.when(n == steps - 1)
    def _():
        out = pltpu.make_async_copy(sums, back_ref.at[pl.ds(start, sums.shape[0])], sem)
        out.start()
        out.wait()


def early_kernel(count, steps, *refs):
    pieces, (hidden_ref, weight_ref, grad_ref, back_ref, cot, sums, sems, sem) = refs[:count], refs[count:]
    here = arrive(pieces, cot, sems, steps)
    grad_ref[...] = jnp.dot(hidden_ref[...], here, preferred_element_type=F32)
    back_step(here, weight_ref, sums, back_ref, 0, sem, steps)


def late_kernel(count, steps, *refs):
    pieces, (hidden_ref, early_ref, *outs, mine_ref, cot, sems) = refs[:count], refs[count:]
    n = pl.program_id(0)
    here = arrive(pieces, cot, sems, steps)
    grad = early_ref[...] + jnp.dot(hidden_ref[...], here, preferred_element_type=F32)
    sent = len(outs)
    mine_ref[...] = grad[sent * 64 :]
    lanes = lax.broadcasted_iota(jnp.int32, (64, 128), 1)
    cols = pl.ds(pl.multiple_of(n * TILE, TILE), TILE)
    for k, out in enumerate(outs):
        rows = grad[k * 64 : (k + 1) * 64]
        most = jnp.maximum(jnp.max(jnp.abs(rows), axis=1, keepdims=True), 1e-30)
        code = jnp.ceil(jnp.log2(most) * FINE)
        out[:, cols] = jnp.round(rows * (TOP / scale_of(code))).astype(jnp.int32).astype(jnp.int16)
        codes = pl.ds(steps * TILE, 128)
        before = jnp.where(n == 0, 0, out[:, codes].astype(jnp.int32))
        out[:, codes] = jnp.where(lanes == n, code.astype(jnp.int32), before).astype(jnp.int16)


def scale_of(code):
    return jnp.exp(code * (0.6931471805599453 / FINE))


def back_kernel(count, start, steps, *refs):
    pieces, (weight_ref, back_in, back_ref, cot, sums, sems, sem) = refs[:count], refs[count:]
    here = arrive(pieces, cot, sems, steps)
    back_step(here, weight_ref, sums, back_ref, start, sem, steps)


def sum_kernel(count, *refs):
    codes, parts, (mine_ref, out_ref) = refs[:count], refs[count : 2 * count], refs[2 * count :]
    n = pl.program_id(0)
    lanes = lax.broadcasted_iota(jnp.int32, (64, 128), 1)
    total = mine_ref[...]
    for code_ref, part_ref in zip(codes, parts):
        code = jnp.where(lanes == n, code_ref[...].astype(jnp.int32).astype(F32), 0.0)
        scale = scale_of(jnp.sum(code, axis=1, keepdims=True)) / TOP
        total += part_ref[...].astype(jnp.int32).astype(F32) * scale
    out_ref[...] = total


ANYWHERE = pl.BlockSpec(memory_space=pl.ANY)


def wide(rows):
    return pl.BlockSpec((rows, TILE), lambda n: (0, n))


def kept(rows, cols, at=0):
    return pl.BlockSpec((rows, cols), lambda n: (0, at))


def early_products(pieces, hidden, weight):
    tokens = sum(p.shape[0] for p in pieces)
    channels, width = weight.shape
    steps = width // TILE
    return pl.pallas_call(
        lambda *refs: early_kernel(len(pieces), steps, *refs),
        grid=(steps,),
        in_specs=[ANYWHERE] * len(pieces) + [kept(channels, tokens), wide(channels)],
        out_specs=[wide(channels), ANYWHERE],
        out_shape=[jax.ShapeDtypeStruct((channels, width), F32), jax.ShapeDtypeStruct((2048, channels), F32)],
        scratch_shapes=[
            pltpu.VMEM((tokens, width), BF16),
            pltpu.VMEM((tokens, channels), F32),
            pltpu.SemaphoreType.DMA((steps, len(pieces))),
            pltpu.SemaphoreType.DMA,
        ],
        compiler_params=params(48),
        cost_estimate=SMALL,
        name="early_products",
    )(*pieces, hidden, weight)


def late_products(pieces, hidden, early):
    tokens = sum(p.shape[0] for p in pieces)
    channels, width = early.shape
    steps = width // TILE
    sent = len(OWNERS) - 1
    code = jax.ShapeDtypeStruct((64, width + 128), jnp.int16)
    return pl.pallas_call(
        lambda *refs: late_kernel(len(pieces), steps, *refs),
        grid=(steps,),
        in_specs=[ANYWHERE] * len(pieces) + [kept(channels, tokens), wide(channels)],
        out_specs=[kept(64, width + 128)] * sent + [wide(64)],
        out_shape=[code] * sent + [jax.ShapeDtypeStruct((64, width), F32)],
        scratch_shapes=[pltpu.VMEM((tokens, width), BF16), pltpu.SemaphoreType.DMA((steps, len(pieces)))],
        compiler_params=params(48),
        cost_estimate=SMALL,
        name="late_products",
    )(*pieces, hidden, early)


def late_back(pieces, weight, back, after):
    tokens = sum(p.shape[0] for p in pieces)
    channels, width = weight.shape
    steps = width // TILE
    start = back.shape[0] - tokens
    count = len(pieces)
    return pl.pallas_call(
        lambda *refs: back_kernel(count, start, steps, *refs[: count + 2], *refs[count + 3 :]),
        grid=(steps,),
        in_specs=[ANYWHERE] * count + [wide(channels), ANYWHERE, ANYWHERE],
        out_specs=ANYWHERE,
        out_shape=jax.ShapeDtypeStruct(back.shape, F32),
        input_output_aliases={count + 1: 0},
        scratch_shapes=[
            pltpu.VMEM((tokens, width), BF16),
            pltpu.VMEM((tokens, channels), F32),
            pltpu.SemaphoreType.DMA((steps, count)),
            pltpu.SemaphoreType.DMA,
        ],
        compiler_params=params(48),
        cost_estimate=SMALL,
        name="late_back",
    )(*pieces, weight, back, after)


def summed(codes, mine):
    width = mine.shape[1]
    return pl.pallas_call(
        lambda *refs: sum_kernel(len(codes), *refs),
        grid=(width // TILE,),
        in_specs=[kept(64, 128, width // 128)] * len(codes) + [wide(64)] * (len(codes) + 1),
        out_specs=wide(64),
        out_shape=jax.ShapeDtypeStruct(mine.shape, F32),
        compiler_params=params(32),
        cost_estimate=SMALL,
        name="summed",
    )(*codes, *codes, mine)


def adam_kernel(where_ref, grad_ref, up_ref, down_ref, master_ref, first_ref, second_ref, arrived_ref, *rest):
    new_master, new_first, new_second = rest[-3:]
    offset, moved, old_count, new_count = where_ref[1], where_ref[2], where_ref[3], where_ref[4]
    width = grad_ref.shape[1]
    slots = lax.broadcasted_iota(jnp.int32, (128, width), 0)
    pad = jnp.zeros((128 - CAP, width), F32)
    grads = jnp.concatenate([up_ref[...], grad_ref[...], down_ref[...], pad], axis=0)
    grad = pltpu.roll(grads, lax.rem(128 - offset, 128), 0)[:CAP] / 8.0

    def placed(k, ref):
        extra = jnp.concatenate([arrived_ref[k * HALO : (k + 1) * HALO, :], jnp.zeros((128 - HALO, width), F32)], axis=0)
        extra = pltpu.roll(extra, old_count, 0)
        joined = jnp.where(slots < old_count, jnp.concatenate([ref[0], pad], axis=0), extra)
        return pltpu.roll(joined, lax.rem(128 - moved, 128), 0)[:CAP]

    valid = slots[:CAP] < new_count
    first = beta_one * placed(1, first_ref) + (1.0 - beta_one) * grad
    new_first[0] = jnp.where(valid, first, 0.0)
    second = beta_two * placed(2, second_ref) + (1.0 - beta_two) * grad * grad
    new_second[0] = jnp.where(valid, second, 0.0)
    corr_one = 1.0 - beta_one**adam_step
    corr_two = 1.0 - beta_two**adam_step
    update = first / corr_one / (jnp.sqrt(second / corr_two) + adam_eps)
    master = placed(0, master_ref)
    new_master[0] = jnp.where(valid, master - learn_rate * (update + weight_decay * master), 0.0)


def adam(where, grad, up, down, states, arrived, made, start, width):
    tile = 512
    at = start // tile
    state_spec = pl.BlockSpec((1, CAP, tile), lambda i, w: (0, 0, at + i))
    part = lambda n: pl.BlockSpec((n, tile), lambda i, w: (0, i))
    whole = jax.ShapeDtypeStruct(states[0].shape, F32)
    in_specs = [part(64), part(HALO), part(HALO), state_spec, state_spec, state_spec]
    in_specs.append(pl.BlockSpec((3 * HALO, tile), lambda i, w: (0, at + i)))
    operands = [grad, up, down, *states, arrived]
    aliases = {}
    if made is not None:
        in_specs += [pl.BlockSpec(memory_space=pl.ANY)] * 3
        operands += made
        aliases = {8: 0, 9: 1, 10: 2}
    return pl.pallas_call(
        adam_kernel,
        grid_spec=pltpu.PrefetchScalarGridSpec(
            num_scalar_prefetch=1,
            grid=(width // tile,),
            in_specs=in_specs,
            out_specs=[state_spec] * 3,
        ),
        out_shape=[whole] * 3,
        input_output_aliases=aliases,
        compiler_params=params(32),
        cost_estimate=SMALL,
        name="adam",
    )(where, *operands)


def local(
    cotangent,
    mixer_out,
    gate,
    norm_gain,
    out_weight,
    old_master,
    old_first,
    old_second,
    old_bounds,
    new_bounds,
):
    dp = lax.axis_index("dp")
    tensor = lax.axis_index("tensor")
    x, zl = dp % 4, dp // 4
    y, zh, core = tensor // 4, (tensor // 2) % 2, tensor % 2
    tokens, channels = mixer_out.shape
    blocks = tokens // BLOCK

    old_row, new_row = old_bounds[0], new_bounds[0]
    new_start = new_row[dp]
    old_start = old_row[dp]
    where = jnp.stack(
        [x, new_start - (64 * dp - HALO), new_start - old_start, old_row[dp + 1] - old_start, new_row[dp + 1] - new_start]
    ).astype(jnp.int32)

    order = jnp.stack(
        [
            ((y + dy) % N_Y * 2 + (zh + dz) % 2) * 2 + (core + dc) % 2
            for group in (EARLY, LATE)
            for dc in (0, 1)
            for dy, dz in group
        ]
        + [x, zl]
    ).astype(jnp.int32)

    own = cotangent
    own_z = move(own, TO_ZHI)
    own_m, own_p = move(own, TO_YP), move(own, TO_YM)
    own_s = move(own, TO_CORE)

    row_spec = pl.BlockSpec((1, 1, BLOCK), lambda i: (i, 0, 0))
    block_spec = pl.BlockSpec((BLOCK, channels), lambda i: (i, 0))
    rows_shape = jax.ShapeDtypeStruct((blocks, 1, BLOCK), F32)

    def group_total(part):
        part = part + move(part, TO_CORE)
        return part + move(part, TO_ZHI)

    squares = pl.pallas_call(
        square_kernel,
        grid=(blocks,),
        in_specs=[block_spec, block_spec],
        out_specs=row_spec,
        out_shape=rows_shape,
        compiler_params=params(32),
        cost_estimate=SMALL,
        name="squares",
    )(mixer_out, gate)
    inverse = lax.rsqrt(group_total(squares) / GROUP + norm_eps)

    gain = norm_gain[None, :]
    there = pl.BlockSpec((BLOCK, channels), lambda i, o: (o[i], 0))
    here = pl.BlockSpec((BLOCK, channels), lambda i, o: (i, 0))
    there_row = pl.BlockSpec((1, 1, BLOCK), lambda i, o: (o[i], 0, 0))
    gain_spec = pl.BlockSpec((1, channels), lambda i, o: (0, 0))

    def ordered(kernel, in_specs, out_specs, out_shape, name, scratch=()):
        return pl.pallas_call(
            kernel,
            grid_spec=pltpu.PrefetchScalarGridSpec(
                num_scalar_prefetch=1, grid=(blocks,), in_specs=in_specs, out_specs=out_specs, scratch_shapes=scratch
            ),
            out_shape=out_shape,
            compiler_params=params(32),
            cost_estimate=SMALL,
            name=name,
        )

    hidden = ordered(
        hidden_kernel,
        [there, there, there_row, gain_spec],
        pl.BlockSpec((channels, BLOCK), lambda i, o: (0, i)),
        jax.ShapeDtypeStruct((channels, tokens), BF16),
        "hidden",
        [pltpu.VMEM((channels, BLOCK), F32)],
    )(order, mixer_out, gate, inverse, gain)

    states = (old_master, old_first, old_second)
    arrived = move(jnp.concatenate([s[0, :HALO] for s in states], axis=0), TO_LAST)

    far_a, far_b = move(own_m[:64], TO_YP), move(own_p[64:], TO_YM)
    other_m, other_p = move(own_z, TO_YP), move(own_z, TO_YM)
    near = move(join([own_z, own_m, own_p], [hidden], "near"), TO_CORE)
    far = join([far_a, far_b], [], "far")
    far_z, far_s = move(far, TO_ZHI), move(far, TO_CORE)
    early, back = early_products([own, own_z, own_m, own_p, far, own_s, near, far_s], hidden, out_weight)
    other = move(join([other_m, other_p, far_z], [early], "other"), TO_CORE)
    late = [other_m, other_p, far_z, other]
    *codes, mine = late_products(late, hidden[:, 1280:], early)
    back = late_back(late, out_weight, back, mine)
    grad = summed([move(code, pairs) for code, pairs in zip(codes, TO_OWNER)], mine)
    up = move(grad[64 - HALO :], TO_NEXT)
    down = move(grad[:HALO], TO_LAST)
    made = adam(where, grad, up, down, states, arrived, None, 0, grad.shape[1])

    centre = ordered(
        centre_kernel,
        [here, there, there, there_row, gain_spec],
        there_row,
        rows_shape,
        "centre",
    )(order, back, mixer_out, gate, inverse, gain)
    centre = group_total(centre) / GROUP
    out_shape = jax.ShapeDtypeStruct((tokens, channels), BF16)
    input_grad, gate_grad = ordered(
        grads_kernel,
        [here, there, there, there_row, there_row, gain_spec],
        [there, there],
        [out_shape, out_shape],
        "grads",
    )(order, back, mixer_out, gate, inverse, centre, gain)
    return (*made, input_grad, gate_grad)


def solution(mesh):
    return jax.shard_map(
        local,
        mesh=mesh,
        in_specs=(
            P(("dp", "tensor"), None),
            P("dp", "tensor"),
            P("dp", "tensor"),
            P("tensor"),
            P("tensor", None),
            P("tensor", "dp", None),
            P("tensor", "dp", None),
            P("tensor", "dp", None),
            P("tensor", None),
            P("tensor", None),
        ),
        out_specs=(
            P("tensor", "dp", None),
            P("tensor", "dp", None),
            P("tensor", "dp", None),
            P("dp", "tensor"),
            P("dp", "tensor"),
        ),
        check_vma=False,
    )
```

time: 351 us -> 223 us (0.64)
  waiting for transfers between devices: 229 us -> 84.5 us
  Pallas kernels: 0 us -> 70.4 us
  matrix products: 33.2 us -> 0 us
  starting transfers between devices: 11.9 us -> 38.3 us
  other arithmetic: 23.6 us -> 0.99 us
  between operations: 20 us -> 5.72 us
  local copies, waits for them, and re-layouts: 28.9 us -> 21.6 us
    all_gather x1 -> x0, waiting for transfers between devices: 97.8 us -> none  [local(): arrived = lax.all_gather(cotangent, 'tensor', axis=0, tiled=True)]
    psum x1 -> x0, waiting for transfers between devices: 84.8 us -> none  [local(): summed_grad = lax.psum(grad_sum, 'dp')]
    pallas_call x0 -> x12, Pallas kernels: none -> 70.4 us  [the longest x1 18.9 us: early_products(): pl.pallas_call(lambda *refs: early_kernel(len(pieces), steps, *refs), gri...]
    ppermute x7 -> x26, waiting for transfers between devices: 46.1 us -> 84.5 us  [move(): return lax.ppermute(value, AXES, pairs)]
    dot_general x2 -> x0, matrix products: 33.2 us -> none  [the longest x1 17.1 us: local(): lax.dot_general(arrived, out_weight, (((1,), (1,)), ((), ())), preferred_...]
    ppermute x7 -> x26, starting transfers between devices: 11.8 us -> 38.3 us  [move(): return lax.ppermute(value, AXES, pairs)]
    gather x3 -> x0, local copies, waits for them, and re-layouts: 8.87 us -> none  [local(): jnp.take(jnp.concatenate([own_state, extra_rows], axis=0), source_row, ax...]
    broadcast_in_dim x1 -> x0, other arithmetic: 7.95 us -> none  [local(): jnp.where(valid, second_new, 0.0)[None]]
  transfers between devices with their start and end apart: 9 -> 26, of which waited for: 7 -> 14; matrix products, arithmetic and copies ran while one was open for 17% -> 3% of each run, Pallas kernels for 0% -> 22%
where the time goes in v1:
time: 223 us; the launch traced here: 222 us
  waiting for transfers between devices  84.5 us (38%)
  Pallas kernels  70.4 us (32%)
  starting transfers between devices  38.3 us (17%)
  local copies, waits for them, and re-layouts  21.6 us (10%)
  between operations  5.72 us (3%)
    ppermute x26, waiting for transfers between devices, move(): return lax.ppermute(value, AXES, pairs)  84.5 us
    ppermute x26, starting transfers between devices, move(): return lax.ppermute(value, AXES, pairs)  38.3 us
    pallas_call x1, Pallas kernels, early_products(): pl.pallas_call(lambda *refs: early_kernel(len(pieces), steps, *refs), gri...  18.9 us
    unnamed x50, local copies, waits for them, and re-layouts  15.6 us
    pallas_call x1, Pallas kernels, adam(): pl.pallas_call(adam_kernel, grid_spec=pltpu.PrefetchScalarGridSpec(num_sc...  9.26 us
    pallas_call x1, Pallas kernels, late_products(): pl.pallas_call(lambda *refs: late_kernel(len(pieces), steps, *refs), grid...  8.9 us
    pallas_call x1, Pallas kernels, late_back(): pl.pallas_call(lambda *refs: back_kernel(count, start, steps, *refs[:coun...  8.71 us
    pallas_call x1, Pallas kernels, local(): ordered(grads_kernel, [here, there, there, there_row, there_row, gain_spe...  7.96 us
  transfers between devices with their start and end apart: 26, of which 14 were waited for; matrix products, arithmetic and copies ran while one was open for 3% of the time, Pallas kernels for 22%

profile of v1, /device:TPU:6, one launch (start us, length us, event | category | flops | bytes accessed | tf_op | source)
XLA Modules:
  0.0 221.5 jit_solution(5468937439727527321)
XLA Ops:
  0.6 4.0 %collective-permute-start = (bf16[128,4096]{1,0:T(8,128)(2,1)}, bf16[128,4096]{1,0:T(8,128)(2,1)}, u32[]{:S(2)}, u32[]{:S(2)}) collective-permute-start(bf16[128,4096]{1,0:T(8,128)(2,1)} %refs_0_.1), channel_id=1, source_target_pairs={{0,2},{1,3},{2,0},{3,1},{4,6},{5,7},{6,4},{7,5},{8,10},{9,11},{10,... | collective-permute-start | bytes 3145736 | tf_op jit(solution)/shard_map/ppermute | solution.py:55
  4.6 1.6 collective-permute-start.3
  6.2 1.7 collective-permute-start.5
  7.8 1.6 copy-done.2
  9.4 1.6 copy-done.4
  11.0 2.5 %squares.1 = f32[16,1,128]{2,1,0:T(1,128)S(1)} custom-call(bf16[2048,512]{1,0:T(8,128)(2,1)S(1)} %copy-done.2, bf16[2048,512]{1,0:T(8,128)(2,1)S(1)} %copy-done.4), custom_call_target="tpu_custom_call" | custom-call | flops 1024 | bytes 1024 | tf_op jit(solution)/shard_map/squares/pallas_call | solution.py:445
  13.7 1.1 collective-permute-done.9
  14.8 0.2 collective-permute-start.10
  15.0 0.1 stack.96.order_ref
  15.1 13.0 %collective-permute-done.10 = f32[16,1,128]{2,1,0:T(1,128)S(1)} collective-permute-done((f32[16,1,128]{2,1,0:T(1,128)S(1)}, f32[16,1,128]{2,1,0:T(1,128)S(1)}, u32[]{:S(2)}, u32[]{:S(2)}) %collective-permute-start.10) | collective-permute-done | bytes 8224 | tf_op jit(solution)/shard_map/ppermute | solution.py:55
  28.2 1.6 copy-done.5
  29.8 4.9 %hidden.1.refs_3_.refs_8_ = bf16[512,2048]{1,0:T(8,128)(2,1)S(1)} custom-call(s32[18]{0:T(128)S(1)} %stack.96.order_ref, bf16[2048,512]{1,0:T(8,128)(2,1)S(1)} %copy-done.3, bf16[2048,512]{1,0:T(8,128)(2,1)S(1)} %copy-done.5, f32[16,1,128]{2,1,0:T(1,128)S(1)} %add_rsqrt_fusion.inverse_ref, f32[1,512]{1,0:T(1,128)S(1)} %bitcast.33), custom_call_target="tpu_custom_call" | custom-call | flops 1024 | bytes 1024 | tf_op jit(solution)/shard_map/hidden/pallas_call | solution.py:475
  34.8 2.3 %near.1 = bf16[384,4096]{1,0:T(8,128)(2,1)S(1)} custom-call(bf16[128,4096]{1,0:T(8,128)(2,1)} %collective-permute-done.refs_0_.refs_1_, bf16[128,4096]{1,0:T(8,128)(2,1)S(1)} %collective-permute-done.3.refs_1_.refs_2_, bf16[128,4096]{1,0:T(8,128)(2,1)} %collective-permute-done.5.refs_2_.refs_3_, bf16[512,2048]{1,0:T(8,128)(2,1)S(1)} %hidden.1.refs_3_.refs_8_), custom_call_target="tpu_custom_call" | custom-call | flops 1024 | bytes 1024 | tf_op jit(solution)/shard_map/near/pallas_call | solution.py:140
  37.1 0.1 collective-permute-start.11
  37.2 0.1 copy-done.19
  37.3 0.4 collective-permute-start.8
  37.8 1.6 collective-permute-start.4
  39.4 1.1 slice.33
  40.5 1.7 collective-permute-start.6
  42.2 10.8 %collective-permute-done.4.refs_0_ = bf16[64,4096]{1,0:T(8,128)(2,1)S(1)} collective-permute-done((bf16[64,4096]{1,0:T(8,128)(2,1)S(1)}, bf16[64,4096]{1,0:T(8,128)(2,1)S(1)}, u32[]{:S(2)}, u32[]{:S(2)}) %collective-permute-start.4) | collective-permute-done | bytes 524320 | tf_op jit(solution)/shard_map/ppermute | solution.py:55
  53.1 1.2 collective-permute-done.6.refs_1_
  54.2 0.1 far.1.refs_4_
  54.4 1.6 collective-permute-start.1
  56.1 1.7 collective-permute-start.2
  57.7 3.2 %collective-permute-start.7 = (bf16[128,4096]{1,0:T(8,128)(2,1)S(1)}, bf16[128,4096]{1,0:T(8,128)(2,1)S(1)}, u32[]{:S(2)}, u32[]{:S(2)}) collective-permute-start(bf16[128,4096]{1,0:T(8,128)(2,1)S(1)} %far.1.refs_4_), channel_id=1, source_target_pairs={{0,2},{1,3},{2,0},{3,1},{4,6},{5,7},{6,4},{7,5},{8,10},{9,11},{10,... | collective-permute-start | bytes 3145736 | tf_op jit(solution)/shard_map/ppermute | solution.py:55
  61.0 1.0 copy-done.22
  62.0 18.9 %early_products.1 = (f32[512,4096]{1,0:T(8,128)}, f32[2048,512]{1,0:T(8,128)}) custom-call(bf16[128,4096]{1,0:T(8,128)(2,1)S(1)} %copy-done.19, bf16[128,4096]{1,0:T(8,128)(2,1)} %collective-permute-done.refs_0_.refs_1_, bf16[128,4096]{1,0:T(8,128)(2,1)S(1)} %collective-permute-done.3.refs_1_.refs_2_, ...), custom_call_target="tpu_custom_call" | custom-call | flops 1024 | bytes 1024 | tf_op jit(solution)/shard_map/early_products/pallas_call | solution.py:263
  80.8 0.6 collective-permute-done.1.refs_0_
  81.5 2.7 %collective-permute-done.7.refs_2_ = bf16[128,4096]{1,0:T(8,128)(2,1)S(1)} collective-permute-done((bf16[128,4096]{1,0:T(8,128)(2,1)S(1)}, bf16[128,4096]{1,0:T(8,128)(2,1)S(1)}, u32[]{:S(2)}, u32[]{:S(2)}) %collective-permute-start.7) | collective-permute-done | bytes 1048608 | tf_op jit(solution)/shard_map/ppermute | solution.py:55
  84.2 3.8 %copy-done.8 = f32[512,4096]{1,0:T(8,128)S(1)} copy-done((f32[512,4096]{1,0:T(8,128)S(1)}, f32[512,4096]{1,0:T(8,128)}, u32[]{:S(2)}) %copy-start.8) | copy-done | bytes 8388632
  88.0 0.2 other.1
  88.2 0.1 collective-permute-start.13
  88.3 1.2 slice.34.refs_4_
  89.5 4.6 %collective-permute-done.13.refs_3_ = bf16[384,4096]{1,0:T(8,128)(2,1)} collective-permute-done((bf16[384,4096]{1,0:T(8,128)(2,1)S(1)}, bf16[384,4096]{1,0:T(8,128)(2,1)}, u32[]{:S(2)}, u32[]{:S(2)}) %collective-permute-start.13) | collective-permute-done | bytes 3145760 | tf_op jit(solution)/shard_map/ppermute | solution.py:55
  94.1 8.9 %late_products.1 = (s16[64,4224]{1,0:T(8,128)(2,1)S(1)}, s16[64,4224]{1,0:T(8,128)(2,1)S(1)}, s16[64,4224]{1,0:T(8,128)(2,1)S(1)}, s16[64,4224]{1,0:T(8,128)(2,1...) custom-call(bf16[128,4096]{1,0:T(8,128)(2,1)} %copy-done.10, ...), custom_call_target="tpu_custom_call" | custom-call | flops 1024 | bytes 1024 | tf_op jit(solution)/shard_map/late_products/pallas_call | solution.py:287
  103.0 2.1 collective-permute-start.14
  105.2 2.3 %collective-permute-start.15 = (s16[64,4224]{1,0:T(8,128)(2,1)S(1)}, s16[64,4224]{1,0:T(8,128)(2,1)S(1)}, u32[]{:S(2)}, u32[]{:S(2)}) collective-permute-start(s16[64,4224]{1,0:T(8,128)(2,1)S(1)} %get-tuple-element.22), channel_id=1, source_target_pairs={{0,80},{1,81},{2,82},{3,83},{4,84},{5,85},{6,86},{7,87},{8,88},{9,... | collective-permute-start | bytes 1622024 | tf_op jit(solution)/shard_map/ppermute | solution.py:55
  107.5 1.1 slice_bitcast_fusion
  108.5 0.7 collective-permute-start.16
  109.2 0.8 collective-permute-start.17
  110.0 2.1 collective-permute-start.18
  112.2 10.0 %collective-permute-done.14.refs_0_.refs_7_ = s16[64,4224]{1,0:T(8,128)(2,1)S(1)} collective-permute-done((s16[64,4224]{1,0:T(8,128)(2,1)S(1)}, s16[64,4224]{1,0:T(8,128)(2,1)S(1)}, u32[]{:S(2)}, u32[]{:S(2)}) %collective-permute-start.14) | collective-permute-done | bytes 540704 | tf_op jit(solution)/shard_map/ppermute | solution.py:55
  122.2 21.6 %collective-permute-done.15.refs_1_.refs_8_ = s16[64,4224]{1,0:T(8,128)(2,1)S(1)} collective-permute-done((s16[64,4224]{1,0:T(8,128)(2,1)S(1)}, s16[64,4224]{1,0:T(8,128)(2,1)S(1)}, u32[]{:S(2)}, u32[]{:S(2)}) %collective-permute-start.15) | collective-permute-done | bytes 540704 | tf_op jit(solution)/shard_map/ppermute | solution.py:55
  143.8 1.0 slice_bitcast_fusion.2
  144.8 0.9 pad_maximum_fusion
  145.7 2.7 %collective-permute-start.23 = (f32[48,4096]{1,0:T(8,128)}, f32[48,4096]{1,0:T(8,128)}, u32[]{:S(2)}, u32[]{:S(2)}) collective-permute-start(f32[48,4096]{1,0:T(8,128)} %pad_maximum_fusion), channel_id=1, source_target_pairs={{16,0},{17,1},{18,2},{19,3},{20,4},{21,5},{22,6},{23,7},{24,8},{25... | collective-permute-start | bytes 2359304 | tf_op jit(solution)/shard_map/ppermute | solution.py:55
  148.4 6.1 %collective-permute-done.17.refs_3_.refs_10_ = s16[64,4224]{1,0:T(8,128)(2,1)S(1)} collective-permute-done((s16[64,4224]{1,0:T(8,128)(2,1)S(1)}, s16[64,4224]{1,0:T(8,128)(2,1)S(1)}, u32[]{:S(2)}, u32[]{:S(2)}) %collective-permute-start.17) | collective-permute-done | bytes 540704 | tf_op jit(solution)/shard_map/ppermute | solution.py:55
  154.6 0.6 collective-permute-done.18.refs_4_.refs_11_
  155.1 10.9 %collective-permute-done.19.refs_5_.refs_12_ = s16[64,4224]{1,0:T(8,128)(2,1)S(1)} collective-permute-done((s16[64,4224]{1,0:T(8,128)(2,1)S(1)}, s16[64,4224]{1,0:T(8,128)(2,1)S(1)}, u32[]{:S(2)}, u32[]{:S(2)}) %collective-permute-start.19) | collective-permute-done | bytes 540704 | tf_op jit(solution)/shard_map/ppermute | solution.py:55
  166.0 2.9 %summed.1.grad_ref = f32[64,4096]{1,0:T(8,128)S(1)} custom-call(s16[64,4224]{1,0:T(8,128)(2,1)S(1)} %collective-permute-done.14.refs_0_.refs_7_, s16[64,4224]{1,0:T(8,128)(2,1)S(1)} %collective-permute-done.15.refs_1_.refs_8_, s16[64,4224]{1,0:T(8,128)(2,1)S(1)} %collective-permute-done.16.refs_2_.refs_9_, ...), custom_call_target="tpu_custom_call" | custom-call | flops 1024 | bytes 1024 | tf_op jit(solution)/shard_map/summed/pallas_call | solution.py:327
  169.0 0.8 fusion
  169.8 3.3 %collective-permute-start.21 = (f32[16,4096]{1,0:T(8,128)}, f32[16,4096]{1,0:T(8,128)S(1)}, u32[]{:S(2)}, u32[]{:S(2)}) collective-permute-start(f32[16,4096]{1,0:T(8,128)} %get-tuple-element.36), channel_id=1, source_target_pairs={{0,16},{1,17},{2,18},{3,19},{4,20},{5,21},{6,22},{7,23},{8,24},{9,... | collective-permute-start | bytes 786440 | tf_op jit(solution)/shard_map/ppermute | solution.py:55
  173.1 2.5 %collective-permute-start.22 = (f32[16,4096]{1,0:T(8,128)}, f32[16,4096]{1,0:T(8,128)}, u32[]{:S(2)}, u32[]{:S(2)}) collective-permute-start(f32[16,4096]{1,0:T(8,128)} %get-tuple-element.35), channel_id=1, source_target_pairs={{16,0},{17,1},{18,2},{19,3},{20,4},{21,5},{22,6},{23,7},{24,8},{25... | collective-permute-start | bytes 786440 | tf_op jit(solution)/shard_map/ppermute | solution.py:55
  175.7 8.7 %late_back.1.back_ref = f32[2048,512]{1,0:T(8,128)} custom-call(bf16[128,4096]{1,0:T(8,128)(2,1)S(1)} %copy-done.11, bf16[128,4096]{1,0:T(8,128)(2,1)S(1)} %copy-done.13, bf16[128,4096]{1,0:T(8,128)(2,1)S(1)} %copy-done.15, bf16[384,4096]{1,0:T(8,128)(2,1)} %collective-permute-done.13.refs_3_, ...), custom_call_target="tpu_custom_call", output_to_operand_aliasing={{}: (5, {})} | custom-call | flops 1024 | bytes 1024 | tf_op jit(solution)/shard_map/late_back/pallas_call | solution.py:306
  184.4 2.2 copy-done
  186.6 3.7 %centre.1 = f32[16,1,128]{2,1,0:T(1,128)S(1)} custom-call(s32[18]{0:T(128)S(1)} %stack.96.order_ref, f32[2048,512]{1,0:T(8,128)S(1)} %copy-done, bf16[2048,512]{1,0:T(8,128)(2,1)S(1)} %copy-done.3, bf16[2048,512]{1,0:T(8,128)(2,1)S(1)} %copy-done.6, f32[16,1,128]{2,1,0:T(1,128)S(1)} %add_rsqrt_fusion.inverse_ref, f32[1,512]{1,0:T(1,128)S(1)} %bitcast.34), custom_call_target="tpu_custom_call" | custom-call | flops 1024 | bytes 1024 | tf_op jit(solution)/shard_map/centre/pallas_call | solution.py:502
  190.4 1.2 collective-permute-done.24
  191.5 3.7 %collective-permute-start.25 = (f32[16,1,128]{2,1,0:T(1,128)S(1)}, f32[16,1,128]{2,1,0:T(1,128)S(1)}, u32[]{:S(2)}, u32[]{:S(2)}) collective-permute-start(f32[16,1,128]{2,1,0:T(1,128)S(1)} %add.275), channel_id=1, source_target_pairs={{0,2},{1,3},{2,0},{3,1},{4,6},{5,7},{6,4},{7,5},{8,10},{9,11},{10,... | collective-permute-start | bytes 24584 | tf_op jit(solution)/shard_map/ppermute | solution.py:55
  195.2 0.6 constant_dynamic-slice_fusion
  200.4 0.1 stack.78.where_ref
  200.5 2.2 copy-done.1
  202.7 1.6 copy-done.7
  204.2 8.0 %grads.1 = (bf16[2048,512]{1,0:T(8,128)(2,1)}, bf16[2048,512]{1,0:T(8,128)(2,1)}) custom-call(s32[18]{0:T(128)S(1)} %stack.96.order_ref, f32[2048,512]{1,0:T(8,128)S(1)} %copy-done.1, bf16[2048,512]{1,0:T(8,128)(2,1)S(1)} %copy-done.3, bf16[2048,512]{1,0:T(8,128)(2,1)S(1)} %copy-done.7, f32[16,1,128]{2,1,0:T(1,128)S(1)} %add_rsqrt_fusion.inverse_ref, ...), custom_call_target="tpu_custom_call" | custom-call | flops 1024 | bytes 1024 | tf_op jit(solution)/shard_map/grads/pallas_call | solution.py:511
  212.2 9.3 %adam.1 = (f32[1,96,4096]{2,1,0:T(8,128)}, f32[1,96,4096]{2,1,0:T(8,128)}, f32[1,96,4096]{2,1,0:T(8,128)}) custom-call(s32[5]{0:T(128)S(1)} %stack.78.where_ref, f32[64,4096]{1,0:T(8,128)S(1)} %summed.1.grad_ref, f32[16,4096]{1,0:T(8,128)S(1)} %collective-permute-done.21.up_ref, f32[16,4096]{1,0:T(8,128)} %collective-permute-done.22.down_ref, ...), custom_call_target="tpu_custom_call" | custom-call | flops 1024 | bytes 1024 | tf_op jit(solution)/shard_map/adam/pallas_call | solution.py:380
  (64 shorter events, 0.6 us)
Async XLA Ops:
  0.6 34.1 %collective-permute-start = (bf16[128,4096]{1,0:T(8,128)(2,1)}, bf16[128,4096]{1,0:T(8,128)(2,1)}, u32[]{:S(2)}, u32[]{:S(2)}) collective-permute-start(bf16[128,4096]{1,0:T(8,128)(2,1)} %refs_0_.1), channel_id=1, source_target_pairs={{0,2},{1,3},{2,0},{3,1},{4,6},{5,7},{6,4},{7,5},{8,10},{9,11},{10,... | collective-permute-start | bytes 3145736 | tf_op jit(solution)/shard_map/ppermute | solution.py:55
  4.6 30.2 %collective-permute-start.3 = (bf16[128,4096]{1,0:T(8,128)(2,1)}, bf16[128,4096]{1,0:T(8,128)(2,1)S(1)}, u32[]{:S(2)}, u32[]{:S(2)}) collective-permute-start(bf16[128,4096]{1,0:T(8,128)(2,1)} %refs_0_.1), channel_id=1, source_target_pairs={{0,4},{1,5},{2,6},{3,7},{4,8},{5,9},{6,10},{7,11},{8,12},{9,13},{1... | collective-permute-start | bytes 3145736 | tf_op jit(solution)/shard_map/ppermute | solution.py:55
  6.2 28.6 %collective-permute-start.5 = (bf16[128,4096]{1,0:T(8,128)(2,1)}, bf16[128,4096]{1,0:T(8,128)(2,1)}, u32[]{:S(2)}, u32[]{:S(2)}) collective-permute-start(bf16[128,4096]{1,0:T(8,128)(2,1)} %refs_0_.1), channel_id=1, source_target_pairs={{0,12},{1,13},{2,14},{3,15},{4,0},{5,1},{6,2},{7,3},{8,4},{9,5},{1... | collective-permute-start | bytes 3145736 | tf_op jit(solution)/shard_map/ppermute | solution.py:55
  7.8 1.6 copy-start.2
  9.4 1.6 copy-start.4
  11.0 17.2 %copy-start.3 = (bf16[2048,512]{1,0:T(8,128)(2,1)S(1)}, bf16[2048,512]{1,0:T(8,128)(2,1)}, u32[]{:S(2)}) copy-start(bf16[2048,512]{1,0:T(8,128)(2,1)} %mixer_ref.7) | copy-start | bytes 6291460
  11.0 17.2 %copy-start.20 = (f32[512]{0:T(512)S(1)}, f32[512]{0:T(512)}, u32[]{:S(2)}) copy-start(f32[512]{0:T(512)} %param.13) | copy-start | bytes 6148
  13.5 1.3 collective-permute-start.9
  14.8 13.4 %collective-permute-start.10 = (f32[16,1,128]{2,1,0:T(1,128)S(1)}, f32[16,1,128]{2,1,0:T(1,128)S(1)}, u32[]{:S(2)}, u32[]{:S(2)}) collective-permute-start(f32[16,1,128]{2,1,0:T(1,128)S(1)} %add.271), channel_id=1, source_target_pairs={{0,2},{1,3},{2,0},{3,1},{4,6},{5,7},{6,4},{7,5},{8,10},{9,11},{10,... | collective-permute-start | bytes 24584 | tf_op jit(solution)/shard_map/ppermute | solution.py:55
  28.2 1.6 copy-start.5
  34.7 2.4 %copy-start.9 = (bf16[512,2048]{1,0:T(8,128)(2,1)}, bf16[512,2048]{1,0:T(8,128)(2,1)S(1)}, u32[]{:S(2)}) copy-start(bf16[512,2048]{1,0:T(8,128)(2,1)S(1)} %hidden.1.refs_3_.refs_8_) | copy-start | bytes 6291460
  34.7 2.6 %copy-start.19 = (bf16[128,4096]{1,0:T(8,128)(2,1)S(1)}, bf16[128,4096]{1,0:T(8,128)(2,1)}, u32[]{:S(2)}) copy-start(bf16[128,4096]{1,0:T(8,128)(2,1)} %refs_0_.1) | copy-start | bytes 3145732
  37.1 23.9 %collective-permute-start.11 = (bf16[384,4096]{1,0:T(8,128)(2,1)S(1)}, bf16[384,4096]{1,0:T(8,128)(2,1)}, u32[]{:S(2)}, u32[]{:S(2)}) collective-permute-start(bf16[384,4096]{1,0:T(8,128)(2,1)S(1)} %near.1), channel_id=1, source_target_pairs={{0,1},{1,0},{2,3},{3,2},{4,5},{5,4},{6,7},{7,6},{8,9},{9,8},{10,11... | collective-permute-start | bytes 9437192 | tf_op jit(solution)/shard_map/ppermute | solution.py:55
  37.3 20.4 %collective-permute-start.8 = (bf16[128,4096]{1,0:T(8,128)(2,1)S(1)}, bf16[128,4096]{1,0:T(8,128)(2,1)S(1)}, u32[]{:S(2)}, u32[]{:S(2)}) collective-permute-start(bf16[128,4096]{1,0:T(8,128)(2,1)S(1)} %copy-done.19), channel_id=1, source_target_pairs={{0,1},{1,0},{2,3},{3,2},{4,5},{5,4},{6,7},{7,6},{8,9},{9,8},{10,11... | collective-permute-start | bytes 3145736 | tf_op jit(solution)/shard_map/ppermute | solution.py:55
  37.8 15.3 %collective-permute-start.4 = (bf16[64,4096]{1,0:T(8,128)(2,1)S(1)}, bf16[64,4096]{1,0:T(8,128)(2,1)S(1)}, u32[]{:S(2)}, u32[]{:S(2)}) collective-permute-start(bf16[64,4096]{1,0:T(8,128)(2,1)S(1)} %slice.32), channel_id=1, source_target_pairs={{0,4},{1,5},{2,6},{3,7},{4,8},{5,9},{6,10},{7,11},{8,12},{9,13},{1... | collective-permute-start | bytes 1572872 | tf_op jit(solution)/shard_map/ppermute | solution.py:55
  40.5 13.7 %collective-permute-start.6 = (bf16[64,4096]{1,0:T(8,128)(2,1)S(1)}, bf16[64,4096]{1,0:T(8,128)(2,1)S(1)}, u32[]{:S(2)}, u32[]{:S(2)}) collective-permute-start(bf16[64,4096]{1,0:T(8,128)(2,1)S(1)} %slice.33), channel_id=1, source_target_pairs={{0,12},{1,13},{2,14},{3,15},{4,0},{5,1},{6,2},{7,3},{8,4},{9,5},{1... | collective-permute-start | bytes 1572872 | tf_op jit(solution)/shard_map/ppermute | solution.py:55
  54.3 6.7 %collective-permute-start.12 = (bf16[128,4096]{1,0:T(8,128)(2,1)S(1)}, bf16[128,4096]{1,0:T(8,128)(2,1)S(1)}, u32[]{:S(2)}, u32[]{:S(2)}) collective-permute-start(bf16[128,4096]{1,0:T(8,128)(2,1)S(1)} %far.1.refs_4_), channel_id=1, source_target_pairs={{0,1},{1,0},{2,3},{3,2},{4,5},{5,4},{6,7},{7,6},{8,9},{9,8},{10,11... | collective-permute-start | bytes 3145736 | tf_op jit(solution)/shard_map/ppermute | solution.py:55
  54.4 27.0 %collective-permute-start.1 = (bf16[128,4096]{1,0:T(8,128)(2,1)}, bf16[128,4096]{1,0:T(8,128)(2,1)S(1)}, u32[]{:S(2)}, u32[]{:S(2)}) collective-permute-start(bf16[128,4096]{1,0:T(8,128)(2,1)} %collective-permute-done.refs_0_.refs_1_), channel_id=1, source_target_pairs={{0,4},{1,5},{2,6},{3,7},{4,8},{5,9},{6,10},{7,11},{8,12},{9,13},{1... | collective-permute-start | bytes 3145736 | tf_op jit(solution)/shard_map/ppermute | solution.py:55
  56.1 25.4 %collective-permute-start.2 = (bf16[128,4096]{1,0:T(8,128)(2,1)}, bf16[128,4096]{1,0:T(8,128)(2,1)S(1)}, u32[]{:S(2)}, u32[]{:S(2)}) collective-permute-start(bf16[128,4096]{1,0:T(8,128)(2,1)} %collective-permute-done.refs_0_.refs_1_), channel_id=1, source_target_pairs={{0,12},{1,13},{2,14},{3,15},{4,0},{5,1},{6,2},{7,3},{8,4},{9,5},{1... | collective-permute-start | bytes 3145736 | tf_op jit(solution)/shard_map/ppermute | solution.py:55
  57.7 3.3 %copy-start.21 = (bf16[128,4096]{1,0:T(8,128)(2,1)}, bf16[128,4096]{1,0:T(8,128)(2,1)S(1)}, u32[]{:S(2)}) copy-start(bf16[128,4096]{1,0:T(8,128)(2,1)S(1)} %collective-permute-done.8.refs_5_) | copy-start | bytes 3145732
  57.7 26.5 %collective-permute-start.7 = (bf16[128,4096]{1,0:T(8,128)(2,1)S(1)}, bf16[128,4096]{1,0:T(8,128)(2,1)S(1)}, u32[]{:S(2)}, u32[]{:S(2)}) collective-permute-start(bf16[128,4096]{1,0:T(8,128)(2,1)S(1)} %far.1.refs_4_), channel_id=1, source_target_pairs={{0,2},{1,3},{2,0},{3,1},{4,6},{5,7},{6,4},{7,5},{8,10},{9,11},{10,... | collective-permute-start | bytes 3145736 | tf_op jit(solution)/shard_map/ppermute | solution.py:55
  61.0 1.0 copy-start.22
  81.4 6.8 %copy-start.10 = (bf16[128,4096]{1,0:T(8,128)(2,1)}, bf16[128,4096]{1,0:T(8,128)(2,1)S(1)}, u32[]{:S(2)}) copy-start(bf16[128,4096]{1,0:T(8,128)(2,1)S(1)} %collective-permute-done.1.refs_0_) | copy-start | bytes 3145732
  81.5 6.7 %copy-start.12 = (bf16[128,4096]{1,0:T(8,128)(2,1)}, bf16[128,4096]{1,0:T(8,128)(2,1)S(1)}, u32[]{:S(2)}) copy-start(bf16[128,4096]{1,0:T(8,128)(2,1)S(1)} %collective-permute-done.2.refs_1_) | copy-start | bytes 3145732
  84.2 4.0 %copy-start.14 = (bf16[128,4096]{1,0:T(8,128)(2,1)}, bf16[128,4096]{1,0:T(8,128)(2,1)S(1)}, u32[]{:S(2)}) copy-start(bf16[128,4096]{1,0:T(8,128)(2,1)S(1)} %collective-permute-done.7.refs_2_) | copy-start | bytes 3145732
  84.2 3.8 %copy-start.8 = (f32[512,4096]{1,0:T(8,128)S(1)}, f32[512,4096]{1,0:T(8,128)}, u32[]{:S(2)}) copy-start(f32[512,4096]{1,0:T(8,128)} %get-tuple-element.20.refs_3_.refs_5_) | copy-start | bytes 25165828
  88.2 5.9 %collective-permute-start.13 = (bf16[384,4096]{1,0:T(8,128)(2,1)S(1)}, bf16[384,4096]{1,0:T(8,128)(2,1)}, u32[]{:S(2)}, u32[]{:S(2)}) collective-permute-start(bf16[384,4096]{1,0:T(8,128)(2,1)S(1)} %other.1), channel_id=1, source_target_pairs={{0,1},{1,0},{2,3},{3,2},{4,5},{5,4},{6,7},{7,6},{8,9},{9,8},{10,11... | collective-permute-start | bytes 9437192 | tf_op jit(solution)/shard_map/ppermute | solution.py:55
  103.0 19.2 %collective-permute-start.14 = (s16[64,4224]{1,0:T(8,128)(2,1)S(1)}, s16[64,4224]{1,0:T(8,128)(2,1)S(1)}, u32[]{:S(2)}, u32[]{:S(2)}) collective-permute-start(s16[64,4224]{1,0:T(8,128)(2,1)S(1)} %get-tuple-element.21), channel_id=1, source_target_pairs={{0,96},{1,97},{2,98},{3,99},{4,100},{5,101},{6,102},{7,103},{8,104... | collective-permute-start | bytes 1622024 | tf_op jit(solution)/shard_map/ppermute | solution.py:55
  105.2 38.7 %collective-permute-start.15 = (s16[64,4224]{1,0:T(8,128)(2,1)S(1)}, s16[64,4224]{1,0:T(8,128)(2,1)S(1)}, u32[]{:S(2)}, u32[]{:S(2)}) collective-permute-start(s16[64,4224]{1,0:T(8,128)(2,1)S(1)} %get-tuple-element.22), channel_id=1, source_target_pairs={{0,80},{1,81},{2,82},{3,83},{4,84},{5,85},{6,86},{7,87},{8,88},{9,... | collective-permute-start | bytes 1622024 | tf_op jit(solution)/shard_map/ppermute | solution.py:55
  108.5 37.2 %collective-permute-start.16 = (s16[64,4224]{1,0:T(8,128)(2,1)S(1)}, s16[64,4224]{1,0:T(8,128)(2,1)S(1)}, u32[]{:S(2)}, u32[]{:S(2)}) collective-permute-start(s16[64,4224]{1,0:T(8,128)(2,1)S(1)} %get-tuple-element.23), channel_id=1, source_target_pairs={{0,112},{1,113},{2,114},{3,115},{4,116},{5,117},{6,118},{7,119},{8... | collective-permute-start | bytes 1622024 | tf_op jit(solution)/shard_map/ppermute | solution.py:55
  109.2 45.3 %collective-permute-start.17 = (s16[64,4224]{1,0:T(8,128)(2,1)S(1)}, s16[64,4224]{1,0:T(8,128)(2,1)S(1)}, u32[]{:S(2)}, u32[]{:S(2)}) collective-permute-start(s16[64,4224]{1,0:T(8,128)(2,1)S(1)} %get-tuple-element.24), channel_id=1, source_target_pairs={{0,64},{1,65},{2,66},{3,67},{4,68},{5,69},{6,70},{7,71},{8,72},{9,... | collective-permute-start | bytes 1622024 | tf_op jit(solution)/shard_map/ppermute | solution.py:55
  110.0 45.1 %collective-permute-start.18 = (s16[64,4224]{1,0:T(8,128)(2,1)S(1)}, s16[64,4224]{1,0:T(8,128)(2,1)S(1)}, u32[]{:S(2)}, u32[]{:S(2)}) collective-permute-start(s16[64,4224]{1,0:T(8,128)(2,1)S(1)} %get-tuple-element.25), channel_id=1, source_target_pairs={{0,32},{1,33},{2,34},{3,35},{4,36},{5,37},{6,38},{7,39},{8,40},{9,... | collective-permute-start | bytes 1622024 | tf_op jit(solution)/shard_map/ppermute | solution.py:55
  122.2 43.8 %collective-permute-start.19 = (s16[64,4224]{1,0:T(8,128)(2,1)S(1)}, s16[64,4224]{1,0:T(8,128)(2,1)S(1)}, u32[]{:S(2)}, u32[]{:S(2)}) collective-permute-start(s16[64,4224]{1,0:T(8,128)(2,1)S(1)} %get-tuple-element.26), channel_id=1, source_target_pairs={{0,16},{1,17},{2,18},{3,19},{4,20},{5,21},{6,22},{7,23},{8,24},{9,... | collective-permute-start | bytes 1622024 | tf_op jit(solution)/shard_map/ppermute | solution.py:55
  143.8 22.2 %collective-permute-start.20 = (s16[64,4224]{1,0:T(8,128)(2,1)S(1)}, s16[64,4224]{1,0:T(8,128)(2,1)S(1)}, u32[]{:S(2)}, u32[]{:S(2)}) collective-permute-start(s16[64,4224]{1,0:T(8,128)(2,1)S(1)} %get-tuple-element.27), channel_id=1, source_target_pairs={{0,48},{1,49},{2,50},{3,51},{4,52},{5,53},{6,54},{7,55},{8,56},{9,... | collective-permute-start | bytes 1622024 | tf_op jit(solution)/shard_map/ppermute | solution.py:55
  145.7 66.5 %collective-permute-start.23 = (f32[48,4096]{1,0:T(8,128)}, f32[48,4096]{1,0:T(8,128)}, u32[]{:S(2)}, u32[]{:S(2)}) collective-permute-start(f32[48,4096]{1,0:T(8,128)} %pad_maximum_fusion), channel_id=1, source_target_pairs={{16,0},{17,1},{18,2},{19,3},{20,4},{21,5},{22,6},{23,7},{24,8},{25... | collective-permute-start | bytes 2359304 | tf_op jit(solution)/shard_map/ppermute | solution.py:55
  166.0 9.6 %copy-start.11 = (bf16[128,4096]{1,0:T(8,128)(2,1)S(1)}, bf16[128,4096]{1,0:T(8,128)(2,1)}, u32[]{:S(2)}) copy-start(bf16[128,4096]{1,0:T(8,128)(2,1)} %copy-done.10) | copy-start | bytes 3145732
  166.0 9.6 %copy-start.13 = (bf16[128,4096]{1,0:T(8,128)(2,1)S(1)}, bf16[128,4096]{1,0:T(8,128)(2,1)}, u32[]{:S(2)}) copy-start(bf16[128,4096]{1,0:T(8,128)(2,1)} %copy-done.12) | copy-start | bytes 3145732
  166.0 9.6 %copy-start.15 = (bf16[128,4096]{1,0:T(8,128)(2,1)S(1)}, bf16[128,4096]{1,0:T(8,128)(2,1)}, u32[]{:S(2)}) copy-start(bf16[128,4096]{1,0:T(8,128)(2,1)} %copy-done.14) | copy-start | bytes 3145732
  169.8 42.4 %collective-permute-start.21 = (f32[16,4096]{1,0:T(8,128)}, f32[16,4096]{1,0:T(8,128)S(1)}, u32[]{:S(2)}, u32[]{:S(2)}) collective-permute-start(f32[16,4096]{1,0:T(8,128)} %get-tuple-element.36), channel_id=1, source_target_pairs={{0,16},{1,17},{2,18},{3,19},{4,20},{5,21},{6,22},{7,23},{8,24},{9,... | collective-permute-start | bytes 786440 | tf_op jit(solution)/shard_map/ppermute | solution.py:55
  173.1 39.1 %collective-permute-start.22 = (f32[16,4096]{1,0:T(8,128)}, f32[16,4096]{1,0:T(8,128)}, u32[]{:S(2)}, u32[]{:S(2)}) collective-permute-start(f32[16,4096]{1,0:T(8,128)} %get-tuple-element.35), channel_id=1, source_target_pairs={{16,0},{17,1},{18,2},{19,3},{20,4},{21,5},{22,6},{23,7},{24,8},{25... | collective-permute-start | bytes 786440 | tf_op jit(solution)/shard_map/ppermute | solution.py:55
  175.7 8.7 %copy-start.6 = (bf16[2048,512]{1,0:T(8,128)(2,1)S(1)}, bf16[2048,512]{1,0:T(8,128)(2,1)}, u32[]{:S(2)}) copy-start(bf16[2048,512]{1,0:T(8,128)(2,1)} %gate_ref.7) | copy-start | bytes 6291460
  184.4 2.2 copy-start
  186.6 8.6 %copy-start.23 = (s32[1,9]{1,0:T(1,128)S(1)}, s32[1,9]{1,0:T(1,128)}, u32[]{:S(2)}) copy-start(s32[1,9]{1,0:T(1,128)} %param.19) | copy-start | bytes 112
  186.6 8.6 %copy-start.24 = (s32[1,9]{1,0:T(1,128)S(1)}, s32[1,9]{1,0:T(1,128)}, u32[]{:S(2)}) copy-start(s32[1,9]{1,0:T(1,128)} %param.18) | copy-start | bytes 112
  190.3 1.3 collective-permute-start.24
  191.5 8.8 %collective-permute-start.25 = (f32[16,1,128]{2,1,0:T(1,128)S(1)}, f32[16,1,128]{2,1,0:T(1,128)S(1)}, u32[]{:S(2)}, u32[]{:S(2)}) collective-permute-start(f32[16,1,128]{2,1,0:T(1,128)S(1)} %add.275), channel_id=1, source_target_pairs={{0,2},{1,3},{2,0},{3,1},{4,6},{5,7},{6,4},{7,5},{8,10},{9,11},{10,... | collective-permute-start | bytes 24584 | tf_op jit(solution)/shard_map/ppermute | solution.py:55
  200.5 2.2 copy-start.1
  202.6 1.6 copy-start.7
  204.2 8.0 %copy-start.16 = (f32[1,96,4096]{2,1,0:T(8,128)S(1)}, f32[1,96,4096]{2,1,0:T(8,128)}, u32[]{:S(2)}) copy-start(f32[1,96,4096]{2,1,0:T(8,128)} %master_ref.1) | copy-start | bytes 4718596
  204.2 8.0 %copy-start.17 = (f32[1,96,4096]{2,1,0:T(8,128)S(1)}, f32[1,96,4096]{2,1,0:T(8,128)}, u32[]{:S(2)}) copy-start(f32[1,96,4096]{2,1,0:T(8,128)} %first_ref.1) | copy-start | bytes 4718596
  204.2 8.0 %copy-start.18 = (f32[1,96,4096]{2,1,0:T(8,128)S(1)}, f32[1,96,4096]{2,1,0:T(8,128)}, u32[]{:S(2)}) copy-start(f32[1,96,4096]{2,1,0:T(8,128)} %second_ref.1) | copy-start | bytes 4718596

commit v2 on v1

v2 whole, which is shorter than its diff:
```python
import jax
import jax.numpy as jnp
from jax import lax
from jax.experimental import pallas as pl
from jax.experimental.pallas import tpu as pltpu
from jax.sharding import PartitionSpec as P

GROUP = 2048

norm_eps = 1e-05
beta_one = 0.9
beta_two = 0.95
adam_eps = 1e-08
learn_rate = 0.0003
weight_decay = 0.1
adam_step = 1000.0

N_X, N_Y = 4, 4
AXES = ("dp", "tensor")
TILE = 1024
TOP, FINE = 32700.0, 256.0
BLOCK = 128
HALO = 16
CAP = 96
OWNERS = ((1, 0), (1, 1), (3, 0), (3, 1), (2, 0), (2, 1), (0, 0), (0, 1))
HALF = 2048
GRANT = 24
EARLY = ((0, 0), (0, 1), (3, 0), (1, 0))
MIDDLE = ((2, 0), (1, 1), (3, 1))
LATE = ((2, 1),)
F32 = jnp.float32
BF16 = jnp.bfloat16


def position(flat):
    dp, tensor = flat // 16, flat % 16
    return dp % 4, tensor // 4, dp // 4, (tensor // 2) % 2, tensor % 2


def flat_of(x, y, zl, zh, c):
    return (zl * 4 + x) * 16 + (y * 2 + zh) * 2 + c


def pairs_of(move):
    return [(i, flat_of(*move(*position(i)))) for i in range(128)]


TO_CORE = pairs_of(lambda x, y, zl, zh, c: (x, y, zl, zh, 1 - c))
TO_ZHI = pairs_of(lambda x, y, zl, zh, c: (x, y, zl, 1 - zh, c))
TO_YP = pairs_of(lambda x, y, zl, zh, c: (x, (y + 1) % N_Y, zl, zh, c))
TO_YM = pairs_of(lambda x, y, zl, zh, c: (x, (y - 1) % N_Y, zl, zh, c))
TO_ZLO = pairs_of(lambda x, y, zl, zh, c: (x, y, 1 - zl, zh, c))
TO_X = [pairs_of(lambda x, y, zl, zh, c: ((x + dx) % N_X, y, zl, zh, c)) for dx in (1, 3, 2)]
TO_NEXT = [(i, i + 16) for i in range(112)]
TO_LAST = [(i + 16, i) for i in range(112)]


def move(value, pairs):
    return lax.ppermute(value, AXES, pairs)


def tied(value, other):
    late = other[(0,) * other.ndim] > 1e38
    return jnp.where(late, jnp.zeros_like(value), value)


def params(mib):
    return pltpu.CompilerParams(vmem_limit_bytes=mib * 2**20)


def cost(time):
    return pl.CostEstimate(flops=0, bytes_accessed=int(time * 3.3e6), transcendentals=0)


def eye():
    rows = lax.broadcasted_iota(jnp.int32, (BLOCK, BLOCK), 0)
    cols = lax.broadcasted_iota(jnp.int32, (BLOCK, BLOCK), 1)
    return rows == cols


def column_of(row):
    return jnp.sum(jnp.where(eye(), jnp.broadcast_to(row, (BLOCK, BLOCK)), 0.0), axis=1, keepdims=True)


def row_of(column):
    return jnp.sum(jnp.where(eye(), jnp.broadcast_to(column, (BLOCK, BLOCK)), 0.0), axis=0, keepdims=True)


def square_kernel(mixer_ref, gate_ref, out_ref):
    gate = gate_ref[...].astype(F32)
    gated = mixer_ref[...].astype(F32) * (gate * jax.nn.sigmoid(gate))
    total = jnp.sum(gated * gated, axis=1, keepdims=True)
    for k in range(out_ref.shape[0]):
        out_ref[k] = row_of(total[k * BLOCK : (k + 1) * BLOCK])


def hidden_kernel(order_ref, mixer_ref, gate_ref, inverse_ref, gain_ref, out_ref, turned):
    gate = gate_ref[...].astype(F32)
    gated = mixer_ref[...].astype(F32) * (gate * jax.nn.sigmoid(gate))
    normed = gated * column_of(inverse_ref[0])
    hidden = normed * gain_ref[...]
    turned[...] = hidden.T
    x, zl = order_ref[16], order_ref[17]
    for k, (dx, dz) in enumerate(OWNERS):
        start = lax.rem(zl + dz, 2) * 256 + lax.rem(x + dx, N_X) * 64
        out_ref[k * 64 : (k + 1) * 64, :] = turned[pl.ds(pl.multiple_of(start, 64), 64), :].astype(BF16)


def centre_kernel(order_ref, back_ref, mixer_ref, gate_ref, inverse_ref, gain_ref, out_ref):
    gate = gate_ref[...].astype(F32)
    gated = mixer_ref[...].astype(F32) * (gate * jax.nn.sigmoid(gate))
    normed = gated * column_of(inverse_ref[0])
    scaled = back_ref[...] * gain_ref[...]
    out_ref[0] = row_of(jnp.sum(scaled * normed, axis=1, keepdims=True))


def grads_kernel(order_ref, back_ref, mixer_ref, gate_ref, inverse_ref, centre_ref, gain_ref, input_ref, gate_out_ref):
    gate = gate_ref[...].astype(F32)
    mixer = mixer_ref[...].astype(F32)
    sig = jax.nn.sigmoid(gate)
    activated = gate * sig
    slope = sig * (1.0 + gate * (1.0 - sig))
    inverse = column_of(inverse_ref[0])
    normed = mixer * activated * inverse
    scaled = back_ref[...] * gain_ref[...]
    gated_back = inverse * (scaled - normed * column_of(centre_ref[0]))
    input_ref[...] = (gated_back * activated).astype(BF16)
    gate_out_ref[...] = (gated_back * mixer * slope).astype(BF16)


def fetches(pieces, cot, sems, n):
    at, made = 0, []
    cols = pl.ds(n * TILE, TILE)
    for piece in pieces:
        rows = piece.shape[0]
        made.append(pltpu.make_async_copy(piece.at[:, cols], cot.at[pl.ds(at, rows), cols], sems.at[n, len(made)]))
        at += rows
    return made


def arrive(pieces, cot, sems, steps, others=()):
    n = pl.program_id(0)

    @pl.when(n == 0)
    def _():
        for copy in others:
            copy.start()
        for k in range(steps):
            for copy in fetches(pieces, cot, sems, k):
                copy.start()
        for copy in others:
            copy.wait()

    for k in range(steps):

        @pl.when(n == k)
        def _():
            for copy in fetches(pieces, cot, sems, k):
                copy.wait()

    return cot[:, pl.ds(pl.multiple_of(n * TILE, TILE), TILE)]


def columns_of(hidden_ref, start, hid, sem):
    return pltpu.make_async_copy(hidden_ref.at[:, pl.ds(start, hid.shape[1])], hid, sem)


def back_step(cot, weight_ref, sums, back_ref, start, sem, steps):
    n = pl.program_id(0)
    part = lax.dot_general(cot, weight_ref[...], (((1,), (1,)), ((), ())), preferred_element_type=F32)

    @pl.when(n == 0)
    def _():
        sums[...] = part

    @pl.when(n > 0)
    def _():
        sums[...] += part

    @pl.when(n == steps - 1)
    def _():
        out = pltpu.make_async_copy(sums, back_ref.at[pl.ds(start, sums.shape[0])], sem)
        out.start()
        out.wait()


def first_kernel(count, start, steps, *refs):
    pieces, (hidden_ref, weight_ref, grad_ref, back_ref, cot, hid, sums, sems, sem) = refs[:count], refs[count:]
    here = arrive(pieces, cot, sems, steps, [columns_of(hidden_ref, start, hid, sem)])
    grad_ref[...] = jnp.dot(hid[...], here, preferred_element_type=F32)
    back_step(here, weight_ref, sums, back_ref, start, sem, steps)


def next_kernel(count, start, steps, *refs):
    pieces = refs[:count]
    hidden_ref, weight_ref, before_ref, _, grad_ref, back_ref, cot, hid, sums, sems, sem = refs[count:]
    here = arrive(pieces, cot, sems, steps, [columns_of(hidden_ref, start, hid, sem)])
    grad_ref[...] = before_ref[...] + jnp.dot(hid[...], here, preferred_element_type=F32)
    back_step(here, weight_ref, sums, back_ref, start, sem, steps)


def scale_of(code):
    return jnp.exp(code * (0.6931471805599453 / FINE))


def encode(rows, out, start, n):
    here = pl.ds(start, rows.shape[0])
    most = jnp.maximum(jnp.max(jnp.abs(rows), axis=1, keepdims=True), 1e-30)
    code = jnp.ceil(jnp.log2(most) * FINE)
    cols = pl.ds(pl.multiple_of(n * TILE, TILE), TILE)
    out[here, cols] = jnp.round(rows * (TOP / scale_of(code))).astype(jnp.int32).astype(jnp.int16)
    lanes = lax.broadcasted_iota(jnp.int32, (rows.shape[0], 128), 1)
    before = jnp.where(n == 0, 0, out[here, HALF:].astype(jnp.int32))
    out[here, HALF:] = jnp.where(lanes == n, code.astype(jnp.int32), before).astype(jnp.int16)


def decode(part_ref, code_ref, n):
    lanes = lax.broadcasted_iota(jnp.int32, code_ref.shape, 1)
    code = jnp.where(lanes == n, code_ref[...].astype(jnp.int32).astype(F32), 0.0)
    scale = scale_of(jnp.sum(code, axis=1, keepdims=True)) / TOP
    return part_ref[...].astype(jnp.int32).astype(F32) * scale


def late_kernel(count, start, steps, *refs):
    pieces = refs[:count]
    hidden_ref, weight_ref, before_ref, _, *to_x, to_z, mine_a, mine_b, back_ref, cot, hid, sums, sems, sem = refs[count:]
    n = pl.program_id(0)
    here = arrive(pieces, cot, sems, steps, [columns_of(hidden_ref, start, hid, sem)])
    back_step(here, weight_ref, sums, back_ref, start, sem, steps)
    grad = before_ref[...] + jnp.dot(hid[...], here, preferred_element_type=F32)

    @pl.when(n < steps // 2)
    def _():
        for k, out in enumerate(to_x):
            encode(grad[k * 128 : (k + 1) * 128], out, 0, n)
        mine_a[...] = grad[384:]

    @pl.when(n >= steps // 2)
    def _():
        for k in range(4):
            encode(grad[k * 128 + 64 : (k + 1) * 128], to_z, k * 64, n - steps // 2)
            mine_b[k * 64 : (k + 1) * 64] = grad[k * 128 : k * 128 + 64]


def middle_kernel(*refs):
    got_a, got_z, (mine_a, mine_b) = refs[:6], refs[6:8], refs[8:10]
    send_a, *send_b, keep_a, keep_b = refs[-6:]
    n = pl.program_id(0)
    total = mine_a[...]
    for k in range(3):
        total += decode(got_a[2 * k], got_a[2 * k + 1], n)
    keep_a[...] = total[:64]
    encode(total[64:], send_a, 0, n)
    total = mine_b[...] + decode(got_z[0], got_z[1], n)
    for k, out in enumerate(send_b):
        encode(total[k * 64 : (k + 1) * 64], out, 0, n)
    keep_b[...] = total[192:]


def sum_kernel(*refs):
    got_a, got_b, (keep_a, keep_b) = refs[:2], refs[2:8], refs[8:10]
    out_ref, up_ref, down_ref = refs[-3:]
    n = pl.program_id(0)
    total_a = keep_a[...] + decode(got_a[0], got_a[1], n)
    total_b = keep_b[...]
    for k in range(3):
        total_b += decode(got_b[2 * k], got_b[2 * k + 1], n)
    for total, start in ((total_a, 0), (total_b, HALF)):
        cols = pl.ds(pl.multiple_of(start + n * TILE, TILE), TILE)
        out_ref[:, cols] = total
        up_ref[:, cols] = total[64 - HALO :]
        down_ref[:, cols] = total[:HALO]


ANYWHERE = pl.BlockSpec(memory_space=pl.ANY)


def wide(rows):
    return pl.BlockSpec((rows, TILE), lambda n: (0, n))


def kept(rows, cols, at=0):
    return pl.BlockSpec((rows, cols), lambda n: (0, at))


def products(pieces, hidden, weight, start, before=None):
    tokens = sum(p.shape[0] for p in pieces)
    channels, width = weight.shape
    steps, count = width // TILE, len(pieces)
    grad = jax.ShapeDtypeStruct((channels, width), F32)
    back = jax.ShapeDtypeStruct((hidden.shape[1], channels), F32)
    kernel = first_kernel if before is None else next_kernel
    return pl.pallas_call(
        lambda *refs: kernel(count, start, steps, *refs),
        grid=(steps,),
        in_specs=[ANYWHERE] * (count + 1) + [wide(channels)] + ([] if before is None else [wide(channels), ANYWHERE]),
        out_specs=[wide(channels), ANYWHERE],
        out_shape=[grad, back],
        input_output_aliases={} if before is None else {count + 3: 1},
        scratch_shapes=[
            pltpu.VMEM((tokens, width), BF16),
            pltpu.VMEM((channels, tokens), BF16),
            pltpu.VMEM((tokens, channels), F32),
            pltpu.SemaphoreType.DMA((steps, count)),
            pltpu.SemaphoreType.DMA,
        ],
        compiler_params=params(GRANT),
        cost_estimate=cost(18 if before is None else 16),
        name="products",
    )(*pieces, hidden, weight, *(before or []))


def late_products(pieces, hidden, weight, start, before):
    tokens = sum(p.shape[0] for p in pieces)
    channels, width = weight.shape
    steps, count = width // TILE, len(pieces)
    half = steps // 2
    code = lambda rows: jax.ShapeDtypeStruct((rows, HALF + 128), jnp.int16)
    full = lambda rows: jax.ShapeDtypeStruct((rows, HALF), F32)
    back = jax.ShapeDtypeStruct(before[1].shape, F32)
    return pl.pallas_call(
        lambda *refs: late_kernel(count, start, steps, *refs),
        grid=(steps,),
        in_specs=[ANYWHERE] * (count + 1) + [wide(channels), wide(channels), ANYWHERE],
        out_specs=[kept(128, HALF + 128)] * 3
        + [
            kept(256, HALF + 128),
            pl.BlockSpec((128, TILE), lambda n: (0, jnp.minimum(n, half - 1))),
            pl.BlockSpec((256, TILE), lambda n: (0, jnp.maximum(n - half, 0))),
            ANYWHERE,
        ],
        out_shape=[code(128)] * 3 + [code(256), full(128), full(256), back],
        input_output_aliases={count + 3: 6},
        scratch_shapes=[
            pltpu.VMEM((tokens, width), BF16),
            pltpu.VMEM((channels, tokens), BF16),
            pltpu.VMEM((tokens, channels), F32),
            pltpu.SemaphoreType.DMA((steps, count)),
            pltpu.SemaphoreType.DMA,
        ],
        compiler_params=params(GRANT),
        cost_estimate=cost(9),
        name="late_products",
    )(*pieces, hidden, weight, *before)


def coded(rows):
    return [wide(rows), kept(rows, 128, HALF // 128)]


def twice(arrays):
    return [a for array in arrays for a in (array, array)]


def middle_sums(got_a, got_z, mine_a, mine_b, after):
    code = jax.ShapeDtypeStruct((64, HALF + 128), jnp.int16)
    keep = jax.ShapeDtypeStruct((64, HALF), F32)
    return pl.pallas_call(
        middle_kernel,
        grid=(HALF // TILE,),
        in_specs=coded(128) * 3 + coded(256) + [wide(128), wide(256)] + [ANYWHERE] * len(after),
        out_specs=[kept(64, HALF + 128)] * 4 + [wide(64)] * 2,
        out_shape=[code] * 4 + [keep] * 2,
        compiler_params=params(GRANT),
        cost_estimate=cost(3),
        name="middle_sums",
    )(*twice(got_a), *twice([got_z]), mine_a, mine_b, *after)


def last_sums(got_a, got_b, keep_a, keep_b, after):
    width = 2 * HALF
    return pl.pallas_call(
        sum_kernel,
        grid=(HALF // TILE,),
        in_specs=coded(64) * 4 + [wide(64)] * 2 + [ANYWHERE] * len(after),
        out_specs=[kept(64, width), kept(HALO, width), kept(HALO, width)],
        out_shape=[jax.ShapeDtypeStruct((rows, width), F32) for rows in (64, HALO, HALO)],
        compiler_params=params(GRANT),
        cost_estimate=cost(3),
        name="last_sums",
    )(*twice([got_a]), *twice(got_b), keep_a, keep_b, *after)


def bounds_of(order_ref, old_ref, new_ref):
    dp = order_ref[17] * 4 + order_ref[16]
    new_start, old_start = new_ref[0, dp], old_ref[0, dp]
    return new_start - (64 * dp - HALO), new_start - old_start, old_ref[0, dp + 1] - old_start, new_ref[0, dp + 1] - new_start


def back_by(rows, by):
    return pltpu.roll(rows, lax.rem(128 - by, 128), 0)[:CAP]


def place_kernel(order_ref, old_ref, new_ref, *refs):
    states, arrived_ref, outs = refs[:3], refs[3], refs[4:]
    _, moved, old_count, _ = bounds_of(order_ref, old_ref, new_ref)
    width = arrived_ref.shape[1]
    slots = lax.broadcasted_iota(jnp.int32, (128, width), 0)
    pad = jnp.zeros((128 - CAP, width), F32)
    for k, (ref, out) in enumerate(zip(states, outs)):
        extra = jnp.concatenate([arrived_ref[k * HALO : (k + 1) * HALO, :], jnp.zeros((128 - HALO, width), F32)], axis=0)
        extra = pltpu.roll(extra, old_count, 0)
        out[...] = back_by(jnp.where(slots < old_count, jnp.concatenate([ref[0], pad], axis=0), extra), moved)


def adam_kernel(order_ref, old_ref, new_ref, grad_ref, up_ref, down_ref, master_ref, first_ref, second_ref, *outs):
    new_master, new_first, new_second = outs
    offset, _, _, new_count = bounds_of(order_ref, old_ref, new_ref)
    width = grad_ref.shape[1]
    pad = jnp.zeros((128 - CAP, width), F32)
    grad = back_by(jnp.concatenate([up_ref[...], grad_ref[...], down_ref[...], pad], axis=0), offset) / 8.0
    valid = lax.broadcasted_iota(jnp.int32, (CAP, width), 0) < new_count
    first = beta_one * first_ref[...] + (1.0 - beta_one) * grad
    new_first[0] = jnp.where(valid, first, 0.0)
    second = beta_two * second_ref[...] + (1.0 - beta_two) * grad * grad
    new_second[0] = jnp.where(valid, second, 0.0)
    corr_one = 1.0 - beta_one**adam_step
    corr_two = 1.0 - beta_two**adam_step
    update = first / corr_one / (jnp.sqrt(second / corr_two) + adam_eps)
    master = master_ref[...]
    new_master[0] = jnp.where(valid, master - learn_rate * (update + weight_decay * master), 0.0)


def share_call(kernel, tile, in_specs, out_specs, out_shape, name):
    width = 2 * HALF
    return pl.pallas_call(
        kernel,
        grid_spec=pltpu.PrefetchScalarGridSpec(
            num_scalar_prefetch=3, grid=(width // tile,), in_specs=in_specs, out_specs=out_specs
        ),
        out_shape=out_shape,
        compiler_params=params(GRANT),
        cost_estimate=cost(6),
        name=name,
    )


def place(scalars, states, arrived):
    tile = 1024
    state = pl.BlockSpec((1, CAP, tile), lambda i, *_: (0, 0, i))
    part = lambda n: pl.BlockSpec((n, tile), lambda i, *_: (0, i))
    out = jax.ShapeDtypeStruct(states[0].shape[1:], F32)
    return share_call(place_kernel, tile, [state] * 3 + [part(3 * HALO)], [part(CAP)] * 3, [out] * 3, "place")(
        *scalars, *states, arrived
    )


def adam(scalars, grad, up, down, placed):
    tile = 1024
    state = pl.BlockSpec((1, CAP, tile), lambda i, *_: (0, 0, i))
    part = lambda n: pl.BlockSpec((n, tile), lambda i, *_: (0, i))
    out = jax.ShapeDtypeStruct((1, *placed[0].shape), F32)
    in_specs = [part(64), part(HALO), part(HALO)] + [part(CAP)] * 3
    return share_call(adam_kernel, tile, in_specs, [state] * 3, [out] * 3, "adam")(*scalars, grad, up, down, *placed)


def local(
    cotangent,
    mixer_out,
    gate,
    norm_gain,
    out_weight,
    old_master,
    old_first,
    old_second,
    old_bounds,
    new_bounds,
):
    dp = lax.axis_index("dp")
    tensor = lax.axis_index("tensor")
    x, zl = dp % 4, dp // 4
    y, zh, core = tensor // 4, (tensor // 2) % 2, tensor % 2
    tokens, channels = mixer_out.shape
    blocks = tokens // BLOCK

    order = jnp.stack(
        [
            ((y + dy) % N_Y * 2 + (zh + dz) % 2) * 2 + (core + dc) % 2
            for group in (EARLY, MIDDLE, LATE)
            for dc in (0, 1)
            for dy, dz in group
        ]
        + [x, zl]
    ).astype(jnp.int32)

    row_spec = pl.BlockSpec((4, 1, BLOCK), lambda i: (i, 0, 0))
    block_spec = pl.BlockSpec((4 * BLOCK, channels), lambda i: (i, 0))
    rows_shape = jax.ShapeDtypeStruct((blocks, 1, BLOCK), F32)

    def chip_total(part):
        return part + move(part, TO_CORE)

    def group_total(part):
        return part + move(part, TO_ZHI)

    squares = pl.pallas_call(
        square_kernel,
        grid=(blocks // 4,),
        in_specs=[block_spec, block_spec],
        out_specs=row_spec,
        out_shape=rows_shape,
        compiler_params=params(60),
        cost_estimate=cost(3),
        name="squares",
    )(mixer_out, gate)
    squares = chip_total(squares)
    inverse = lax.rsqrt(group_total(squares) / GROUP + norm_eps)

    gain = norm_gain[None, :]
    there = pl.BlockSpec((BLOCK, channels), lambda i, o: (o[i], 0))
    here = pl.BlockSpec((BLOCK, channels), lambda i, o: (i, 0))
    there_row = pl.BlockSpec((1, 1, BLOCK), lambda i, o: (o[i], 0, 0))
    gain_spec = pl.BlockSpec((1, channels), lambda i, o: (0, 0))

    def ordered(kernel, in_specs, out_specs, out_shape, name, time, scratch=()):
        return pl.pallas_call(
            kernel,
            grid_spec=pltpu.PrefetchScalarGridSpec(
                num_scalar_prefetch=1, grid=(blocks,), in_specs=in_specs, out_specs=out_specs, scratch_shapes=scratch
            ),
            out_shape=out_shape,
            compiler_params=params(16),
            cost_estimate=cost(time),
            name=name,
        )

    hidden = ordered(
        hidden_kernel,
        [there, there, there_row, gain_spec],
        pl.BlockSpec((channels, BLOCK), lambda i, o: (0, i)),
        jax.ShapeDtypeStruct((channels, tokens), BF16),
        "hidden",
        5,
        [pltpu.VMEM((channels, BLOCK), F32)],
    )(order, mixer_out, gate, inverse, gain)

    states = (old_master, old_first, old_second)
    arrived = move(jnp.concatenate([s[0, :HALO] for s in states], axis=0), TO_LAST)

    own = cotangent
    own_z = move(own, TO_ZHI)
    own_m, own_p = move(own, TO_YP), move(own, TO_YM)
    own_s = move(own, TO_CORE)
    own_z, own_m = tied(own_z, squares), tied(own_m, squares)
    far = move(own_m, TO_YP)
    other_p, other_m = move(own_z, TO_YM), move(own_m, TO_ZHI)
    early = [own, own_z, own_m, own_p, own_s, move(own_z, TO_CORE), move(own_m, TO_CORE), move(own_p, TO_CORE)]
    at = 0
    sums = products(early, hidden, out_weight, at)
    at += 8 * BLOCK
    half = BLOCK // 2
    last_a = move(tied(other_m[:half], sums[0]), TO_YP)
    last_b = move(tied(other_p[half:], sums[0]), TO_YM)
    middle = [far, other_p, other_m, move(far, TO_CORE), move(other_p, TO_CORE), move(other_m, TO_CORE)]
    sums = products(middle, hidden, out_weight, at, sums)
    at += 6 * BLOCK
    last_a, last_b = tied(last_a, sums[0]), tied(last_b, sums[0])
    last = [last_a, last_b, move(last_a, TO_CORE), move(last_b, TO_CORE)]
    *to_x, to_z, mine_a, mine_b, back = late_products(last, hidden, out_weight, at, sums)
    got_x, got_z = [move(code, pairs) for code, pairs in zip(to_x, TO_X)], move(to_z, TO_ZLO)

    centre = ordered(
        centre_kernel,
        [here, there, there, there_row, gain_spec],
        there_row,
        rows_shape,
        "centre",
        4,
    )(order, back, mixer_out, gate, inverse, gain)
    send_a, *send_b, keep_a, keep_b = middle_sums(got_x, got_z, mine_a, mine_b, [centre])
    centre = group_total(chip_total(centre)) / GROUP
    out_shape = jax.ShapeDtypeStruct((tokens, channels), BF16)
    input_grad, gate_grad = ordered(
        grads_kernel,
        [here, there, there, there_row, there_row, gain_spec],
        [there, there],
        [out_shape, out_shape],
        "grads",
        8,
    )(order, back, mixer_out, gate, inverse, centre, gain)

    scalars = (order, old_bounds, new_bounds)
    placed = place(scalars, states, arrived)
    got_a, got_b = move(send_a, TO_ZLO), [move(code, pairs) for code, pairs in zip(send_b, TO_X)]
    grad, last_rows, first_rows = last_sums(got_a, got_b, keep_a, keep_b, [input_grad, placed[0]])
    made = adam(scalars, grad, move(last_rows, TO_NEXT), move(first_rows, TO_LAST), placed)
    return (*made, input_grad, gate_grad)


def solution(mesh):
    return jax.shard_map(
        local,
        mesh=mesh,
        in_specs=(
            P(("dp", "tensor"), None),
            P("dp", "tensor"),
            P("dp", "tensor"),
            P("tensor"),
            P("tensor", None),
            P("tensor", "dp", None),
            P("tensor", "dp", None),
            P("tensor", "dp", None),
            P("tensor", None),
            P("tensor", None),
        ),
        out_specs=(
            P("tensor", "dp", None),
            P("tensor", "dp", None),
            P("tensor", "dp", None),
            P("dp", "tensor"),
            P("dp", "tensor"),
        ),
        check_vma=False,
    )
```

time: 223 us -> 184 us (0.83)
  waiting for transfers between devices: 84.5 us -> 64.7 us
  local copies, waits for them, and re-layouts: 21.6 us -> 5.37 us
  Pallas kernels: 70.4 us -> 65.3 us
  other arithmetic: 0.99 us -> 3.71 us
  starting transfers between devices: 38.3 us -> 41 us
  between operations: 5.72 us -> 3.24 us
    ppermute x26 -> x32, waiting for transfers between devices: 84.5 us -> 64.7 us  [move(): return lax.ppermute(value, AXES, pairs)]
    unnamed x50 -> x24, local copies, waits for them, and re-layouts: 15.6 us -> 2.61 us
    pallas_call x9 -> x8, Pallas kernels: 53.8 us -> 48.8 us  [the longest x2 24 us: products(): pl.pallas_call(lambda *refs: kernel(count, start, steps, *refs), grid=(st...]
    select_n x0 -> x6, other arithmetic: none -> 2.9 us  [tied(): return jnp.where(late, jnp.zeros_like(value), value)]
    ppermute x26 -> x32, starting transfers between devices: 38.3 us -> 41 us  [move(): return lax.ppermute(value, AXES, pairs)]
  transfers between devices with their start and end apart: 26 -> 32, of which waited for: 14 -> 11; matrix products, arithmetic and copies ran while one was open for 3% -> 4% of each run, Pallas kernels for 22% -> 29%
where the time goes in v2:
time: 184 us; the launch traced here: 183 us
  Pallas kernels  65.3 us (35%)
  waiting for transfers between devices  64.7 us (35%)
  starting transfers between devices  41 us (22%)
  local copies, waits for them, and re-layouts  5.37 us (3%)
  other arithmetic  3.71 us (2%)
  between operations  3.24 us (2%)
    ppermute x32, waiting for transfers between devices, move(): return lax.ppermute(value, AXES, pairs)  64.7 us
    ppermute x32, starting transfers between devices, move(): return lax.ppermute(value, AXES, pairs)  41 us
    pallas_call x2, Pallas kernels, products(): pl.pallas_call(lambda *refs: kernel(count, start, steps, *refs), grid=(st...  24 us
    pallas_call x1, Pallas kernels, local(): ordered(grads_kernel, [here, there, there, there_row, there_row, gain_spe...  7.99 us
    pallas_call x1, Pallas kernels, late_products(): pl.pallas_call(lambda *refs: late_kernel(count, start, steps, *refs), gri...  7.06 us
    pallas_call x1, Pallas kernels, place(): share_call(place_kernel, tile, [state] * 3 + [part(3 * HALO)], [part(CAP)...  6.09 us
    pallas_call x1, Pallas kernels, local(): ordered(hidden_kernel, [there, there, there_row, gain_spec], pl.BlockSpec...  4.86 us
    pallas_call x1, Pallas kernels, local(): pl.pallas_call(square_kernel, grid=(blocks // 4,), in_specs=[block_spec,...  4.33 us
  transfers between devices with their start and end apart: 32, of which 11 were waited for; matrix products, arithmetic and copies ran while one was open for 4% of the time, Pallas kernels for 29%

profile of v2, /device:TPU:6, one launch (start us, length us, event | category | flops | bytes accessed | tf_op | source)
XLA Modules:
  0.0 183.3 jit_solution(15245779867736413364)
XLA Ops:
  0.6 1.6 collective-permute-start.1
  2.3 4.3 %squares.1 = f32[16,1,128]{2,1,0:T(1,128)} custom-call(bf16[2048,512]{1,0:T(8,128)(2,1)} %mixer_ref.7, bf16[2048,512]{1,0:T(8,128)(2,1)} %gate_ref.7), custom_call_target="tpu_custom_call" | custom-call | bytes 9900000 | tf_op jit(solution)/shard_map/squares/pallas_call | solution.py:496
  6.6 3.9 %collective-permute-start.3 = (bf16[128,4096]{1,0:T(8,128)(2,1)}, bf16[128,4096]{1,0:T(8,128)(2,1)}, u32[]{:S(2)}, u32[]{:S(2)}) collective-permute-start(bf16[128,4096]{1,0:T(8,128)(2,1)} %refs_0_.2), channel_id=1, source_target_pairs={{0,2},{1,3},{2,0},{3,1},{4,6},{5,7},{6,4},{7,5},{8,10},{9,11},{10,... | collective-permute-start | bytes 3145736 | tf_op jit(solution)/shard_map/ppermute | solution.py:59
  10.5 1.7 collective-permute-start.10
  12.2 0.7 add.253
  12.9 0.5 slice.35
  14.0 13.0 %collective-permute-done.1 = bf16[128,4096]{1,0:T(8,128)(2,1)S(1)} collective-permute-done((bf16[128,4096]{1,0:T(8,128)(2,1)}, bf16[128,4096]{1,0:T(8,128)(2,1)S(1)}, u32[]{:S(2)}, u32[]{:S(2)}) %collective-permute-start.1) | collective-permute-done | bytes 1048608 | tf_op jit(solution)/shard_map/ppermute | solution.py:59
  27.1 1.0 copy-done.11
  28.1 1.4 broadcast_select_fusion.1.refs_2_
  29.5 0.1 collective-permute-start.13
  29.8 0.1 stack.75.order_ref
  29.9 0.0 copy-start.1
  29.9 0.0 copy-start.8
  29.9 4.0 %collective-permute-start.9 = (f32[16,1,128]{2,1,0:T(1,128)S(1)}, f32[16,1,128]{2,1,0:T(1,128)S(1)}, u32[]{:S(2)}, u32[]{:S(2)}) collective-permute-start(f32[16,1,128]{2,1,0:T(1,128)S(1)} %add.253), channel_id=1, source_target_pairs={{0,2},{1,3},{2,0},{3,1},{4,6},{5,7},{6,4},{7,5},{8,10},{9,11},{10,... | collective-permute-start | bytes 24584 | tf_op jit(solution)/shard_map/ppermute | solution.py:59
  33.9 0.8 collective-permute-done.3
  34.6 3.2 %collective-permute-start.5 = (bf16[128,4096]{1,0:T(8,128)(2,1)S(1)}, bf16[128,4096]{1,0:T(8,128)(2,1)S(1)}, u32[]{:S(2)}, u32[]{:S(2)}) collective-permute-start(bf16[128,4096]{1,0:T(8,128)(2,1)S(1)} %broadcast_select_fusion.1.refs_2_), channel_id=1, source_target_pairs={{0,2},{1,3},{2,0},{3,1},{4,6},{5,7},{6,4},{7,5},{8,10},{9,11},{10,... | collective-permute-start | bytes 3145736 | tf_op jit(solution)/shard_map/ppermute | solution.py:59
  37.9 1.3 broadcast_select_fusion.refs_1_
  39.2 1.7 collective-permute-start.2
  40.9 1.6 collective-permute-start.4
  42.6 0.2 collective-permute-start.14
  42.7 1.1 slice_bitcast_fusion
  43.9 0.0 copy-start
  43.9 4.9 %hidden.1.refs_8_.refs_6_.refs_4_ = bf16[512,2048]{1,0:T(8,128)(2,1)S(1)} custom-call(s32[18]{0:T(128)S(1)} %stack.75.order_ref, bf16[2048,512]{1,0:T(8,128)(2,1)S(1)} %copy-done.1, bf16[2048,512]{1,0:T(8,128)(2,1)S(1)} %copy-done.2, f32[16,1,128]{2,1,0:T(1,128)S(1)} %add_rsqrt_fusion.inverse_ref, f32[1,512]{1,0:T(1,128)S(1)} %bitcast.28), custom_call_target="tpu_custom_call" | custom-call | bytes 16500000 | tf_op jit(solution)/shard_map/hidden/pallas_call | solution.py:527
  48.8 12.9 %products.2 = (f32[512,4096]{1,0:T(8,128)S(1)}, f32[2048,512]{1,0:T(8,128)S(1)}) custom-call(bf16[128,4096]{1,0:T(8,128)(2,1)} %refs_0_.2, bf16[128,4096]{1,0:T(8,128)(2,1)S(1)} %broadcast_select_fusion.refs_1_, bf16[128,4096]{1,0:T(8,128)(2,1)S(1)} %broadcast_select_fusion.1.refs_2_, bf16[128,4096]{1,0:T(8,128)(2,1)} %collective-permute-done.10.refs_3_, ...), custom_call_target="tpu_custom_call" | custom-call | bytes 59400000 | tf_op jit(solution)/shard_map/products/pallas_call | solution.py:293
  61.7 0.6 slice.29
  62.9 0.4 collective-permute-start.8
  63.4 1.6 collective-permute-done.2.refs_0_
  65.0 1.5 collective-permute-done.4.refs_1_
  66.6 2.9 %collective-permute-start.16 = (bf16[64,4096]{1,0:T(8,128)(2,1)S(1)}, bf16[64,4096]{1,0:T(8,128)(2,1)S(1)}, u32[]{:S(2)}, u32[]{:S(2)}) collective-permute-start(bf16[64,4096]{1,0:T(8,128)(2,1)S(1)} %slice_select_fusion), channel_id=1, source_target_pairs={{0,12},{1,13},{2,14},{3,15},{4,0},{5,1},{6,2},{7,3},{8,4},{9,5},{1... | collective-permute-start | bytes 1572872 | tf_op jit(solution)/shard_map/ppermute | solution.py:59
  69.5 0.1 collective-permute-start.15
  69.6 11.1 %products.3 = (f32[512,4096]{1,0:T(8,128)S(1)}, f32[2048,512]{1,0:T(8,128)S(1)}) custom-call(bf16[128,4096]{1,0:T(8,128)(2,1)S(1)} %collective-permute-done.2.refs_0_, bf16[128,4096]{1,0:T(8,128)(2,1)S(1)} %collective-permute-done.4.refs_1_, bf16[128,4096]{1,0:T(8,128)(2,1)S(1)} %collective-permute-done.5.refs_2_, ...), custom_call_target="tpu_custom_call", output_to_operand_aliasing={{1}: (9, {})} | custom-call | bytes 52800000 | tf_op jit(solution)/shard_map/products/pallas_call | solution.py:293
  80.7 0.0 copy-start.4
  80.7 0.5 slice.28
  82.0 0.3 collective-permute-start.18
  82.3 2.5 %collective-permute-done.15 = bf16[64,4096]{1,0:T(8,128)(2,1)S(1)} collective-permute-done((bf16[64,4096]{1,0:T(8,128)(2,1)S(1)}, bf16[64,4096]{1,0:T(8,128)(2,1)S(1)}, u32[]{:S(2)}, u32[]{:S(2)}) %collective-permute-start.15) | collective-permute-done | bytes 524320 | tf_op jit(solution)/shard_map/ppermute | solution.py:59
  84.8 0.3 collective-permute-start.17
  85.1 1.8 %collective-permute-done.17.refs_2_ = bf16[64,4096]{1,0:T(8,128)(2,1)S(1)} collective-permute-done((bf16[64,4096]{1,0:T(8,128)(2,1)S(1)}, bf16[64,4096]{1,0:T(8,128)(2,1)S(1)}, u32[]{:S(2)}, u32[]{:S(2)}) %collective-permute-start.17) | collective-permute-done | bytes 524320 | tf_op jit(solution)/shard_map/ppermute | solution.py:59
  87.0 7.1 %late_products.1 = (s16[128,2176]{1,0:T(8,128)(2,1)S(1)}, s16[128,2176]{1,0:T(8,128)(2,1)S(1)}, s16[128,2176]{1,0:T(8,128)(2,1)S(1)}, s16[256,2176]{1,0:T(8,128)...) custom-call(bf16[64,4096]{1,0:T(8,128)(2,1)S(1)} %broadcast_select_f, ...), custom_call_target="tpu_custom_call", output_to_operand_aliasing={{6}: (7, {})} | custom-call | bytes 29700000 | tf_op jit(solution)/shard_map/late_products/pallas_call | solution.py:321
  94.1 1.1 collective-permute-start.22
  95.2 0.1 pad_maximum_fusion
  95.2 2.7 %collective-permute-start.29 = (f32[48,4096]{1,0:T(8,128)S(1)}, f32[48,4096]{1,0:T(8,128)S(1)}, u32[]{:S(2)}, u32[]{:S(2)}) collective-permute-start(f32[48,4096]{1,0:T(8,128)S(1)} %pad_maximum_fusion), channel_id=1, source_target_pairs={{16,0},{17,1},{18,2},{19,3},{20,4},{21,5},{22,6},{23,7},{24,8},{25... | collective-permute-start | bytes 2359304 | tf_op jit(solution)/shard_map/ppermute | solution.py:59
  98.0 0.1 collective-permute-start.19
  98.0 2.0 %collective-permute-start.20 = (s16[128,2176]{1,0:T(8,128)(2,1)S(1)}, s16[128,2176]{1,0:T(8,128)(2,1)S(1)}, u32[]{:S(2)}, u32[]{:S(2)}) collective-permute-start(s16[128,2176]{1,0:T(8,128)(2,1)S(1)} %get-tuple-element.38), channel_id=1, source_target_pairs={{0,48},{1,49},{2,50},{3,51},{4,52},{5,53},{6,54},{7,55},{8,56},{9,... | collective-permute-start | bytes 1671176 | tf_op jit(solution)/shard_map/ppermute | solution.py:59
  100.1 1.1 collective-permute-start.21
  101.2 3.7 %centre.1.refs_10_ = f32[16,1,128]{2,1,0:T(1,128)S(1)} custom-call(s32[18]{0:T(128)S(1)} %stack.75.order_ref, f32[2048,512]{1,0:T(8,128)S(1)} %get-tuple-element.43.back_ref, bf16[2048,512]{1,0:T(8,128)(2,1)S(1)} %copy-done.1, bf16[2048,512]{1,0:T(8,128)(2,1)S(1)} %copy-done.2, f32[16,1,128]{2,1,0:T(1,128)S(1)} %add_rsqrt_fusion.inverse_ref, ...), custom_call_target="tpu_custom_call" | custom-call | bytes 13200000 | tf_op jit(solution)/shard_map/centre/pallas_call | solution.py:562
  104.9 8.7 %collective-permute-done.19.refs_0_.refs_1_ = s16[128,2176]{1,0:T(8,128)(2,1)S(1)} collective-permute-done((s16[128,2176]{1,0:T(8,128)(2,1)S(1)}, s16[128,2176]{1,0:T(8,128)(2,1)S(1)}, u32[]{:S(2)}, u32[]{:S(2)}) %collective-permute-start.19) | collective-permute-done | bytes 557088 | tf_op jit(solution)/shard_map/ppermute | solution.py:59
  113.6 14.2 %collective-permute-done.20.refs_2_.refs_3_ = s16[128,2176]{1,0:T(8,128)(2,1)S(1)} collective-permute-done((s16[128,2176]{1,0:T(8,128)(2,1)S(1)}, s16[128,2176]{1,0:T(8,128)(2,1)S(1)}, u32[]{:S(2)}, u32[]{:S(2)}) %collective-permute-start.20) | collective-permute-done | bytes 557088 | tf_op jit(solution)/shard_map/ppermute | solution.py:59
  127.8 12.4 %collective-permute-done.21.refs_4_.refs_5_ = s16[128,2176]{1,0:T(8,128)(2,1)S(1)} collective-permute-done((s16[128,2176]{1,0:T(8,128)(2,1)S(1)}, s16[128,2176]{1,0:T(8,128)(2,1)S(1)}, u32[]{:S(2)}, u32[]{:S(2)}) %collective-permute-start.21) | collective-permute-done | bytes 557088 | tf_op jit(solution)/shard_map/ppermute | solution.py:59
  140.2 0.0 copy-start.10
  140.2 2.1 %middle_sums.1 = (s16[64,2176]{1,0:T(8,128)(2,1)S(1)}, s16[64,2176]{1,0:T(8,128)(2,1)S(1)}, s16[64,2176]{1,0:T(8,128)(2,1)S(1)}, s16[64,2176]{1,0:T(8,128)(2,1)S...) custom-call(s16[128,2176]{1,0:T(8,128)(2,1)S(1)} %collective-permute-done.19.refs_0_.refs_1_, ...), custom_call_target="tpu_custom_call" | custom-call | bytes 9900000 | tf_op jit(solution)/shard_map/middle_sums/pallas_call | solution.py:358
  142.4 2.9 %collective-permute-start.23 = (s16[64,2176]{1,0:T(8,128)(2,1)S(1)}, s16[64,2176]{1,0:T(8,128)(2,1)S(1)}, u32[]{:S(2)}, u32[]{:S(2)}) collective-permute-start(s16[64,2176]{1,0:T(8,128)(2,1)S(1)} %get-tuple-element.44), channel_id=1, source_target_pairs={{0,64},{1,65},{2,66},{3,67},{4,68},{5,69},{6,70},{7,71},{8,72},{9,... | collective-permute-start | bytes 835592 | tf_op jit(solution)/shard_map/ppermute | solution.py:59
  145.3 2.0 %collective-permute-start.25 = (s16[64,2176]{1,0:T(8,128)(2,1)S(1)}, s16[64,2176]{1,0:T(8,128)(2,1)S(1)}, u32[]{:S(2)}, u32[]{:S(2)}) collective-permute-start(s16[64,2176]{1,0:T(8,128)(2,1)S(1)} %get-tuple-element.46), channel_id=1, source_target_pairs={{0,48},{1,49},{2,50},{3,51},{4,52},{5,53},{6,54},{7,55},{8,56},{9,... | collective-permute-start | bytes 835592 | tf_op jit(solution)/shard_map/ppermute | solution.py:59
  147.3 0.6 collective-permute-start.26
  148.0 0.6 collective-permute-start.28
  148.6 6.1 %place.1 = (f32[96,4096]{1,0:T(8,128)S(1)}, f32[96,4096]{1,0:T(8,128)S(1)}, f32[96,4096]{1,0:T(8,128)S(1)}) custom-call(s32[18]{0:T(128)S(1)} %stack.75.order_ref, s32[1,9]{1,0:T(1,128)S(1)} %copy-done.9, s32[1,9]{1,0:T(1,128)S(1)} %copy-done.10, f32[1,96,4096]{2,1,0:T(8,128)S(1)} %copy-done.4, f32[1,96,4096]{2,1,0:T(8,128)S(1)} %copy-done.5, ...), custom_call_target="tpu_custom_call" | custom-call | bytes 19800000 | tf_op jit(solution)/shard_map/place/pallas_call | solution.py:443
  154.7 8.0 %grads.1 = (bf16[2048,512]{1,0:T(8,128)(2,1)}, bf16[2048,512]{1,0:T(8,128)(2,1)}) custom-call(s32[18]{0:T(128)S(1)} %stack.75.order_ref, f32[2048,512]{1,0:T(8,128)S(1)} %get-tuple-element.43.back_ref, bf16[2048,512]{1,0:T(8,128)(2,1)S(1)} %copy-done.1, bf16[2048,512]{1,0:T(8,128)(2,1)S(1)} %copy-done.2, f32[16,1,128]{2,1,0:T(1,128)S(1)} %add_rsqrt_fusion.inverse_ref, ...), custom_call_target="tpu_custom_call" | custom-call | bytes 26400000 | tf_op jit(solution)/shard_map/grads/pallas_call | solution.py:573
  162.7 0.0 copy-start.7
  162.8 1.6 copy-done.7
  164.3 0.9 last_sums.1
  165.3 3.5 %collective-permute-start.30 = (f32[16,4096]{1,0:T(8,128)S(1)}, f32[16,4096]{1,0:T(8,128)S(1)}, u32[]{:S(2)}, u32[]{:S(2)}) collective-permute-start(f32[16,4096]{1,0:T(8,128)S(1)} %get-tuple-element.53), channel_id=1, source_target_pairs={{0,16},{1,17},{2,18},{3,19},{4,20},{5,21},{6,22},{7,23},{8,24},{9,... | collective-permute-start | bytes 786440 | tf_op jit(solution)/shard_map/ppermute | solution.py:59
  168.8 2.4 %collective-permute-start.31 = (f32[16,4096]{1,0:T(8,128)S(1)}, f32[16,4096]{1,0:T(8,128)S(1)}, u32[]{:S(2)}, u32[]{:S(2)}) collective-permute-start(f32[16,4096]{1,0:T(8,128)S(1)} %get-tuple-element.54), channel_id=1, source_target_pairs={{16,0},{17,1},{18,2},{19,3},{20,4},{21,5},{22,6},{23,7},{24,8},{25... | collective-permute-start | bytes 786440 | tf_op jit(solution)/shard_map/ppermute | solution.py:59
  171.2 2.4 %collective-permute-done.30.up_ref = f32[16,4096]{1,0:T(8,128)S(1)} collective-permute-done((f32[16,4096]{1,0:T(8,128)S(1)}, f32[16,4096]{1,0:T(8,128)S(1)}, u32[]{:S(2)}, u32[]{:S(2)}) %collective-permute-start.30) | collective-permute-done | bytes 262176 | tf_op jit(solution)/shard_map/ppermute | solution.py:59
  173.6 5.6 %collective-permute-done.31.down_ref = f32[16,4096]{1,0:T(8,128)S(1)} collective-permute-done((f32[16,4096]{1,0:T(8,128)S(1)}, f32[16,4096]{1,0:T(8,128)S(1)}, u32[]{:S(2)}, u32[]{:S(2)}) %collective-permute-start.31) | collective-permute-done | bytes 262176 | tf_op jit(solution)/shard_map/ppermute | solution.py:59
  179.2 4.2 %adam.1 = (f32[1,96,4096]{2,1,0:T(8,128)}, f32[1,96,4096]{2,1,0:T(8,128)}, f32[1,96,4096]{2,1,0:T(8,128)}) custom-call(s32[18]{0:T(128)S(1)} %stack.75.order_ref, s32[1,9]{1,0:T(1,128)S(1)} %copy-done.9, s32[1,9]{1,0:T(1,128)S(1)} %copy-done.10, f32[64,4096]{1,0:T(8,128)S(1)} %get-tuple-element.52.grad_ref, f32[16,4096]{1,0:T(8,128)S(1)} %collective-permute-done.30.up_ref, ...), custom_call_target="tpu_custom_call" | custom-call | bytes 19800000 | tf_op jit(solution)/shard_map/adam/pallas_call | solution.py:454
  (52 shorter events, 0.3 us)
Async XLA Ops:
  0.6 26.5 %collective-permute-start.1 = (bf16[128,4096]{1,0:T(8,128)(2,1)}, bf16[128,4096]{1,0:T(8,128)(2,1)S(1)}, u32[]{:S(2)}, u32[]{:S(2)}) collective-permute-start(bf16[128,4096]{1,0:T(8,128)(2,1)} %refs_0_.2), channel_id=1, source_target_pairs={{0,4},{1,5},{2,6},{3,7},{4,8},{5,9},{6,10},{7,11},{8,12},{9,13},{1... | collective-permute-start | bytes 3145736 | tf_op jit(solution)/shard_map/ppermute | solution.py:59
  6.6 5.5 %collective-permute-start = (f32[16,1,128]{2,1,0:T(1,128)}, f32[16,1,128]{2,1,0:T(1,128)S(1)}, u32[]{:S(2)}, u32[]{:S(2)}) collective-permute-start(f32[16,1,128]{2,1,0:T(1,128)} %squares.1), channel_id=1, source_target_pairs={{0,1},{1,0},{2,3},{3,2},{4,5},{5,4},{6,7},{7,6},{8,9},{9,8},{10,11... | collective-permute-start | bytes 24584 | tf_op jit(solution)/shard_map/ppermute | solution.py:59
  6.6 28.0 %collective-permute-start.3 = (bf16[128,4096]{1,0:T(8,128)(2,1)}, bf16[128,4096]{1,0:T(8,128)(2,1)}, u32[]{:S(2)}, u32[]{:S(2)}) collective-permute-start(bf16[128,4096]{1,0:T(8,128)(2,1)} %refs_0_.2), channel_id=1, source_target_pairs={{0,2},{1,3},{2,0},{3,1},{4,6},{5,7},{6,4},{7,5},{8,10},{9,11},{10,... | collective-permute-start | bytes 3145736 | tf_op jit(solution)/shard_map/ppermute | solution.py:59
  10.5 30.4 %collective-permute-start.10 = (bf16[128,4096]{1,0:T(8,128)(2,1)}, bf16[128,4096]{1,0:T(8,128)(2,1)}, u32[]{:S(2)}, u32[]{:S(2)}) collective-permute-start(bf16[128,4096]{1,0:T(8,128)(2,1)} %refs_0_.2), channel_id=1, source_target_pairs={{0,12},{1,13},{2,14},{3,15},{4,0},{5,1},{6,2},{7,3},{8,4},{9,5},{1... | collective-permute-start | bytes 3145736 | tf_op jit(solution)/shard_map/ppermute | solution.py:59
  12.2 28.8 %collective-permute-start.11 = (bf16[128,4096]{1,0:T(8,128)(2,1)}, bf16[128,4096]{1,0:T(8,128)(2,1)}, u32[]{:S(2)}, u32[]{:S(2)}) collective-permute-start(bf16[128,4096]{1,0:T(8,128)(2,1)} %refs_0_.2), channel_id=1, source_target_pairs={{0,1},{1,0},{2,3},{3,2},{4,5},{5,4},{6,7},{7,6},{8,9},{9,8},{10,11... | collective-permute-start | bytes 3145736 | tf_op jit(solution)/shard_map/ppermute | solution.py:59
  27.1 1.0 copy-start.11
  28.1 15.8 %copy-start.2 = (bf16[2048,512]{1,0:T(8,128)(2,1)S(1)}, bf16[2048,512]{1,0:T(8,128)(2,1)}, u32[]{:S(2)}) copy-start(bf16[2048,512]{1,0:T(8,128)(2,1)} %gate_ref.7) | copy-start | bytes 6291460
  29.5 13.1 %collective-permute-start.13 = (bf16[128,4096]{1,0:T(8,128)(2,1)S(1)}, bf16[128,4096]{1,0:T(8,128)(2,1)}, u32[]{:S(2)}, u32[]{:S(2)}) collective-permute-start(bf16[128,4096]{1,0:T(8,128)(2,1)S(1)} %broadcast_select_fusion.1.refs_2_), channel_id=1, source_target_pairs={{0,1},{1,0},{2,3},{3,2},{4,5},{5,4},{6,7},{7,6},{8,9},{9,8},{10,11... | collective-permute-start | bytes 3145736 | tf_op jit(solution)/shard_map/ppermute | solution.py:59
  29.9 14.0 %copy-start.1 = (bf16[2048,512]{1,0:T(8,128)(2,1)S(1)}, bf16[2048,512]{1,0:T(8,128)(2,1)}, u32[]{:S(2)}) copy-start(bf16[2048,512]{1,0:T(8,128)(2,1)} %mixer_ref.7) | copy-start | bytes 6291460
  29.9 14.0 %copy-start.8 = (f32[512]{0:T(512)S(1)}, f32[512]{0:T(512)}, u32[]{:S(2)}) copy-start(f32[512]{0:T(512)} %param.13) | copy-start | bytes 6148
  29.9 9.3 %collective-permute-start.9 = (f32[16,1,128]{2,1,0:T(1,128)S(1)}, f32[16,1,128]{2,1,0:T(1,128)S(1)}, u32[]{:S(2)}, u32[]{:S(2)}) collective-permute-start(f32[16,1,128]{2,1,0:T(1,128)S(1)} %add.253), channel_id=1, source_target_pairs={{0,2},{1,3},{2,0},{3,1},{4,6},{5,7},{6,4},{7,5},{8,10},{9,11},{10,... | collective-permute-start | bytes 24584 | tf_op jit(solution)/shard_map/ppermute | solution.py:59
  34.6 28.3 %collective-permute-start.5 = (bf16[128,4096]{1,0:T(8,128)(2,1)S(1)}, bf16[128,4096]{1,0:T(8,128)(2,1)S(1)}, u32[]{:S(2)}, u32[]{:S(2)}) collective-permute-start(bf16[128,4096]{1,0:T(8,128)(2,1)S(1)} %broadcast_select_fusion.1.refs_2_), channel_id=1, source_target_pairs={{0,2},{1,3},{2,0},{3,1},{4,6},{5,7},{6,4},{7,5},{8,10},{9,11},{10,... | collective-permute-start | bytes 3145736 | tf_op jit(solution)/shard_map/ppermute | solution.py:59
  39.2 25.8 %collective-permute-start.2 = (bf16[128,4096]{1,0:T(8,128)(2,1)S(1)}, bf16[128,4096]{1,0:T(8,128)(2,1)S(1)}, u32[]{:S(2)}, u32[]{:S(2)}) collective-permute-start(bf16[128,4096]{1,0:T(8,128)(2,1)S(1)} %broadcast_select_fusion.1.refs_2_), channel_id=1, source_target_pairs={{0,4},{1,5},{2,6},{3,7},{4,8},{5,9},{6,10},{7,11},{8,12},{9,13},{1... | collective-permute-start | bytes 3145736 | tf_op jit(solution)/shard_map/ppermute | solution.py:59
  40.9 7.8 %collective-permute-start.12 = (bf16[128,4096]{1,0:T(8,128)(2,1)S(1)}, bf16[128,4096]{1,0:T(8,128)(2,1)S(1)}, u32[]{:S(2)}, u32[]{:S(2)}) collective-permute-start(bf16[128,4096]{1,0:T(8,128)(2,1)S(1)} %broadcast_select_fusion.refs_1_), channel_id=1, source_target_pairs={{0,1},{1,0},{2,3},{3,2},{4,5},{5,4},{6,7},{7,6},{8,9},{9,8},{10,11... | collective-permute-start | bytes 3145736 | tf_op jit(solution)/shard_map/ppermute | solution.py:59
  40.9 25.6 %collective-permute-start.4 = (bf16[128,4096]{1,0:T(8,128)(2,1)S(1)}, bf16[128,4096]{1,0:T(8,128)(2,1)S(1)}, u32[]{:S(2)}, u32[]{:S(2)}) collective-permute-start(bf16[128,4096]{1,0:T(8,128)(2,1)S(1)} %broadcast_select_fusion.refs_1_), channel_id=1, source_target_pairs={{0,12},{1,13},{2,14},{3,15},{4,0},{5,1},{6,2},{7,3},{8,4},{9,5},{1... | collective-permute-start | bytes 3145736 | tf_op jit(solution)/shard_map/ppermute | solution.py:59
  42.6 6.2 %collective-permute-start.14 = (bf16[128,4096]{1,0:T(8,128)(2,1)}, bf16[128,4096]{1,0:T(8,128)(2,1)S(1)}, u32[]{:S(2)}, u32[]{:S(2)}) collective-permute-start(bf16[128,4096]{1,0:T(8,128)(2,1)} %collective-permute-done.10.refs_3_), channel_id=1, source_target_pairs={{0,1},{1,0},{2,3},{3,2},{4,5},{5,4},{6,7},{7,6},{8,9},{9,8},{10,11... | collective-permute-start | bytes 3145736 | tf_op jit(solution)/shard_map/ppermute | solution.py:59
  43.9 4.9 %copy-start = (bf16[512,4096]{1,0:T(8,128)(2,1)S(1)}, bf16[512,4096]{1,0:T(8,128)(2,1)}, u32[]{:S(2)}) copy-start(bf16[512,4096]{1,0:T(8,128)(2,1)} %refs_5_.1) | copy-start | bytes 12582916
  61.7 7.9 %copy-start.3 = (f32[512,4096]{1,0:T(8,128)}, f32[512,4096]{1,0:T(8,128)S(1)}, u32[]{:S(2)}) copy-start(f32[512,4096]{1,0:T(8,128)S(1)} %get-tuple-element.33.refs_8_) | copy-start | bytes 25165828
  62.9 6.6 %collective-permute-start.8 = (bf16[128,4096]{1,0:T(8,128)(2,1)S(1)}, bf16[128,4096]{1,0:T(8,128)(2,1)S(1)}, u32[]{:S(2)}, u32[]{:S(2)}) collective-permute-start(bf16[128,4096]{1,0:T(8,128)(2,1)S(1)} %collective-permute-done.5.refs_2_), channel_id=1, source_target_pairs={{0,1},{1,0},{2,3},{3,2},{4,5},{5,4},{6,7},{7,6},{8,9},{9,8},{10,11... | collective-permute-start | bytes 3145736 | tf_op jit(solution)/shard_map/ppermute | solution.py:59
  65.0 4.6 %collective-permute-start.6 = (bf16[128,4096]{1,0:T(8,128)(2,1)S(1)}, bf16[128,4096]{1,0:T(8,128)(2,1)S(1)}, u32[]{:S(2)}, u32[]{:S(2)}) collective-permute-start(bf16[128,4096]{1,0:T(8,128)(2,1)S(1)} %collective-permute-done.2.refs_0_), channel_id=1, source_target_pairs={{0,1},{1,0},{2,3},{3,2},{4,5},{5,4},{6,7},{7,6},{8,9},{9,8},{10,11... | collective-permute-start | bytes 3145736 | tf_op jit(solution)/shard_map/ppermute | solution.py:59
  66.5 3.0 %collective-permute-start.7 = (bf16[128,4096]{1,0:T(8,128)(2,1)S(1)}, bf16[128,4096]{1,0:T(8,128)(2,1)S(1)}, u32[]{:S(2)}, u32[]{:S(2)}) collective-permute-start(bf16[128,4096]{1,0:T(8,128)(2,1)S(1)} %collective-permute-done.4.refs_1_), channel_id=1, source_target_pairs={{0,1},{1,0},{2,3},{3,2},{4,5},{5,4},{6,7},{7,6},{8,9},{9,8},{10,11... | collective-permute-start | bytes 3145736 | tf_op jit(solution)/shard_map/ppermute | solution.py:59
  66.6 15.3 %collective-permute-start.16 = (bf16[64,4096]{1,0:T(8,128)(2,1)S(1)}, bf16[64,4096]{1,0:T(8,128)(2,1)S(1)}, u32[]{:S(2)}, u32[]{:S(2)}) collective-permute-start(bf16[64,4096]{1,0:T(8,128)(2,1)S(1)} %slice_select_fusion), channel_id=1, source_target_pairs={{0,12},{1,13},{2,14},{3,15},{4,0},{5,1},{6,2},{7,3},{8,4},{9,5},{1... | collective-permute-start | bytes 1572872 | tf_op jit(solution)/shard_map/ppermute | solution.py:59
  69.5 15.3 %collective-permute-start.15 = (bf16[64,4096]{1,0:T(8,128)(2,1)S(1)}, bf16[64,4096]{1,0:T(8,128)(2,1)S(1)}, u32[]{:S(2)}, u32[]{:S(2)}) collective-permute-start(bf16[64,4096]{1,0:T(8,128)(2,1)S(1)} %slice_select_fusion.1), channel_id=1, source_target_pairs={{0,4},{1,5},{2,6},{3,7},{4,8},{5,9},{6,10},{7,11},{8,12},{9,13},{1... | collective-permute-start | bytes 1572872 | tf_op jit(solution)/shard_map/ppermute | solution.py:59
  80.7 4.4 %copy-start.4 = (f32[1,96,4096]{2,1,0:T(8,128)S(1)}, f32[1,96,4096]{2,1,0:T(8,128)}, u32[]{:S(2)}) copy-start(f32[1,96,4096]{2,1,0:T(8,128)} %refs_0_.3) | copy-start | bytes 4718596
  82.0 3.2 %collective-permute-start.18 = (bf16[64,4096]{1,0:T(8,128)(2,1)S(1)}, bf16[64,4096]{1,0:T(8,128)(2,1)S(1)}, u32[]{:S(2)}, u32[]{:S(2)}) collective-permute-start(bf16[64,4096]{1,0:T(8,128)(2,1)S(1)} %broadcast_select_fusion.2.refs_1_), channel_id=1, source_target_pairs={{0,1},{1,0},{2,3},{3,2},{4,5},{5,4},{6,7},{7,6},{8,9},{9,8},{10,11... | collective-permute-start | bytes 1572872 | tf_op jit(solution)/shard_map/ppermute | solution.py:59
  84.8 2.2 %collective-permute-start.17 = (bf16[64,4096]{1,0:T(8,128)(2,1)S(1)}, bf16[64,4096]{1,0:T(8,128)(2,1)S(1)}, u32[]{:S(2)}, u32[]{:S(2)}) collective-permute-start(bf16[64,4096]{1,0:T(8,128)(2,1)S(1)} %broadcast_select_fusion.3.refs_0_), channel_id=1, source_target_pairs={{0,1},{1,0},{2,3},{3,2},{4,5},{5,4},{6,7},{7,6},{8,9},{9,8},{10,11... | collective-permute-start | bytes 1572872 | tf_op jit(solution)/shard_map/ppermute | solution.py:59
  94.1 46.1 %collective-permute-start.22 = (s16[256,2176]{1,0:T(8,128)(2,1)S(1)}, s16[256,2176]{1,0:T(8,128)(2,1)S(1)}, u32[]{:S(2)}, u32[]{:S(2)}) collective-permute-start(s16[256,2176]{1,0:T(8,128)(2,1)S(1)} %get-tuple-element.40), channel_id=1, source_target_pairs={{0,64},{1,65},{2,66},{3,67},{4,68},{5,69},{6,70},{7,71},{8,72},{9,... | collective-permute-start | bytes 3342344 | tf_op jit(solution)/shard_map/ppermute | solution.py:59
  95.2 52.7 %collective-permute-start.29 = (f32[48,4096]{1,0:T(8,128)S(1)}, f32[48,4096]{1,0:T(8,128)S(1)}, u32[]{:S(2)}, u32[]{:S(2)}) collective-permute-start(f32[48,4096]{1,0:T(8,128)S(1)} %pad_maximum_fusion), channel_id=1, source_target_pairs={{16,0},{17,1},{18,2},{19,3},{20,4},{21,5},{22,6},{23,7},{24,8},{25... | collective-permute-start | bytes 2359304 | tf_op jit(solution)/shard_map/ppermute | solution.py:59
  98.0 15.6 %collective-permute-start.19 = (s16[128,2176]{1,0:T(8,128)(2,1)S(1)}, s16[128,2176]{1,0:T(8,128)(2,1)S(1)}, u32[]{:S(2)}, u32[]{:S(2)}) collective-permute-start(s16[128,2176]{1,0:T(8,128)(2,1)S(1)} %get-tuple-element.37), channel_id=1, source_target_pairs={{0,16},{1,17},{2,18},{3,19},{4,20},{5,21},{6,22},{7,23},{8,24},{9,... | collective-permute-start | bytes 1671176 | tf_op jit(solution)/shard_map/ppermute | solution.py:59
  98.0 29.8 %collective-permute-start.20 = (s16[128,2176]{1,0:T(8,128)(2,1)S(1)}, s16[128,2176]{1,0:T(8,128)(2,1)S(1)}, u32[]{:S(2)}, u32[]{:S(2)}) collective-permute-start(s16[128,2176]{1,0:T(8,128)(2,1)S(1)} %get-tuple-element.38), channel_id=1, source_target_pairs={{0,48},{1,49},{2,50},{3,51},{4,52},{5,53},{6,54},{7,55},{8,56},{9,... | collective-permute-start | bytes 1671176 | tf_op jit(solution)/shard_map/ppermute | solution.py:59
  100.1 40.1 %collective-permute-start.21 = (s16[128,2176]{1,0:T(8,128)(2,1)S(1)}, s16[128,2176]{1,0:T(8,128)(2,1)S(1)}, u32[]{:S(2)}, u32[]{:S(2)}) collective-permute-start(s16[128,2176]{1,0:T(8,128)(2,1)S(1)} %get-tuple-element.39), channel_id=1, source_target_pairs={{0,32},{1,33},{2,34},{3,35},{4,36},{5,37},{6,38},{7,39},{8,40},{9,... | collective-permute-start | bytes 1671176 | tf_op jit(solution)/shard_map/ppermute | solution.py:59
  113.6 33.7 %collective-permute-start.27 = (f32[16,1,128]{2,1,0:T(1,128)S(1)}, f32[16,1,128]{2,1,0:T(1,128)S(1)}, u32[]{:S(2)}, u32[]{:S(2)}) collective-permute-start(f32[16,1,128]{2,1,0:T(1,128)S(1)} %centre.1.refs_10_), channel_id=1, source_target_pairs={{0,1},{1,0},{2,3},{3,2},{4,5},{5,4},{6,7},{7,6},{8,9},{9,8},{10,11... | collective-permute-start | bytes 24584 | tf_op jit(solution)/shard_map/ppermute | solution.py:59
  140.2 8.4 %copy-start.5 = (f32[1,96,4096]{2,1,0:T(8,128)S(1)}, f32[1,96,4096]{2,1,0:T(8,128)}, u32[]{:S(2)}) copy-start(f32[1,96,4096]{2,1,0:T(8,128)} %refs_1_.1) | copy-start | bytes 4718596
  140.2 8.4 %copy-start.6 = (f32[1,96,4096]{2,1,0:T(8,128)S(1)}, f32[1,96,4096]{2,1,0:T(8,128)}, u32[]{:S(2)}) copy-start(f32[1,96,4096]{2,1,0:T(8,128)} %refs_2_.1) | copy-start | bytes 4718596
  140.2 8.4 %copy-start.9 = (s32[1,9]{1,0:T(1,128)S(1)}, s32[1,9]{1,0:T(1,128)}, u32[]{:S(2)}) copy-start(s32[1,9]{1,0:T(1,128)} %old_ref.3) | copy-start | bytes 112
  140.2 8.4 %copy-start.10 = (s32[1,9]{1,0:T(1,128)S(1)}, s32[1,9]{1,0:T(1,128)}, u32[]{:S(2)}) copy-start(s32[1,9]{1,0:T(1,128)} %new_ref.3) | copy-start | bytes 112
  142.4 20.3 %collective-permute-start.23 = (s16[64,2176]{1,0:T(8,128)(2,1)S(1)}, s16[64,2176]{1,0:T(8,128)(2,1)S(1)}, u32[]{:S(2)}, u32[]{:S(2)}) collective-permute-start(s16[64,2176]{1,0:T(8,128)(2,1)S(1)} %get-tuple-element.44), channel_id=1, source_target_pairs={{0,64},{1,65},{2,66},{3,67},{4,68},{5,69},{6,70},{7,71},{8,72},{9,... | collective-permute-start | bytes 835592 | tf_op jit(solution)/shard_map/ppermute | solution.py:59
  145.3 17.4 %collective-permute-start.24 = (s16[64,2176]{1,0:T(8,128)(2,1)S(1)}, s16[64,2176]{1,0:T(8,128)(2,1)S(1)}, u32[]{:S(2)}, u32[]{:S(2)}) collective-permute-start(s16[64,2176]{1,0:T(8,128)(2,1)S(1)} %get-tuple-element.45), channel_id=1, source_target_pairs={{0,16},{1,17},{2,18},{3,19},{4,20},{5,21},{6,22},{7,23},{8,24},{9,... | collective-permute-start | bytes 835592 | tf_op jit(solution)/shard_map/ppermute | solution.py:59
  145.3 17.4 %collective-permute-start.25 = (s16[64,2176]{1,0:T(8,128)(2,1)S(1)}, s16[64,2176]{1,0:T(8,128)(2,1)S(1)}, u32[]{:S(2)}, u32[]{:S(2)}) collective-permute-start(s16[64,2176]{1,0:T(8,128)(2,1)S(1)} %get-tuple-element.46), channel_id=1, source_target_pairs={{0,48},{1,49},{2,50},{3,51},{4,52},{5,53},{6,54},{7,55},{8,56},{9,... | collective-permute-start | bytes 835592 | tf_op jit(solution)/shard_map/ppermute | solution.py:59
  147.3 15.4 %collective-permute-start.26 = (s16[64,2176]{1,0:T(8,128)(2,1)S(1)}, s16[64,2176]{1,0:T(8,128)(2,1)S(1)}, u32[]{:S(2)}, u32[]{:S(2)}) collective-permute-start(s16[64,2176]{1,0:T(8,128)(2,1)S(1)} %get-tuple-element.47), channel_id=1, source_target_pairs={{0,32},{1,33},{2,34},{3,35},{4,36},{5,37},{6,38},{7,39},{8,40},{9,... | collective-permute-start | bytes 835592 | tf_op jit(solution)/shard_map/ppermute | solution.py:59
  148.0 6.8 %collective-permute-start.28 = (f32[16,1,128]{2,1,0:T(1,128)S(1)}, f32[16,1,128]{2,1,0:T(1,128)S(1)}, u32[]{:S(2)}, u32[]{:S(2)}) collective-permute-start(f32[16,1,128]{2,1,0:T(1,128)S(1)} %add.257), channel_id=1, source_target_pairs={{0,2},{1,3},{2,0},{3,1},{4,6},{5,7},{6,4},{7,5},{8,10},{9,11},{10,... | collective-permute-start | bytes 24584 | tf_op jit(solution)/shard_map/ppermute | solution.py:59
  162.7 1.6 copy-start.7
  165.3 8.3 %collective-permute-start.30 = (f32[16,4096]{1,0:T(8,128)S(1)}, f32[16,4096]{1,0:T(8,128)S(1)}, u32[]{:S(2)}, u32[]{:S(2)}) collective-permute-start(f32[16,4096]{1,0:T(8,128)S(1)} %get-tuple-element.53), channel_id=1, source_target_pairs={{0,16},{1,17},{2,18},{3,19},{4,20},{5,21},{6,22},{7,23},{8,24},{9,... | collective-permute-start | bytes 786440 | tf_op jit(solution)/shard_map/ppermute | solution.py:59
  168.8 10.4 %collective-permute-start.31 = (f32[16,4096]{1,0:T(8,128)S(1)}, f32[16,4096]{1,0:T(8,128)S(1)}, u32[]{:S(2)}, u32[]{:S(2)}) collective-permute-start(f32[16,4096]{1,0:T(8,128)S(1)} %get-tuple-element.54), channel_id=1, source_target_pairs={{16,0},{17,1},{18,2},{19,3},{20,4},{21,5},{22,6},{23,7},{24,8},{25... | collective-permute-start | bytes 786440 | tf_op jit(solution)/shard_map/ppermute | solution.py:59

commit v3 on v2

--- a/solution.py
+++ b/solution.py
@@ -310,7 +310,7 @@
     )(*pieces, hidden, weight, *(before or []))
 
 
-def late_products(pieces, hidden, weight, start, before):
+def late_products(pieces, hidden, weight, start, before, arrived):
     tokens = sum(p.shape[0] for p in pieces)
     channels, width = weight.shape
     steps, count = width // TILE, len(pieces)
@@ -319,9 +319,9 @@
     full = lambda rows: jax.ShapeDtypeStruct((rows, HALF), F32)
     back = jax.ShapeDtypeStruct(before[1].shape, F32)
     return pl.pallas_call(
-        lambda *refs: late_kernel(count, start, steps, *refs),
+        lambda *refs: late_kernel(count, start, steps, *refs[: count + 4], *refs[count + 5 :]),
         grid=(steps,),
-        in_specs=[ANYWHERE] * (count + 1) + [wide(channels), wide(channels), ANYWHERE],
+        in_specs=[ANYWHERE] * (count + 1) + [wide(channels), wide(channels), ANYWHERE, ANYWHERE],
         out_specs=[kept(128, HALF + 128)] * 3
         + [
             kept(256, HALF + 128),
@@ -341,7 +341,7 @@
         compiler_params=params(GRANT),
         cost_estimate=cost(9),
         name="late_products",
-    )(*pieces, hidden, weight, *before)
+    )(*pieces, hidden, weight, *before, arrived)
 
 
 def coded(rows):
@@ -503,8 +503,9 @@
         cost_estimate=cost(3),
         name="squares",
     )(mixer_out, gate)
-    squares = chip_total(squares)
-    inverse = lax.rsqrt(group_total(squares) / GROUP + norm_eps)
+    raw = squares
+    squares = group_total(squares)
+    inverse = lax.rsqrt(chip_total(squares) / GROUP + norm_eps)
 
     gain = norm_gain[None, :]
     there = pl.BlockSpec((BLOCK, channels), lambda i, o: (o[i], 0))
@@ -535,13 +536,12 @@
     )(order, mixer_out, gate, inverse, gain)
 
     states = (old_master, old_first, old_second)
-    arrived = move(jnp.concatenate([s[0, :HALO] for s in states], axis=0), TO_LAST)
 
     own = cotangent
     own_z = move(own, TO_ZHI)
     own_m, own_p = move(own, TO_YP), move(own, TO_YM)
     own_s = move(own, TO_CORE)
-    own_z, own_m = tied(own_z, squares), tied(own_m, squares)
+    own_p = tied(own_p, raw)
     far = move(own_m, TO_YP)
     other_p, other_m = move(own_z, TO_YM), move(own_m, TO_ZHI)
     early = [own, own_z, own_m, own_p, own_s, move(own_z, TO_CORE), move(own_m, TO_CORE), move(own_p, TO_CORE)]
@@ -549,6 +549,7 @@
     sums = products(early, hidden, out_weight, at)
     at += 8 * BLOCK
     half = BLOCK // 2
+    arrived = move(tied(jnp.concatenate([s[0, :HALO] for s in states], axis=0), sums[0]), TO_LAST)
     last_a = move(tied(other_m[:half], sums[0]), TO_YP)
     last_b = move(tied(other_p[half:], sums[0]), TO_YM)
     middle = [far, other_p, other_m, move(far, TO_CORE), move(other_p, TO_CORE), move(other_m, TO_CORE)]
@@ -556,7 +557,7 @@
     at += 6 * BLOCK
     last_a, last_b = tied(last_a, sums[0]), tied(last_b, sums[0])
     last = [last_a, last_b, move(last_a, TO_CORE), move(last_b, TO_CORE)]
-    *to_x, to_z, mine_a, mine_b, back = late_products(last, hidden, out_weight, at, sums)
+    *to_x, to_z, mine_a, mine_b, back = late_products(last, hidden, out_weight, at, sums, arrived)
     got_x, got_z = [move(code, pairs) for code, pairs in zip(to_x, TO_X)], move(to_z, TO_ZLO)
 
     centre = ordered(
@@ -567,8 +568,10 @@
         "centre",
         4,
     )(order, back, mixer_out, gate, inverse, gain)
-    send_a, *send_b, keep_a, keep_b = middle_sums(got_x, got_z, mine_a, mine_b, [centre])
+    scalars = (order, old_bounds, new_bounds)
+    placed = place(scalars, states, arrived)
     centre = group_total(chip_total(centre)) / GROUP
+    send_a, *send_b, keep_a, keep_b = middle_sums(got_x, got_z, mine_a, mine_b, [centre, placed[0]])
     out_shape = jax.ShapeDtypeStruct((tokens, channels), BF16)
     input_grad, gate_grad = ordered(
         grads_kernel,
@@ -579,10 +582,8 @@
         8,
     )(order, back, mixer_out, gate, inverse, centre, gain)
 
-    scalars = (order, old_bounds, new_bounds)
-    placed = place(scalars, states, arrived)
     got_a, got_b = move(send_a, TO_ZLO), [move(code, pairs) for code, pairs in zip(send_b, TO_X)]
-    grad, last_rows, first_rows = last_sums(got_a, got_b, keep_a, keep_b, [input_grad, placed[0]])
+    grad, last_rows, first_rows = last_sums(got_a, got_b, keep_a, keep_b, [input_grad])
     made = adam(scalars, grad, move(last_rows, TO_NEXT), move(first_rows, TO_LAST), placed)
     return (*made, input_grad, gate_grad)
 

time: 184 us -> 166 us (0.902)
  waiting for transfers between devices: 64.7 us -> 46.4 us
  local copies, waits for them, and re-layouts: 5.37 us -> 9.26 us
  starting transfers between devices: 41 us -> 38.9 us
  other arithmetic: 3.71 us -> 1.72 us
    ppermute x32, waiting for transfers between devices: 64.7 us -> 46.4 us  [move(): return lax.ppermute(value, AXES, pairs)]
    ppermute x32, starting transfers between devices: 41 us -> 38.9 us  [move(): return lax.ppermute(value, AXES, pairs)]
    unnamed x24 -> x34, local copies, waits for them, and re-layouts: 2.61 us -> 4.21 us
  transfers between devices with their start and end apart: 32 -> 32, of which waited for: 11 -> 12; matrix products, arithmetic and copies ran while one was open for 4% -> 4% of each run, Pallas kernels for 29% -> 31%
where the time goes in v3:
time: 166 us; the launch traced here: 165 us
  Pallas kernels  65.8 us (40%)
  waiting for transfers between devices  46.4 us (28%)
  starting transfers between devices  38.9 us (23%)
  local copies, waits for them, and re-layouts  9.26 us (6%)
  between operations  3.16 us (2%)
  other arithmetic  1.72 us (1%)
    ppermute x32, waiting for transfers between devices, move(): return lax.ppermute(value, AXES, pairs)  46.4 us
    ppermute x32, starting transfers between devices, move(): return lax.ppermute(value, AXES, pairs)  38.9 us
    pallas_call x2, Pallas kernels, products(): pl.pallas_call(lambda *refs: kernel(count, start, steps, *refs), grid=(st...  24.5 us
    pallas_call x1, Pallas kernels, local(): ordered(grads_kernel, [here, there, there, there_row, there_row, gain_spe...  8.01 us
    pallas_call x1, Pallas kernels, late_products(): pl.pallas_call(lambda *refs: late_kernel(count, start, steps, *refs[:coun...  7.11 us
    pallas_call x1, Pallas kernels, place(): share_call(place_kernel, tile, [state] * 3 + [part(3 * HALO)], [part(CAP)...  6.09 us
    pallas_call x1, Pallas kernels, local(): ordered(hidden_kernel, [there, there, there_row, gain_spec], pl.BlockSpec...  4.86 us
    pallas_call x1, Pallas kernels, local(): pl.pallas_call(square_kernel, grid=(blocks // 4,), in_specs=[block_spec,...  4.34 us
  transfers between devices with their start and end apart: 32, of which 12 were waited for; matrix products, arithmetic and copies ran while one was open for 4% of the time, Pallas kernels for 31%

profile of v3, /device:TPU:6, one launch (start us, length us, event | category | flops | bytes accessed | tf_op | source)
XLA Modules:
  0.0 165.2 jit_solution(11342395694143771489)
XLA Ops:
  0.6 3.1 %collective-permute-start.10 = (bf16[128,4096]{1,0:T(8,128)(2,1)}, bf16[128,4096]{1,0:T(8,128)(2,1)S(1)}, u32[]{:S(2)}, u32[]{:S(2)}) collective-permute-start(bf16[128,4096]{1,0:T(8,128)(2,1)} %refs_0_.2), channel_id=1, source_target_pairs={{0,12},{1,13},{2,14},{3,15},{4,0},{5,1},{6,2},{7,3},{8,4},{9,5},{1... | collective-permute-start | bytes 3145736 | tf_op jit(solution)/shard_map/ppermute | solution.py:59
  3.7 3.9 %collective-permute-start.2 = (bf16[128,4096]{1,0:T(8,128)(2,1)}, bf16[128,4096]{1,0:T(8,128)(2,1)}, u32[]{:S(2)}, u32[]{:S(2)}) collective-permute-start(bf16[128,4096]{1,0:T(8,128)(2,1)} %refs_0_.2), channel_id=1, source_target_pairs={{0,2},{1,3},{2,0},{3,1},{4,6},{5,7},{6,4},{7,5},{8,10},{9,11},{10,... | collective-permute-start | bytes 3145736 | tf_op jit(solution)/shard_map/ppermute | solution.py:59
  7.6 4.3 %squares.1 = f32[16,1,128]{2,1,0:T(1,128)} custom-call(bf16[2048,512]{1,0:T(8,128)(2,1)} %mixer_ref.7, bf16[2048,512]{1,0:T(8,128)(2,1)} %gate_ref.7), custom_call_target="tpu_custom_call" | custom-call | bytes 9900000 | tf_op jit(solution)/shard_map/squares/pallas_call | solution.py:496
  11.9 0.0 collective-permute-start.8
  12.0 1.2 slice.35
  13.8 12.6 %collective-permute-done.10 = bf16[128,4096]{1,0:T(8,128)(2,1)S(1)} collective-permute-done((bf16[128,4096]{1,0:T(8,128)(2,1)}, bf16[128,4096]{1,0:T(8,128)(2,1)S(1)}, u32[]{:S(2)}, u32[]{:S(2)}) %collective-permute-start.10) | collective-permute-done | bytes 1048608 | tf_op jit(solution)/shard_map/ppermute | solution.py:59
  26.4 1.0 copy-done.14
  27.4 1.4 broadcast_select_fusion.refs_3_
  28.9 0.1 collective-permute-start.14
  29.0 1.8 %slice_bitcast_fusion = (f32[16,4096]{1,0:T(8,128)S(1)}, f32[16,4096]{1,0:T(8,128)}) fusion(f32[1,96,4096]{2,1,0:T(8,128)} %refs_2_.1, f32[1,96,4096]{2,1,0:T(8,128)} %refs_1_.1), kind=kLoop, calls=%fused_computation.6 | loop fusion | bytes 1048576 | tf_op jit(solution)/shard_map/squeeze | solution.py:552
  30.7 0.2 collective-permute-done.8
  31.0 0.4 collective-permute-start.9
  31.3 0.1 stack.75.order_ref
  31.4 0.3 collective-permute-start.12
  31.7 0.5 collective-permute-done.9
  32.2 3.5 %collective-permute-start.3 = (bf16[128,4096]{1,0:T(8,128)(2,1)}, bf16[128,4096]{1,0:T(8,128)(2,1)S(1)}, u32[]{:S(2)}, u32[]{:S(2)}) collective-permute-start(bf16[128,4096]{1,0:T(8,128)(2,1)} %collective-permute-done.2.refs_1_), channel_id=1, source_target_pairs={{0,12},{1,13},{2,14},{3,15},{4,0},{5,1},{6,2},{7,3},{8,4},{9,5},{1... | collective-permute-start | bytes 3145736 | tf_op jit(solution)/shard_map/ppermute | solution.py:59
  35.7 0.1 collective-permute-start.13
  35.8 1.0 slice_bitcast_fusion.2
  36.8 4.0 %collective-permute-start.4 = (bf16[128,4096]{1,0:T(8,128)(2,1)}, bf16[128,4096]{1,0:T(8,128)(2,1)S(1)}, u32[]{:S(2)}, u32[]{:S(2)}) collective-permute-start(bf16[128,4096]{1,0:T(8,128)(2,1)} %collective-permute-done.refs_2_), channel_id=1, source_target_pairs={{0,2},{1,3},{2,0},{3,1},{4,6},{5,7},{6,4},{7,5},{8,10},{9,11},{10,... | collective-permute-start | bytes 3145736 | tf_op jit(solution)/shard_map/ppermute | solution.py:59
  40.8 0.0 copy-start.2
  40.8 1.6 copy-done.2
  42.4 4.9 %hidden.1.refs_8_.refs_6_.refs_4_ = bf16[512,2048]{1,0:T(8,128)(2,1)S(1)} custom-call(s32[18]{0:T(128)S(1)} %stack.75.order_ref, bf16[2048,512]{1,0:T(8,128)(2,1)S(1)} %copy-done.1, bf16[2048,512]{1,0:T(8,128)(2,1)S(1)} %copy-done.2, f32[16,1,128]{2,1,0:T(1,128)S(1)} %add_rsqrt_fusion.inverse_ref, f32[1,512]{1,0:T(1,128)S(1)} %bitcast.28), custom_call_target="tpu_custom_call" | custom-call | bytes 16500000 | tf_op jit(solution)/shard_map/hidden/pallas_call | solution.py:528
  47.3 0.0 copy-start.3
  47.3 13.3 %products.2 = (f32[512,4096]{1,0:T(8,128)S(1)}, f32[2048,512]{1,0:T(8,128)S(1)}) custom-call(bf16[128,4096]{1,0:T(8,128)(2,1)S(1)} %copy-done.10, bf16[128,4096]{1,0:T(8,128)(2,1)} %collective-permute-done.2.refs_1_, bf16[128,4096]{1,0:T(8,128)(2,1)} %collective-permute-done.refs_2_, bf16[128,4096]{1,0:T(8,128)(2,1)S(1)} %broadcast_select_fusion.refs_3_, ...), custom_call_target="tpu_custom_call" | custom-call | bytes 59400000 | tf_op jit(solution)/shard_map/products/pallas_call | solution.py:293
  60.6 0.0 copy-start.15
  60.6 0.5 slice.29
  61.9 3.3 %collective-permute-start.16 = (bf16[64,4096]{1,0:T(8,128)(2,1)S(1)}, bf16[64,4096]{1,0:T(8,128)(2,1)S(1)}, u32[]{:S(2)}, u32[]{:S(2)}) collective-permute-start(bf16[64,4096]{1,0:T(8,128)(2,1)S(1)} %slice_select_fusion), channel_id=1, source_target_pairs={{0,12},{1,13},{2,14},{3,15},{4,0},{5,1},{6,2},{7,3},{8,4},{9,5},{1... | collective-permute-start | bytes 1572872 | tf_op jit(solution)/shard_map/ppermute | solution.py:59
  65.2 0.5 collective-permute-start.7
  65.7 1.7 %collective-permute-done.1.refs_0_ = bf16[128,4096]{1,0:T(8,128)(2,1)S(1)} collective-permute-done((bf16[128,4096]{1,0:T(8,128)(2,1)}, bf16[128,4096]{1,0:T(8,128)(2,1)S(1)}, u32[]{:S(2)}, u32[]{:S(2)}) %collective-permute-start.1) | collective-permute-done | bytes 1048608 | tf_op jit(solution)/shard_map/ppermute | solution.py:59
  67.5 0.1 collective-permute-start.15
  67.5 0.1 maximum_select_fusion
  67.6 1.7 %collective-permute-done.7.refs_5_ = bf16[128,4096]{1,0:T(8,128)(2,1)S(1)} collective-permute-done((bf16[128,4096]{1,0:T(8,128)(2,1)S(1)}, bf16[128,4096]{1,0:T(8,128)(2,1)S(1)}, u32[]{:S(2)}, u32[]{:S(2)}) %collective-permute-start.7) | collective-permute-done | bytes 1048608 | tf_op jit(solution)/shard_map/ppermute | solution.py:59
  69.4 2.7 %collective-permute-start.19 = (f32[48,4096]{1,0:T(8,128)S(1)}, f32[48,4096]{1,0:T(8,128)S(1)}, u32[]{:S(2)}, u32[]{:S(2)}) collective-permute-start(f32[48,4096]{1,0:T(8,128)S(1)} %maximum_select_fusion), channel_id=1, source_target_pairs={{16,0},{17,1},{18,2},{19,3},{20,4},{21,5},{22,6},{23,7},{24,8},{25... | collective-permute-start | bytes 2359304 | tf_op jit(solution)/shard_map/ppermute | solution.py:59
  72.2 11.2 %products.3 = (f32[512,4096]{1,0:T(8,128)S(1)}, f32[2048,512]{1,0:T(8,128)S(1)}) custom-call(bf16[128,4096]{1,0:T(8,128)(2,1)S(1)} %collective-permute-done.1.refs_0_, bf16[128,4096]{1,0:T(8,128)(2,1)S(1)} %collective-permute-done.3.refs_1_, bf16[128,4096]{1,0:T(8,128)(2,1)S(1)} %collective-permute-done.4.refs_2_, ...), custom_call_target="tpu_custom_call", output_to_operand_aliasing={{1}: (9, {})} | custom-call | bytes 52800000 | tf_op jit(solution)/shard_map/products/pallas_call | solution.py:293
  83.3 0.5 slice.28
  84.7 0.1 collective-permute-start.18
  84.8 0.7 collective-permute-start.17
  85.6 7.4 %collective-permute-done.19.refs_8_.refs_3_ = f32[48,4096]{1,0:T(8,128)S(1)} collective-permute-done((f32[48,4096]{1,0:T(8,128)S(1)}, f32[48,4096]{1,0:T(8,128)S(1)}, u32[]{:S(2)}, u32[]{:S(2)}) %collective-permute-start.19) | collective-permute-done | bytes 786464 | tf_op jit(solution)/shard_map/ppermute | solution.py:59
  92.9 7.1 %late_products.1 = (s16[128,2176]{1,0:T(8,128)(2,1)S(1)}, s16[128,2176]{1,0:T(8,128)(2,1)S(1)}, s16[128,2176]{1,0:T(8,128)(2,1)S(1)}, s16[256,2176]{1,0:T(8,128)...) custom-call(bf16[64,4096]{1,0:T(8,128)(2,1)S(1)} %broadcast_select_f, ...), custom_call_target="tpu_custom_call", output_to_operand_aliasing={{6}: (7, {})} | custom-call | bytes 29700000 | tf_op jit(solution)/shard_map/late_products/pallas_call | solution.py:321
  100.1 0.1 collective-permute-start.23
  100.2 0.1 collective-permute-start.20
  100.2 2.0 %collective-permute-start.21 = (s16[128,2176]{1,0:T(8,128)(2,1)S(1)}, s16[128,2176]{1,0:T(8,128)(2,1)S(1)}, u32[]{:S(2)}, u32[]{:S(2)}) collective-permute-start(s16[128,2176]{1,0:T(8,128)(2,1)S(1)} %get-tuple-element.38), channel_id=1, source_target_pairs={{0,48},{1,49},{2,50},{3,51},{4,52},{5,53},{6,54},{7,55},{8,56},{9,... | collective-permute-start | bytes 1671176 | tf_op jit(solution)/shard_map/ppermute | solution.py:59
  102.2 0.2 collective-permute-start.22
  102.5 3.7 %centre.1 = f32[16,1,128]{2,1,0:T(1,128)S(1)} custom-call(s32[18]{0:T(128)S(1)} %stack.75.order_ref, f32[2048,512]{1,0:T(8,128)S(1)} %get-tuple-element.43.back_ref, bf16[2048,512]{1,0:T(8,128)(2,1)S(1)} %copy-done.1, bf16[2048,512]{1,0:T(8,128)(2,1)S(1)} %copy-done.2, f32[16,1,128]{2,1,0:T(1,128)S(1)} %add_rsqrt_fusion.inverse_ref, f32[1,512]{1,0:T(1,128)S(1)} %bitcast.29), custom_call_target="tpu_custom_call" | custom-call | bytes 13200000 | tf_op jit(solution)/shard_map/centre/pallas_call | solution.py:563
  106.2 0.1 collective-permute-start.24
  106.3 1.2 collective-permute-done.24
  107.5 2.1 %collective-permute-start.25 = (f32[16,1,128]{2,1,0:T(1,128)S(1)}, f32[16,1,128]{2,1,0:T(1,128)S(1)}, u32[]{:S(2)}, u32[]{:S(2)}) collective-permute-start(f32[16,1,128]{2,1,0:T(1,128)S(1)} %add.257), channel_id=1, source_target_pairs={{0,2},{1,3},{2,0},{3,1},{4,6},{5,7},{6,4},{7,5},{8,10},{9,11},{10,... | collective-permute-start | bytes 24584 | tf_op jit(solution)/shard_map/ppermute | solution.py:59
  109.5 6.1 %place.1 = (f32[96,4096]{1,0:T(8,128)S(1)}, f32[96,4096]{1,0:T(8,128)S(1)}, f32[96,4096]{1,0:T(8,128)S(1)}) custom-call(s32[18]{0:T(128)S(1)} %stack.75.order_ref, s32[1,9]{1,0:T(1,128)S(1)} %copy-done.12, s32[1,9]{1,0:T(1,128)S(1)} %copy-done.13, f32[1,96,4096]{2,1,0:T(8,128)S(1)} %copy-done.6, f32[1,96,4096]{2,1,0:T(8,128)S(1)} %copy-done.8, ...), custom_call_target="tpu_custom_call" | custom-call | bytes 19800000 | tf_op jit(solution)/shard_map/place/pallas_call | solution.py:443
  115.6 10.1 %collective-permute-done.25 = f32[16,1,128]{2,1,0:T(1,128)S(1)} collective-permute-done((f32[16,1,128]{2,1,0:T(1,128)S(1)}, f32[16,1,128]{2,1,0:T(1,128)S(1)}, u32[]{:S(2)}, u32[]{:S(2)}) %collective-permute-start.25) | collective-permute-done | bytes 8224 | tf_op jit(solution)/shard_map/ppermute | solution.py:59
  125.7 1.6 collective-permute-done.21.refs_2_.refs_3_
  127.3 2.1 %middle_sums.1 = (s16[64,2176]{1,0:T(8,128)(2,1)S(1)}, s16[64,2176]{1,0:T(8,128)(2,1)S(1)}, s16[64,2176]{1,0:T(8,128)(2,1)S(1)}, s16[64,2176]{1,0:T(8,128)(2,1)S...) custom-call(s16[128,2176]{1,0:T(8,128)(2,1)S(1)} %collective-permute-done.20.refs_0_.refs_1_, ...), custom_call_target="tpu_custom_call" | custom-call | bytes 9900000 | tf_op jit(solution)/shard_map/middle_sums/pallas_call | solution.py:358
  129.4 1.7 %collective-permute-start.26 = (s16[64,2176]{1,0:T(8,128)(2,1)S(1)}, s16[64,2176]{1,0:T(8,128)(2,1)S(1)}, u32[]{:S(2)}, u32[]{:S(2)}) collective-permute-start(s16[64,2176]{1,0:T(8,128)(2,1)S(1)} %get-tuple-element.45), channel_id=1, source_target_pairs={{0,64},{1,65},{2,66},{3,67},{4,68},{5,69},{6,70},{7,71},{8,72},{9,... | collective-permute-start | bytes 835592 | tf_op jit(solution)/shard_map/ppermute | solution.py:59
  131.1 1.5 collective-permute-start.27
  132.5 0.6 collective-permute-start.28
  133.1 2.0 %collective-permute-start.29 = (s16[64,2176]{1,0:T(8,128)(2,1)S(1)}, s16[64,2176]{1,0:T(8,128)(2,1)S(1)}, u32[]{:S(2)}, u32[]{:S(2)}) collective-permute-start(s16[64,2176]{1,0:T(8,128)(2,1)S(1)} %get-tuple-element.48), channel_id=1, source_target_pairs={{0,32},{1,33},{2,34},{3,35},{4,36},{5,37},{6,38},{7,39},{8,40},{9,... | collective-permute-start | bytes 835592 | tf_op jit(solution)/shard_map/ppermute | solution.py:59
  135.1 8.0 %grads.1 = (bf16[2048,512]{1,0:T(8,128)(2,1)}, bf16[2048,512]{1,0:T(8,128)(2,1)}) custom-call(s32[18]{0:T(128)S(1)} %stack.75.order_ref, f32[2048,512]{1,0:T(8,128)S(1)} %get-tuple-element.43.back_ref, bf16[2048,512]{1,0:T(8,128)(2,1)S(1)} %copy-done.1, bf16[2048,512]{1,0:T(8,128)(2,1)S(1)} %copy-done.2, f32[16,1,128]{2,1,0:T(1,128)S(1)} %add_rsqrt_fusion.inverse_ref, ...), custom_call_target="tpu_custom_call" | custom-call | bytes 26400000 | tf_op jit(solution)/shard_map/grads/pallas_call | solution.py:576
  143.2 2.7 %collective-permute-done.28.refs_4_.refs_5_ = s16[64,2176]{1,0:T(8,128)(2,1)S(1)} collective-permute-done((s16[64,2176]{1,0:T(8,128)(2,1)S(1)}, s16[64,2176]{1,0:T(8,128)(2,1)S(1)}, u32[]{:S(2)}, u32[]{:S(2)}) %collective-permute-start.28) | collective-permute-done | bytes 278560 | tf_op jit(solution)/shard_map/ppermute | solution.py:59
  145.8 1.6 copy-done.9
  147.4 0.9 last_sums.1
  148.4 2.3 %collective-permute-start.30 = (f32[16,4096]{1,0:T(8,128)S(1)}, f32[16,4096]{1,0:T(8,128)S(1)}, u32[]{:S(2)}, u32[]{:S(2)}) collective-permute-start(f32[16,4096]{1,0:T(8,128)S(1)} %get-tuple-element.53), channel_id=1, source_target_pairs={{0,16},{1,17},{2,18},{3,19},{4,20},{5,21},{6,22},{7,23},{8,24},{9,... | collective-permute-start | bytes 786440 | tf_op jit(solution)/shard_map/ppermute | solution.py:59
  150.6 3.6 %collective-permute-start.31 = (f32[16,4096]{1,0:T(8,128)S(1)}, f32[16,4096]{1,0:T(8,128)S(1)}, u32[]{:S(2)}, u32[]{:S(2)}) collective-permute-start(f32[16,4096]{1,0:T(8,128)S(1)} %get-tuple-element.54), channel_id=1, source_target_pairs={{16,0},{17,1},{18,2},{19,3},{20,4},{21,5},{22,6},{23,7},{24,8},{25... | collective-permute-start | bytes 786440 | tf_op jit(solution)/shard_map/ppermute | solution.py:59
  154.2 2.4 %collective-permute-done.30.up_ref = f32[16,4096]{1,0:T(8,128)S(1)} collective-permute-done((f32[16,4096]{1,0:T(8,128)S(1)}, f32[16,4096]{1,0:T(8,128)S(1)}, u32[]{:S(2)}, u32[]{:S(2)}) %collective-permute-start.30) | collective-permute-done | bytes 262176 | tf_op jit(solution)/shard_map/ppermute | solution.py:59
  156.6 4.4 %collective-permute-done.31.down_ref = f32[16,4096]{1,0:T(8,128)S(1)} collective-permute-done((f32[16,4096]{1,0:T(8,128)S(1)}, f32[16,4096]{1,0:T(8,128)S(1)}, u32[]{:S(2)}, u32[]{:S(2)}) %collective-permute-start.31) | collective-permute-done | bytes 262176 | tf_op jit(solution)/shard_map/ppermute | solution.py:59
  161.0 4.2 %adam.1 = (f32[1,96,4096]{2,1,0:T(8,128)}, f32[1,96,4096]{2,1,0:T(8,128)}, f32[1,96,4096]{2,1,0:T(8,128)}) custom-call(s32[18]{0:T(128)S(1)} %stack.75.order_ref, s32[1,9]{1,0:T(1,128)S(1)} %copy-done.12, s32[1,9]{1,0:T(1,128)S(1)} %copy-done.13, f32[64,4096]{1,0:T(8,128)S(1)} %get-tuple-element.52.grad_ref, f32[16,4096]{1,0:T(8,128)S(1)} %collective-permute-done.30.up_ref, ...), custom_call_target="tpu_custom_call" | custom-call | bytes 19800000 | tf_op jit(solution)/shard_map/adam/pallas_call | solution.py:454
  (61 shorter events, 0.3 us)
Async XLA Ops:
  0.6 25.8 %collective-permute-start.10 = (bf16[128,4096]{1,0:T(8,128)(2,1)}, bf16[128,4096]{1,0:T(8,128)(2,1)S(1)}, u32[]{:S(2)}, u32[]{:S(2)}) collective-permute-start(bf16[128,4096]{1,0:T(8,128)(2,1)} %refs_0_.2), channel_id=1, source_target_pairs={{0,12},{1,13},{2,14},{3,15},{4,0},{5,1},{6,2},{7,3},{8,4},{9,5},{1... | collective-permute-start | bytes 3145736 | tf_op jit(solution)/shard_map/ppermute | solution.py:59
  3.7 32.0 %collective-permute-start = (bf16[128,4096]{1,0:T(8,128)(2,1)}, bf16[128,4096]{1,0:T(8,128)(2,1)}, u32[]{:S(2)}, u32[]{:S(2)}) collective-permute-start(bf16[128,4096]{1,0:T(8,128)(2,1)} %refs_0_.2), channel_id=1, source_target_pairs={{0,4},{1,5},{2,6},{3,7},{4,8},{5,9},{6,10},{7,11},{8,12},{9,13},{1... | collective-permute-start | bytes 3145736 | tf_op jit(solution)/shard_map/ppermute | solution.py:59
  3.7 27.7 %collective-permute-start.2 = (bf16[128,4096]{1,0:T(8,128)(2,1)}, bf16[128,4096]{1,0:T(8,128)(2,1)}, u32[]{:S(2)}, u32[]{:S(2)}) collective-permute-start(bf16[128,4096]{1,0:T(8,128)(2,1)} %refs_0_.2), channel_id=1, source_target_pairs={{0,2},{1,3},{2,0},{3,1},{4,6},{5,7},{6,4},{7,5},{8,10},{9,11},{10,... | collective-permute-start | bytes 3145736 | tf_op jit(solution)/shard_map/ppermute | solution.py:59
  7.6 29.2 %collective-permute-start.11 = (bf16[128,4096]{1,0:T(8,128)(2,1)}, bf16[128,4096]{1,0:T(8,128)(2,1)}, u32[]{:S(2)}, u32[]{:S(2)}) collective-permute-start(bf16[128,4096]{1,0:T(8,128)(2,1)} %refs_0_.2), channel_id=1, source_target_pairs={{0,1},{1,0},{2,3},{3,2},{4,5},{5,4},{6,7},{7,6},{8,9},{9,8},{10,11... | collective-permute-start | bytes 3145736 | tf_op jit(solution)/shard_map/ppermute | solution.py:59
  11.9 19.0 %collective-permute-start.8 = (f32[16,1,128]{2,1,0:T(1,128)}, f32[16,1,128]{2,1,0:T(1,128)S(1)}, u32[]{:S(2)}, u32[]{:S(2)}) collective-permute-start(f32[16,1,128]{2,1,0:T(1,128)} %squares.1), channel_id=1, source_target_pairs={{0,2},{1,3},{2,0},{3,1},{4,6},{5,7},{6,4},{7,5},{8,10},{9,11},{10,... | collective-permute-start | bytes 24584 | tf_op jit(solution)/shard_map/ppermute | solution.py:59
  26.4 1.0 copy-start.14
  27.4 3.5 %copy-start.16 = (f32[16,1,128]{2,1,0:T(1,128)S(1)}, f32[16,1,128]{2,1,0:T(1,128)}, u32[]{:S(2)}) copy-start(f32[16,1,128]{2,1,0:T(1,128)} %squares.1) | copy-start | bytes 24580
  27.4 13.4 %copy-start.1 = (bf16[2048,512]{1,0:T(8,128)(2,1)S(1)}, bf16[2048,512]{1,0:T(8,128)(2,1)}, u32[]{:S(2)}) copy-start(bf16[2048,512]{1,0:T(8,128)(2,1)} %mixer_ref.7) | copy-start | bytes 6291460
  27.4 13.4 %copy-start.11 = (f32[512]{0:T(512)S(1)}, f32[512]{0:T(512)}, u32[]{:S(2)}) copy-start(f32[512]{0:T(512)} %param.13) | copy-start | bytes 6148
  28.9 11.9 %collective-permute-start.14 = (bf16[128,4096]{1,0:T(8,128)(2,1)S(1)}, bf16[128,4096]{1,0:T(8,128)(2,1)}, u32[]{:S(2)}, u32[]{:S(2)}) collective-permute-start(bf16[128,4096]{1,0:T(8,128)(2,1)S(1)} %broadcast_select_fusion.refs_3_), channel_id=1, source_target_pairs={{0,1},{1,0},{2,3},{3,2},{4,5},{5,4},{6,7},{7,6},{8,9},{9,8},{10,11... | collective-permute-start | bytes 3145736 | tf_op jit(solution)/shard_map/ppermute | solution.py:59
  31.0 1.3 collective-permute-start.9
  31.4 15.9 %collective-permute-start.12 = (bf16[128,4096]{1,0:T(8,128)(2,1)}, bf16[128,4096]{1,0:T(8,128)(2,1)S(1)}, u32[]{:S(2)}, u32[]{:S(2)}) collective-permute-start(bf16[128,4096]{1,0:T(8,128)(2,1)} %collective-permute-done.2.refs_1_), channel_id=1, source_target_pairs={{0,1},{1,0},{2,3},{3,2},{4,5},{5,4},{6,7},{7,6},{8,9},{9,8},{10,11... | collective-permute-start | bytes 3145736 | tf_op jit(solution)/shard_map/ppermute | solution.py:59
  32.2 29.6 %collective-permute-start.3 = (bf16[128,4096]{1,0:T(8,128)(2,1)}, bf16[128,4096]{1,0:T(8,128)(2,1)S(1)}, u32[]{:S(2)}, u32[]{:S(2)}) collective-permute-start(bf16[128,4096]{1,0:T(8,128)(2,1)} %collective-permute-done.2.refs_1_), channel_id=1, source_target_pairs={{0,12},{1,13},{2,14},{3,15},{4,0},{5,1},{6,2},{7,3},{8,4},{9,5},{1... | collective-permute-start | bytes 3145736 | tf_op jit(solution)/shard_map/ppermute | solution.py:59
  35.7 11.5 %collective-permute-start.13 = (bf16[128,4096]{1,0:T(8,128)(2,1)}, bf16[128,4096]{1,0:T(8,128)(2,1)S(1)}, u32[]{:S(2)}, u32[]{:S(2)}) collective-permute-start(bf16[128,4096]{1,0:T(8,128)(2,1)} %collective-permute-done.refs_2_), channel_id=1, source_target_pairs={{0,1},{1,0},{2,3},{3,2},{4,5},{5,4},{6,7},{7,6},{8,9},{9,8},{10,11... | collective-permute-start | bytes 3145736 | tf_op jit(solution)/shard_map/ppermute | solution.py:59
  36.8 28.4 %collective-permute-start.4 = (bf16[128,4096]{1,0:T(8,128)(2,1)}, bf16[128,4096]{1,0:T(8,128)(2,1)S(1)}, u32[]{:S(2)}, u32[]{:S(2)}) collective-permute-start(bf16[128,4096]{1,0:T(8,128)(2,1)} %collective-permute-done.refs_2_), channel_id=1, source_target_pairs={{0,2},{1,3},{2,0},{3,1},{4,6},{5,7},{6,4},{7,5},{8,10},{9,11},{10,... | collective-permute-start | bytes 3145736 | tf_op jit(solution)/shard_map/ppermute | solution.py:59
  40.8 26.7 %collective-permute-start.1 = (bf16[128,4096]{1,0:T(8,128)(2,1)}, bf16[128,4096]{1,0:T(8,128)(2,1)S(1)}, u32[]{:S(2)}, u32[]{:S(2)}) collective-permute-start(bf16[128,4096]{1,0:T(8,128)(2,1)} %collective-permute-done.refs_2_), channel_id=1, source_target_pairs={{0,4},{1,5},{2,6},{3,7},{4,8},{5,9},{6,10},{7,11},{8,12},{9,13},{1... | collective-permute-start | bytes 3145736 | tf_op jit(solution)/shard_map/ppermute | solution.py:59
  40.8 1.6 copy-start.2
  42.4 4.9 %copy-start = (bf16[512,4096]{1,0:T(8,128)(2,1)S(1)}, bf16[512,4096]{1,0:T(8,128)(2,1)}, u32[]{:S(2)}) copy-start(bf16[512,4096]{1,0:T(8,128)(2,1)} %refs_5_.1) | copy-start | bytes 12582916
  42.4 4.9 %copy-start.10 = (bf16[128,4096]{1,0:T(8,128)(2,1)S(1)}, bf16[128,4096]{1,0:T(8,128)(2,1)}, u32[]{:S(2)}) copy-start(bf16[128,4096]{1,0:T(8,128)(2,1)} %refs_0_.2) | copy-start | bytes 3145732
  47.3 24.9 %copy-start.3 = (bf16[512,2048]{1,0:T(8,128)(2,1)}, bf16[512,2048]{1,0:T(8,128)(2,1)S(1)}, u32[]{:S(2)}) copy-start(bf16[512,2048]{1,0:T(8,128)(2,1)S(1)} %hidden.1.refs_8_.refs_6_.refs_4_) | copy-start | bytes 6291460
  60.6 11.5 %copy-start.5 = (f32[512,4096]{1,0:T(8,128)}, f32[512,4096]{1,0:T(8,128)S(1)}, u32[]{:S(2)}) copy-start(f32[512,4096]{1,0:T(8,128)S(1)} %get-tuple-element.33.refs_8_) | copy-start | bytes 25165828
  60.6 6.9 %copy-start.15 = (f32[16,4096]{1,0:T(8,128)S(1)}, f32[16,4096]{1,0:T(8,128)}, u32[]{:S(2)}) copy-start(f32[16,4096]{1,0:T(8,128)} %get-tuple-element.62) | copy-start | bytes 786436
  61.9 22.7 %collective-permute-start.16 = (bf16[64,4096]{1,0:T(8,128)(2,1)S(1)}, bf16[64,4096]{1,0:T(8,128)(2,1)S(1)}, u32[]{:S(2)}, u32[]{:S(2)}) collective-permute-start(bf16[64,4096]{1,0:T(8,128)(2,1)S(1)} %slice_select_fusion), channel_id=1, source_target_pairs={{0,12},{1,13},{2,14},{3,15},{4,0},{5,1},{6,2},{7,3},{8,4},{9,5},{1... | collective-permute-start | bytes 1572872 | tf_op jit(solution)/shard_map/ppermute | solution.py:59
  65.2 6.9 %collective-permute-start.6 = (bf16[128,4096]{1,0:T(8,128)(2,1)S(1)}, bf16[128,4096]{1,0:T(8,128)(2,1)S(1)}, u32[]{:S(2)}, u32[]{:S(2)}) collective-permute-start(bf16[128,4096]{1,0:T(8,128)(2,1)S(1)} %collective-permute-done.3.refs_1_), channel_id=1, source_target_pairs={{0,1},{1,0},{2,3},{3,2},{4,5},{5,4},{6,7},{7,6},{8,9},{9,8},{10,11... | collective-permute-start | bytes 3145736 | tf_op jit(solution)/shard_map/ppermute | solution.py:59
  65.2 4.2 %collective-permute-start.7 = (bf16[128,4096]{1,0:T(8,128)(2,1)S(1)}, bf16[128,4096]{1,0:T(8,128)(2,1)S(1)}, u32[]{:S(2)}, u32[]{:S(2)}) collective-permute-start(bf16[128,4096]{1,0:T(8,128)(2,1)S(1)} %collective-permute-done.4.refs_2_), channel_id=1, source_target_pairs={{0,1},{1,0},{2,3},{3,2},{4,5},{5,4},{6,7},{7,6},{8,9},{9,8},{10,11... | collective-permute-start | bytes 3145736 | tf_op jit(solution)/shard_map/ppermute | solution.py:59
  67.4 4.7 %collective-permute-start.5 = (bf16[128,4096]{1,0:T(8,128)(2,1)S(1)}, bf16[128,4096]{1,0:T(8,128)(2,1)S(1)}, u32[]{:S(2)}, u32[]{:S(2)}) collective-permute-start(bf16[128,4096]{1,0:T(8,128)(2,1)S(1)} %collective-permute-done.1.refs_0_), channel_id=1, source_target_pairs={{0,1},{1,0},{2,3},{3,2},{4,5},{5,4},{6,7},{7,6},{8,9},{9,8},{10,11... | collective-permute-start | bytes 3145736 | tf_op jit(solution)/shard_map/ppermute | solution.py:59
  67.5 17.3 %collective-permute-start.15 = (bf16[64,4096]{1,0:T(8,128)(2,1)S(1)}, bf16[64,4096]{1,0:T(8,128)(2,1)S(1)}, u32[]{:S(2)}, u32[]{:S(2)}) collective-permute-start(bf16[64,4096]{1,0:T(8,128)(2,1)S(1)} %slice_select_fusion.1), channel_id=1, source_target_pairs={{0,4},{1,5},{2,6},{3,7},{4,8},{5,9},{6,10},{7,11},{8,12},{9,13},{1... | collective-permute-start | bytes 1572872 | tf_op jit(solution)/shard_map/ppermute | solution.py:59
  69.4 23.6 %collective-permute-start.19 = (f32[48,4096]{1,0:T(8,128)S(1)}, f32[48,4096]{1,0:T(8,128)S(1)}, u32[]{:S(2)}, u32[]{:S(2)}) collective-permute-start(f32[48,4096]{1,0:T(8,128)S(1)} %maximum_select_fusion), channel_id=1, source_target_pairs={{16,0},{17,1},{18,2},{19,3},{20,4},{21,5},{22,6},{23,7},{24,8},{25... | collective-permute-start | bytes 2359304 | tf_op jit(solution)/shard_map/ppermute | solution.py:59
  83.3 9.6 %copy-start.4 = (bf16[512,2048]{1,0:T(8,128)(2,1)S(1)}, bf16[512,2048]{1,0:T(8,128)(2,1)}, u32[]{:S(2)}) copy-start(bf16[512,2048]{1,0:T(8,128)(2,1)} %copy-done.3) | copy-start | bytes 6291460
  84.7 8.3 %collective-permute-start.18 = (bf16[64,4096]{1,0:T(8,128)(2,1)S(1)}, bf16[64,4096]{1,0:T(8,128)(2,1)S(1)}, u32[]{:S(2)}, u32[]{:S(2)}) collective-permute-start(bf16[64,4096]{1,0:T(8,128)(2,1)S(1)} %broadcast_select_fusion.1.refs_1_), channel_id=1, source_target_pairs={{0,1},{1,0},{2,3},{3,2},{4,5},{5,4},{6,7},{7,6},{8,9},{9,8},{10,11... | collective-permute-start | bytes 1572872 | tf_op jit(solution)/shard_map/ppermute | solution.py:59
  84.8 8.1 %collective-permute-start.17 = (bf16[64,4096]{1,0:T(8,128)(2,1)S(1)}, bf16[64,4096]{1,0:T(8,128)(2,1)S(1)}, u32[]{:S(2)}, u32[]{:S(2)}) collective-permute-start(bf16[64,4096]{1,0:T(8,128)(2,1)S(1)} %broadcast_select_fusion.2.refs_0_), channel_id=1, source_target_pairs={{0,1},{1,0},{2,3},{3,2},{4,5},{5,4},{6,7},{7,6},{8,9},{9,8},{10,11... | collective-permute-start | bytes 1572872 | tf_op jit(solution)/shard_map/ppermute | solution.py:59
  100.1 27.2 %collective-permute-start.23 = (s16[256,2176]{1,0:T(8,128)(2,1)S(1)}, s16[256,2176]{1,0:T(8,128)(2,1)S(1)}, u32[]{:S(2)}, u32[]{:S(2)}) collective-permute-start(s16[256,2176]{1,0:T(8,128)(2,1)S(1)} %get-tuple-element.40), channel_id=1, source_target_pairs={{0,64},{1,65},{2,66},{3,67},{4,68},{5,69},{6,70},{7,71},{8,72},{9,... | collective-permute-start | bytes 3342344 | tf_op jit(solution)/shard_map/ppermute | solution.py:59
  100.2 25.6 %collective-permute-start.20 = (s16[128,2176]{1,0:T(8,128)(2,1)S(1)}, s16[128,2176]{1,0:T(8,128)(2,1)S(1)}, u32[]{:S(2)}, u32[]{:S(2)}) collective-permute-start(s16[128,2176]{1,0:T(8,128)(2,1)S(1)} %get-tuple-element.37), channel_id=1, source_target_pairs={{0,16},{1,17},{2,18},{3,19},{4,20},{5,21},{6,22},{7,23},{8,24},{9,... | collective-permute-start | bytes 1671176 | tf_op jit(solution)/shard_map/ppermute | solution.py:59
  100.2 27.0 %collective-permute-start.21 = (s16[128,2176]{1,0:T(8,128)(2,1)S(1)}, s16[128,2176]{1,0:T(8,128)(2,1)S(1)}, u32[]{:S(2)}, u32[]{:S(2)}) collective-permute-start(s16[128,2176]{1,0:T(8,128)(2,1)S(1)} %get-tuple-element.38), channel_id=1, source_target_pairs={{0,48},{1,49},{2,50},{3,51},{4,52},{5,53},{6,54},{7,55},{8,56},{9,... | collective-permute-start | bytes 1671176 | tf_op jit(solution)/shard_map/ppermute | solution.py:59
  102.2 25.1 %collective-permute-start.22 = (s16[128,2176]{1,0:T(8,128)(2,1)S(1)}, s16[128,2176]{1,0:T(8,128)(2,1)S(1)}, u32[]{:S(2)}, u32[]{:S(2)}) collective-permute-start(s16[128,2176]{1,0:T(8,128)(2,1)S(1)} %get-tuple-element.39), channel_id=1, source_target_pairs={{0,32},{1,33},{2,34},{3,35},{4,36},{5,37},{6,38},{7,39},{8,40},{9,... | collective-permute-start | bytes 1671176 | tf_op jit(solution)/shard_map/ppermute | solution.py:59
  102.5 7.0 %copy-start.6 = (f32[1,96,4096]{2,1,0:T(8,128)S(1)}, f32[1,96,4096]{2,1,0:T(8,128)}, u32[]{:S(2)}) copy-start(f32[1,96,4096]{2,1,0:T(8,128)} %refs_0_.3) | copy-start | bytes 4718596
  102.5 7.0 %copy-start.7 = (f32[1,96,4096]{2,1,0:T(8,128)S(1)}, f32[1,96,4096]{2,1,0:T(8,128)}, u32[]{:S(2)}) copy-start(f32[1,96,4096]{2,1,0:T(8,128)} %refs_2_.1) | copy-start | bytes 4718596
  102.5 7.0 %copy-start.8 = (f32[1,96,4096]{2,1,0:T(8,128)S(1)}, f32[1,96,4096]{2,1,0:T(8,128)}, u32[]{:S(2)}) copy-start(f32[1,96,4096]{2,1,0:T(8,128)} %refs_1_.1) | copy-start | bytes 4718596
  102.5 7.0 %copy-start.12 = (s32[1,9]{1,0:T(1,128)S(1)}, s32[1,9]{1,0:T(1,128)}, u32[]{:S(2)}) copy-start(s32[1,9]{1,0:T(1,128)} %old_ref.3) | copy-start | bytes 112
  102.5 7.0 %copy-start.13 = (s32[1,9]{1,0:T(1,128)S(1)}, s32[1,9]{1,0:T(1,128)}, u32[]{:S(2)}) copy-start(s32[1,9]{1,0:T(1,128)} %new_ref.3) | copy-start | bytes 112
  106.2 1.3 collective-permute-start.24
  107.5 18.3 %collective-permute-start.25 = (f32[16,1,128]{2,1,0:T(1,128)S(1)}, f32[16,1,128]{2,1,0:T(1,128)S(1)}, u32[]{:S(2)}, u32[]{:S(2)}) collective-permute-start(f32[16,1,128]{2,1,0:T(1,128)S(1)} %add.257), channel_id=1, source_target_pairs={{0,2},{1,3},{2,0},{3,1},{4,6},{5,7},{6,4},{7,5},{8,10},{9,11},{10,... | collective-permute-start | bytes 24584 | tf_op jit(solution)/shard_map/ppermute | solution.py:59
  129.4 13.7 %collective-permute-start.26 = (s16[64,2176]{1,0:T(8,128)(2,1)S(1)}, s16[64,2176]{1,0:T(8,128)(2,1)S(1)}, u32[]{:S(2)}, u32[]{:S(2)}) collective-permute-start(s16[64,2176]{1,0:T(8,128)(2,1)S(1)} %get-tuple-element.45), channel_id=1, source_target_pairs={{0,64},{1,65},{2,66},{3,67},{4,68},{5,69},{6,70},{7,71},{8,72},{9,... | collective-permute-start | bytes 835592 | tf_op jit(solution)/shard_map/ppermute | solution.py:59
  131.1 12.1 %collective-permute-start.27 = (s16[64,2176]{1,0:T(8,128)(2,1)S(1)}, s16[64,2176]{1,0:T(8,128)(2,1)S(1)}, u32[]{:S(2)}, u32[]{:S(2)}) collective-permute-start(s16[64,2176]{1,0:T(8,128)(2,1)S(1)} %get-tuple-element.46), channel_id=1, source_target_pairs={{0,16},{1,17},{2,18},{3,19},{4,20},{5,21},{6,22},{7,23},{8,24},{9,... | collective-permute-start | bytes 835592 | tf_op jit(solution)/shard_map/ppermute | solution.py:59
  132.5 13.3 %collective-permute-start.28 = (s16[64,2176]{1,0:T(8,128)(2,1)S(1)}, s16[64,2176]{1,0:T(8,128)(2,1)S(1)}, u32[]{:S(2)}, u32[]{:S(2)}) collective-permute-start(s16[64,2176]{1,0:T(8,128)(2,1)S(1)} %get-tuple-element.47), channel_id=1, source_target_pairs={{0,48},{1,49},{2,50},{3,51},{4,52},{5,53},{6,54},{7,55},{8,56},{9,... | collective-permute-start | bytes 835592 | tf_op jit(solution)/shard_map/ppermute | solution.py:59
  133.1 12.7 %collective-permute-start.29 = (s16[64,2176]{1,0:T(8,128)(2,1)S(1)}, s16[64,2176]{1,0:T(8,128)(2,1)S(1)}, u32[]{:S(2)}, u32[]{:S(2)}) collective-permute-start(s16[64,2176]{1,0:T(8,128)(2,1)S(1)} %get-tuple-element.48), channel_id=1, source_target_pairs={{0,32},{1,33},{2,34},{3,35},{4,36},{5,37},{6,38},{7,39},{8,40},{9,... | collective-permute-start | bytes 835592 | tf_op jit(solution)/shard_map/ppermute | solution.py:59
  145.8 1.6 copy-start.9
  148.4 8.3 %collective-permute-start.30 = (f32[16,4096]{1,0:T(8,128)S(1)}, f32[16,4096]{1,0:T(8,128)S(1)}, u32[]{:S(2)}, u32[]{:S(2)}) collective-permute-start(f32[16,4096]{1,0:T(8,128)S(1)} %get-tuple-element.53), channel_id=1, source_target_pairs={{0,16},{1,17},{2,18},{3,19},{4,20},{5,21},{6,22},{7,23},{8,24},{9,... | collective-permute-start | bytes 786440 | tf_op jit(solution)/shard_map/ppermute | solution.py:59
  150.6 10.4 %collective-permute-start.31 = (f32[16,4096]{1,0:T(8,128)S(1)}, f32[16,4096]{1,0:T(8,128)S(1)}, u32[]{:S(2)}, u32[]{:S(2)}) collective-permute-start(f32[16,4096]{1,0:T(8,128)S(1)} %get-tuple-element.54), channel_id=1, source_target_pairs={{16,0},{17,1},{18,2},{19,3},{20,4},{21,5},{22,6},{23,7},{24,8},{25... | collective-permute-start | bytes 786440 | tf_op jit(solution)/shard_map/ppermute | solution.py:59

commit v4 on v3

--- a/solution.py
+++ b/solution.py
@@ -296,7 +296,7 @@
         in_specs=[ANYWHERE] * (count + 1) + [wide(channels)] + ([] if before is None else [wide(channels), ANYWHERE]),
         out_specs=[wide(channels), ANYWHERE],
         out_shape=[grad, back],
-        input_output_aliases={} if before is None else {count + 3: 1},
+        input_output_aliases={} if before is None else {count + 2: 0, count + 3: 1},
         scratch_shapes=[
             pltpu.VMEM((tokens, width), BF16),
             pltpu.VMEM((channels, tokens), BF16),

time: 166 us -> 166 us (level)
    unnamed x34 -> x32, local copies, waits for them, and re-layouts: 4.21 us -> 4.21 us
where the time goes in v4:
time: 166 us; the launch traced here: 165 us
  Pallas kernels  64.8 us (39%)
  waiting for transfers between devices  47.4 us (29%)
  starting transfers between devices  38.9 us (23%)
  local copies, waits for them, and re-layouts  9.26 us (6%)
  between operations  3.11 us (2%)
  other arithmetic  1.72 us (1%)
    ppermute x32, waiting for transfers between devices, move(): return lax.ppermute(value, AXES, pairs)  47.4 us
    ppermute x32, starting transfers between devices, move(): return lax.ppermute(value, AXES, pairs)  38.9 us
    pallas_call x2, Pallas kernels, products(): pl.pallas_call(lambda *refs: kernel(count, start, steps, *refs), grid=(st...  23.5 us
    pallas_call x1, Pallas kernels, local(): ordered(grads_kernel, [here, there, there, there_row, there_row, gain_spe...  8.01 us
    pallas_call x1, Pallas kernels, late_products(): pl.pallas_call(lambda *refs: late_kernel(count, start, steps, *refs[:coun...  7.11 us
    pallas_call x1, Pallas kernels, place(): share_call(place_kernel, tile, [state] * 3 + [part(3 * HALO)], [part(CAP)...  6.09 us
    pallas_call x1, Pallas kernels, local(): ordered(hidden_kernel, [there, there, there_row, gain_spec], pl.BlockSpec...  4.86 us
    pallas_call x1, Pallas kernels, local(): pl.pallas_call(square_kernel, grid=(blocks // 4,), in_specs=[block_spec,...  4.34 us
  transfers between devices with their start and end apart: 32, of which 12 were waited for; matrix products, arithmetic and copies ran while one was open for 4% of the time, Pallas kernels for 31%

profile of v4, /device:TPU:6, one launch (start us, length us, event | category | flops | bytes accessed | tf_op | source)
XLA Modules:
  0.0 165.2 jit_solution(13817190651740295999)
XLA Ops:
  0.6 3.1 %collective-permute-start.10 = (bf16[128,4096]{1,0:T(8,128)(2,1)}, bf16[128,4096]{1,0:T(8,128)(2,1)S(1)}, u32[]{:S(2)}, u32[]{:S(2)}) collective-permute-start(bf16[128,4096]{1,0:T(8,128)(2,1)} %refs_0_.2), channel_id=1, source_target_pairs={{0,12},{1,13},{2,14},{3,15},{4,0},{5,1},{6,2},{7,3},{8,4},{9,5},{1... | collective-permute-start | bytes 3145736 | tf_op jit(solution)/shard_map/ppermute | solution.py:59
  3.7 3.9 %collective-permute-start.2 = (bf16[128,4096]{1,0:T(8,128)(2,1)}, bf16[128,4096]{1,0:T(8,128)(2,1)}, u32[]{:S(2)}, u32[]{:S(2)}) collective-permute-start(bf16[128,4096]{1,0:T(8,128)(2,1)} %refs_0_.2), channel_id=1, source_target_pairs={{0,2},{1,3},{2,0},{3,1},{4,6},{5,7},{6,4},{7,5},{8,10},{9,11},{10,... | collective-permute-start | bytes 3145736 | tf_op jit(solution)/shard_map/ppermute | solution.py:59
  7.6 4.3 %squares.1 = f32[16,1,128]{2,1,0:T(1,128)} custom-call(bf16[2048,512]{1,0:T(8,128)(2,1)} %mixer_ref.7, bf16[2048,512]{1,0:T(8,128)(2,1)} %gate_ref.7), custom_call_target="tpu_custom_call" | custom-call | bytes 9900000 | tf_op jit(solution)/shard_map/squares/pallas_call | solution.py:496
  11.9 0.0 collective-permute-start.8
  12.0 1.2 slice.35
  13.8 12.6 %collective-permute-done.10 = bf16[128,4096]{1,0:T(8,128)(2,1)S(1)} collective-permute-done((bf16[128,4096]{1,0:T(8,128)(2,1)}, bf16[128,4096]{1,0:T(8,128)(2,1)S(1)}, u32[]{:S(2)}, u32[]{:S(2)}) %collective-permute-start.10) | collective-permute-done | bytes 1048608 | tf_op jit(solution)/shard_map/ppermute | solution.py:59
  26.4 1.0 copy-done.13
  27.4 1.4 broadcast_select_fusion.refs_3_
  28.9 0.1 collective-permute-start.14
  29.0 1.8 %slice_bitcast_fusion = (f32[16,4096]{1,0:T(8,128)S(1)}, f32[16,4096]{1,0:T(8,128)}) fusion(f32[1,96,4096]{2,1,0:T(8,128)} %refs_2_.1, f32[1,96,4096]{2,1,0:T(8,128)} %refs_1_.1), kind=kLoop, calls=%fused_computation.6 | loop fusion | bytes 1048576 | tf_op jit(solution)/shard_map/squeeze | solution.py:552
  30.7 0.2 collective-permute-done.8
  31.0 0.4 collective-permute-start.9
  31.3 0.1 stack.75.order_ref
  31.4 0.3 collective-permute-start.12
  31.7 0.5 collective-permute-done.9
  32.2 3.5 %collective-permute-start.3 = (bf16[128,4096]{1,0:T(8,128)(2,1)}, bf16[128,4096]{1,0:T(8,128)(2,1)S(1)}, u32[]{:S(2)}, u32[]{:S(2)}) collective-permute-start(bf16[128,4096]{1,0:T(8,128)(2,1)} %collective-permute-done.2.refs_1_), channel_id=1, source_target_pairs={{0,12},{1,13},{2,14},{3,15},{4,0},{5,1},{6,2},{7,3},{8,4},{9,5},{1... | collective-permute-start | bytes 3145736 | tf_op jit(solution)/shard_map/ppermute | solution.py:59
  35.7 0.1 collective-permute-start.13
  35.8 1.0 slice_bitcast_fusion.2
  36.8 4.0 %collective-permute-start.4 = (bf16[128,4096]{1,0:T(8,128)(2,1)}, bf16[128,4096]{1,0:T(8,128)(2,1)S(1)}, u32[]{:S(2)}, u32[]{:S(2)}) collective-permute-start(bf16[128,4096]{1,0:T(8,128)(2,1)} %collective-permute-done.refs_2_), channel_id=1, source_target_pairs={{0,2},{1,3},{2,0},{3,1},{4,6},{5,7},{6,4},{7,5},{8,10},{9,11},{10,... | collective-permute-start | bytes 3145736 | tf_op jit(solution)/shard_map/ppermute | solution.py:59
  40.8 0.0 copy-start.2
  40.8 1.6 copy-done.2
  42.4 4.9 %hidden.1.refs_8_.refs_6_.refs_4_ = bf16[512,2048]{1,0:T(8,128)(2,1)S(1)} custom-call(s32[18]{0:T(128)S(1)} %stack.75.order_ref, bf16[2048,512]{1,0:T(8,128)(2,1)S(1)} %copy-done.1, bf16[2048,512]{1,0:T(8,128)(2,1)S(1)} %copy-done.2, f32[16,1,128]{2,1,0:T(1,128)S(1)} %add_rsqrt_fusion.inverse_ref, f32[1,512]{1,0:T(1,128)S(1)} %bitcast.28), custom_call_target="tpu_custom_call" | custom-call | bytes 16500000 | tf_op jit(solution)/shard_map/hidden/pallas_call | solution.py:528
  47.3 13.3 %products.2 = (f32[512,4096]{1,0:T(8,128)S(1)}, f32[2048,512]{1,0:T(8,128)S(1)}) custom-call(bf16[128,4096]{1,0:T(8,128)(2,1)S(1)} %copy-done.9, bf16[128,4096]{1,0:T(8,128)(2,1)} %collective-permute-done.2.refs_1_, bf16[128,4096]{1,0:T(8,128)(2,1)} %collective-permute-done.refs_2_, bf16[128,4096]{1,0:T(8,128)(2,1)S(1)} %broadcast_select_fusion.refs_3_, ...), custom_call_target="tpu_custom_call" | custom-call | bytes 59400000 | tf_op jit(solution)/shard_map/products/pallas_call | solution.py:293
  60.6 0.5 slice.29
  61.9 3.3 %collective-permute-start.16 = (bf16[64,4096]{1,0:T(8,128)(2,1)S(1)}, bf16[64,4096]{1,0:T(8,128)(2,1)S(1)}, u32[]{:S(2)}, u32[]{:S(2)}) collective-permute-start(bf16[64,4096]{1,0:T(8,128)(2,1)S(1)} %slice_select_fusion), channel_id=1, source_target_pairs={{0,12},{1,13},{2,14},{3,15},{4,0},{5,1},{6,2},{7,3},{8,4},{9,5},{1... | collective-permute-start | bytes 1572872 | tf_op jit(solution)/shard_map/ppermute | solution.py:59
  65.2 0.5 collective-permute-start.7
  65.7 1.7 %collective-permute-done.1.refs_0_ = bf16[128,4096]{1,0:T(8,128)(2,1)S(1)} collective-permute-done((bf16[128,4096]{1,0:T(8,128)(2,1)}, bf16[128,4096]{1,0:T(8,128)(2,1)S(1)}, u32[]{:S(2)}, u32[]{:S(2)}) %collective-permute-start.1) | collective-permute-done | bytes 1048608 | tf_op jit(solution)/shard_map/ppermute | solution.py:59
  67.5 0.1 collective-permute-start.15
  67.5 0.1 maximum_select_fusion
  67.6 1.7 %collective-permute-done.7.refs_5_ = bf16[128,4096]{1,0:T(8,128)(2,1)S(1)} collective-permute-done((bf16[128,4096]{1,0:T(8,128)(2,1)S(1)}, bf16[128,4096]{1,0:T(8,128)(2,1)S(1)}, u32[]{:S(2)}, u32[]{:S(2)}) %collective-permute-start.7) | collective-permute-done | bytes 1048608 | tf_op jit(solution)/shard_map/ppermute | solution.py:59
  69.3 2.7 %collective-permute-start.19 = (f32[48,4096]{1,0:T(8,128)S(1)}, f32[48,4096]{1,0:T(8,128)S(1)}, u32[]{:S(2)}, u32[]{:S(2)}) collective-permute-start(f32[48,4096]{1,0:T(8,128)S(1)} %maximum_select_fusion), channel_id=1, source_target_pairs={{16,0},{17,1},{18,2},{19,3},{20,4},{21,5},{22,6},{23,7},{24,8},{25... | collective-permute-start | bytes 2359304 | tf_op jit(solution)/shard_map/ppermute | solution.py:59
  72.1 10.2 %products.3 = (f32[512,4096]{1,0:T(8,128)S(1)}, f32[2048,512]{1,0:T(8,128)S(1)}) custom-call(bf16[128,4096]{1,0:T(8,128)(2,1)S(1)} %collective-permute-done.1.refs_0_, bf16[128,4096]{1,0:T(8,128)(2,1)S(1)} %collective-permute-done.3.refs_1_, bf16[128,4096]{1,0:T(8,128)(2,1)S(1)} %collective-permute-done.4.refs_2_, ...), custom_call_target="tpu_custom_call", output_to_operand_aliasing={{0}: (8, {}), {1}: (9, {})} | custom-call | bytes 52800000 | tf_op jit(solution)/shard_map/products/pallas_call | solution.py:293
  82.3 0.0 copy-start.4
  82.3 0.5 slice.28
  83.6 0.1 collective-permute-start.18
  83.8 0.7 collective-permute-start.17
  84.5 8.4 %collective-permute-done.19.refs_8_.refs_3_ = f32[48,4096]{1,0:T(8,128)S(1)} collective-permute-done((f32[48,4096]{1,0:T(8,128)S(1)}, f32[48,4096]{1,0:T(8,128)S(1)}, u32[]{:S(2)}, u32[]{:S(2)}) %collective-permute-start.19) | collective-permute-done | bytes 786464 | tf_op jit(solution)/shard_map/ppermute | solution.py:59
  92.9 7.1 %late_products.1 = (s16[128,2176]{1,0:T(8,128)(2,1)S(1)}, s16[128,2176]{1,0:T(8,128)(2,1)S(1)}, s16[128,2176]{1,0:T(8,128)(2,1)S(1)}, s16[256,2176]{1,0:T(8,128)...) custom-call(bf16[64,4096]{1,0:T(8,128)(2,1)S(1)} %broadcast_select_f, ...), custom_call_target="tpu_custom_call", output_to_operand_aliasing={{6}: (7, {})} | custom-call | bytes 29700000 | tf_op jit(solution)/shard_map/late_products/pallas_call | solution.py:321
  100.0 0.1 collective-permute-start.23
  100.1 0.1 collective-permute-start.20
  100.2 2.0 %collective-permute-start.21 = (s16[128,2176]{1,0:T(8,128)(2,1)S(1)}, s16[128,2176]{1,0:T(8,128)(2,1)S(1)}, u32[]{:S(2)}, u32[]{:S(2)}) collective-permute-start(s16[128,2176]{1,0:T(8,128)(2,1)S(1)} %get-tuple-element.38), channel_id=1, source_target_pairs={{0,48},{1,49},{2,50},{3,51},{4,52},{5,53},{6,54},{7,55},{8,56},{9,... | collective-permute-start | bytes 1671176 | tf_op jit(solution)/shard_map/ppermute | solution.py:59
  102.2 0.2 collective-permute-start.22
  102.5 0.0 copy-start.12
  102.5 3.7 %centre.1 = f32[16,1,128]{2,1,0:T(1,128)S(1)} custom-call(s32[18]{0:T(128)S(1)} %stack.75.order_ref, f32[2048,512]{1,0:T(8,128)S(1)} %get-tuple-element.43.back_ref, bf16[2048,512]{1,0:T(8,128)(2,1)S(1)} %copy-done.1, bf16[2048,512]{1,0:T(8,128)(2,1)S(1)} %copy-done.2, f32[16,1,128]{2,1,0:T(1,128)S(1)} %add_rsqrt_fusion.inverse_ref, f32[1,512]{1,0:T(1,128)S(1)} %bitcast.29), custom_call_target="tpu_custom_call" | custom-call | bytes 13200000 | tf_op jit(solution)/shard_map/centre/pallas_call | solution.py:563
  106.2 0.1 collective-permute-start.24
  106.3 1.2 collective-permute-done.24
  107.4 2.1 %collective-permute-start.25 = (f32[16,1,128]{2,1,0:T(1,128)S(1)}, f32[16,1,128]{2,1,0:T(1,128)S(1)}, u32[]{:S(2)}, u32[]{:S(2)}) collective-permute-start(f32[16,1,128]{2,1,0:T(1,128)S(1)} %add.257), channel_id=1, source_target_pairs={{0,2},{1,3},{2,0},{3,1},{4,6},{5,7},{6,4},{7,5},{8,10},{9,11},{10,... | collective-permute-start | bytes 24584 | tf_op jit(solution)/shard_map/ppermute | solution.py:59
  109.5 6.1 %place.1 = (f32[96,4096]{1,0:T(8,128)S(1)}, f32[96,4096]{1,0:T(8,128)S(1)}, f32[96,4096]{1,0:T(8,128)S(1)}) custom-call(s32[18]{0:T(128)S(1)} %stack.75.order_ref, s32[1,9]{1,0:T(1,128)S(1)} %copy-done.11, s32[1,9]{1,0:T(1,128)S(1)} %copy-done.12, f32[1,96,4096]{2,1,0:T(8,128)S(1)} %copy-done.5, f32[1,96,4096]{2,1,0:T(8,128)S(1)} %copy-done.7, ...), custom_call_target="tpu_custom_call" | custom-call | bytes 19800000 | tf_op jit(solution)/shard_map/place/pallas_call | solution.py:443
  115.6 10.1 %collective-permute-done.25 = f32[16,1,128]{2,1,0:T(1,128)S(1)} collective-permute-done((f32[16,1,128]{2,1,0:T(1,128)S(1)}, f32[16,1,128]{2,1,0:T(1,128)S(1)}, u32[]{:S(2)}, u32[]{:S(2)}) %collective-permute-start.25) | collective-permute-done | bytes 8224 | tf_op jit(solution)/shard_map/ppermute | solution.py:59
  125.7 1.5 collective-permute-done.21.refs_2_.refs_3_
  127.3 2.1 %middle_sums.1 = (s16[64,2176]{1,0:T(8,128)(2,1)S(1)}, s16[64,2176]{1,0:T(8,128)(2,1)S(1)}, s16[64,2176]{1,0:T(8,128)(2,1)S(1)}, s16[64,2176]{1,0:T(8,128)(2,1)S...) custom-call(s16[128,2176]{1,0:T(8,128)(2,1)S(1)} %collective-permute-done.20.refs_0_.refs_1_, ...), custom_call_target="tpu_custom_call" | custom-call | bytes 9900000 | tf_op jit(solution)/shard_map/middle_sums/pallas_call | solution.py:358
  129.4 1.7 %collective-permute-start.26 = (s16[64,2176]{1,0:T(8,128)(2,1)S(1)}, s16[64,2176]{1,0:T(8,128)(2,1)S(1)}, u32[]{:S(2)}, u32[]{:S(2)}) collective-permute-start(s16[64,2176]{1,0:T(8,128)(2,1)S(1)} %get-tuple-element.45), channel_id=1, source_target_pairs={{0,64},{1,65},{2,66},{3,67},{4,68},{5,69},{6,70},{7,71},{8,72},{9,... | collective-permute-start | bytes 835592 | tf_op jit(solution)/shard_map/ppermute | solution.py:59
  131.0 1.5 collective-permute-start.27
  132.5 0.6 collective-permute-start.28
  133.1 2.0 %collective-permute-start.29 = (s16[64,2176]{1,0:T(8,128)(2,1)S(1)}, s16[64,2176]{1,0:T(8,128)(2,1)S(1)}, u32[]{:S(2)}, u32[]{:S(2)}) collective-permute-start(s16[64,2176]{1,0:T(8,128)(2,1)S(1)} %get-tuple-element.48), channel_id=1, source_target_pairs={{0,32},{1,33},{2,34},{3,35},{4,36},{5,37},{6,38},{7,39},{8,40},{9,... | collective-permute-start | bytes 835592 | tf_op jit(solution)/shard_map/ppermute | solution.py:59
  135.1 8.0 %grads.1 = (bf16[2048,512]{1,0:T(8,128)(2,1)}, bf16[2048,512]{1,0:T(8,128)(2,1)}) custom-call(s32[18]{0:T(128)S(1)} %stack.75.order_ref, f32[2048,512]{1,0:T(8,128)S(1)} %get-tuple-element.43.back_ref, bf16[2048,512]{1,0:T(8,128)(2,1)S(1)} %copy-done.1, bf16[2048,512]{1,0:T(8,128)(2,1)S(1)} %copy-done.2, f32[16,1,128]{2,1,0:T(1,128)S(1)} %add_rsqrt_fusion.inverse_ref, ...), custom_call_target="tpu_custom_call" | custom-call | bytes 26400000 | tf_op jit(solution)/shard_map/grads/pallas_call | solution.py:576
  143.1 2.7 %collective-permute-done.28.refs_4_.refs_5_ = s16[64,2176]{1,0:T(8,128)(2,1)S(1)} collective-permute-done((s16[64,2176]{1,0:T(8,128)(2,1)S(1)}, s16[64,2176]{1,0:T(8,128)(2,1)S(1)}, u32[]{:S(2)}, u32[]{:S(2)}) %collective-permute-start.28) | collective-permute-done | bytes 278560 | tf_op jit(solution)/shard_map/ppermute | solution.py:59
  145.8 1.6 copy-done.8
  147.4 0.9 last_sums.1
  148.3 2.3 %collective-permute-start.30 = (f32[16,4096]{1,0:T(8,128)S(1)}, f32[16,4096]{1,0:T(8,128)S(1)}, u32[]{:S(2)}, u32[]{:S(2)}) collective-permute-start(f32[16,4096]{1,0:T(8,128)S(1)} %get-tuple-element.53), channel_id=1, source_target_pairs={{0,16},{1,17},{2,18},{3,19},{4,20},{5,21},{6,22},{7,23},{8,24},{9,... | collective-permute-start | bytes 786440 | tf_op jit(solution)/shard_map/ppermute | solution.py:59
  150.6 3.6 %collective-permute-start.31 = (f32[16,4096]{1,0:T(8,128)S(1)}, f32[16,4096]{1,0:T(8,128)S(1)}, u32[]{:S(2)}, u32[]{:S(2)}) collective-permute-start(f32[16,4096]{1,0:T(8,128)S(1)} %get-tuple-element.54), channel_id=1, source_target_pairs={{16,0},{17,1},{18,2},{19,3},{20,4},{21,5},{22,6},{23,7},{24,8},{25... | collective-permute-start | bytes 786440 | tf_op jit(solution)/shard_map/ppermute | solution.py:59
  154.2 2.4 %collective-permute-done.30.up_ref = f32[16,4096]{1,0:T(8,128)S(1)} collective-permute-done((f32[16,4096]{1,0:T(8,128)S(1)}, f32[16,4096]{1,0:T(8,128)S(1)}, u32[]{:S(2)}, u32[]{:S(2)}) %collective-permute-start.30) | collective-permute-done | bytes 262176 | tf_op jit(solution)/shard_map/ppermute | solution.py:59
  156.6 4.4 %collective-permute-done.31.down_ref = f32[16,4096]{1,0:T(8,128)S(1)} collective-permute-done((f32[16,4096]{1,0:T(8,128)S(1)}, f32[16,4096]{1,0:T(8,128)S(1)}, u32[]{:S(2)}, u32[]{:S(2)}) %collective-permute-start.31) | collective-permute-done | bytes 262176 | tf_op jit(solution)/shard_map/ppermute | solution.py:59
  161.0 4.2 %adam.1 = (f32[1,96,4096]{2,1,0:T(8,128)}, f32[1,96,4096]{2,1,0:T(8,128)}, f32[1,96,4096]{2,1,0:T(8,128)}) custom-call(s32[18]{0:T(128)S(1)} %stack.75.order_ref, s32[1,9]{1,0:T(1,128)S(1)} %copy-done.11, s32[1,9]{1,0:T(1,128)S(1)} %copy-done.12, f32[64,4096]{1,0:T(8,128)S(1)} %get-tuple-element.52.grad_ref, f32[16,4096]{1,0:T(8,128)S(1)} %collective-permute-done.30.up_ref, ...), custom_call_target="tpu_custom_call" | custom-call | bytes 19800000 | tf_op jit(solution)/shard_map/adam/pallas_call | solution.py:454
  (59 shorter events, 0.3 us)
Async XLA Ops:
  0.6 25.8 %collective-permute-start.10 = (bf16[128,4096]{1,0:T(8,128)(2,1)}, bf16[128,4096]{1,0:T(8,128)(2,1)S(1)}, u32[]{:S(2)}, u32[]{:S(2)}) collective-permute-start(bf16[128,4096]{1,0:T(8,128)(2,1)} %refs_0_.2), channel_id=1, source_target_pairs={{0,12},{1,13},{2,14},{3,15},{4,0},{5,1},{6,2},{7,3},{8,4},{9,5},{1... | collective-permute-start | bytes 3145736 | tf_op jit(solution)/shard_map/ppermute | solution.py:59
  3.7 32.0 %collective-permute-start = (bf16[128,4096]{1,0:T(8,128)(2,1)}, bf16[128,4096]{1,0:T(8,128)(2,1)}, u32[]{:S(2)}, u32[]{:S(2)}) collective-permute-start(bf16[128,4096]{1,0:T(8,128)(2,1)} %refs_0_.2), channel_id=1, source_target_pairs={{0,4},{1,5},{2,6},{3,7},{4,8},{5,9},{6,10},{7,11},{8,12},{9,13},{1... | collective-permute-start | bytes 3145736 | tf_op jit(solution)/shard_map/ppermute | solution.py:59
  3.7 27.7 %collective-permute-start.2 = (bf16[128,4096]{1,0:T(8,128)(2,1)}, bf16[128,4096]{1,0:T(8,128)(2,1)}, u32[]{:S(2)}, u32[]{:S(2)}) collective-permute-start(bf16[128,4096]{1,0:T(8,128)(2,1)} %refs_0_.2), channel_id=1, source_target_pairs={{0,2},{1,3},{2,0},{3,1},{4,6},{5,7},{6,4},{7,5},{8,10},{9,11},{10,... | collective-permute-start | bytes 3145736 | tf_op jit(solution)/shard_map/ppermute | solution.py:59
  7.6 29.2 %collective-permute-start.11 = (bf16[128,4096]{1,0:T(8,128)(2,1)}, bf16[128,4096]{1,0:T(8,128)(2,1)}, u32[]{:S(2)}, u32[]{:S(2)}) collective-permute-start(bf16[128,4096]{1,0:T(8,128)(2,1)} %refs_0_.2), channel_id=1, source_target_pairs={{0,1},{1,0},{2,3},{3,2},{4,5},{5,4},{6,7},{7,6},{8,9},{9,8},{10,11... | collective-permute-start | bytes 3145736 | tf_op jit(solution)/shard_map/ppermute | solution.py:59
  11.9 19.0 %collective-permute-start.8 = (f32[16,1,128]{2,1,0:T(1,128)}, f32[16,1,128]{2,1,0:T(1,128)S(1)}, u32[]{:S(2)}, u32[]{:S(2)}) collective-permute-start(f32[16,1,128]{2,1,0:T(1,128)} %squares.1), channel_id=1, source_target_pairs={{0,2},{1,3},{2,0},{3,1},{4,6},{5,7},{6,4},{7,5},{8,10},{9,11},{10,... | collective-permute-start | bytes 24584 | tf_op jit(solution)/shard_map/ppermute | solution.py:59
  26.4 1.0 copy-start.13
  27.4 3.5 %copy-start.15 = (f32[16,1,128]{2,1,0:T(1,128)S(1)}, f32[16,1,128]{2,1,0:T(1,128)}, u32[]{:S(2)}) copy-start(f32[16,1,128]{2,1,0:T(1,128)} %squares.1) | copy-start | bytes 24580
  27.4 13.4 %copy-start.1 = (bf16[2048,512]{1,0:T(8,128)(2,1)S(1)}, bf16[2048,512]{1,0:T(8,128)(2,1)}, u32[]{:S(2)}) copy-start(bf16[2048,512]{1,0:T(8,128)(2,1)} %mixer_ref.7) | copy-start | bytes 6291460
  27.4 13.4 %copy-start.10 = (f32[512]{0:T(512)S(1)}, f32[512]{0:T(512)}, u32[]{:S(2)}) copy-start(f32[512]{0:T(512)} %param.13) | copy-start | bytes 6148
  28.9 11.9 %collective-permute-start.14 = (bf16[128,4096]{1,0:T(8,128)(2,1)S(1)}, bf16[128,4096]{1,0:T(8,128)(2,1)}, u32[]{:S(2)}, u32[]{:S(2)}) collective-permute-start(bf16[128,4096]{1,0:T(8,128)(2,1)S(1)} %broadcast_select_fusion.refs_3_), channel_id=1, source_target_pairs={{0,1},{1,0},{2,3},{3,2},{4,5},{5,4},{6,7},{7,6},{8,9},{9,8},{10,11... | collective-permute-start | bytes 3145736 | tf_op jit(solution)/shard_map/ppermute | solution.py:59
  31.0 1.3 collective-permute-start.9
  31.4 15.9 %collective-permute-start.12 = (bf16[128,4096]{1,0:T(8,128)(2,1)}, bf16[128,4096]{1,0:T(8,128)(2,1)S(1)}, u32[]{:S(2)}, u32[]{:S(2)}) collective-permute-start(bf16[128,4096]{1,0:T(8,128)(2,1)} %collective-permute-done.2.refs_1_), channel_id=1, source_target_pairs={{0,1},{1,0},{2,3},{3,2},{4,5},{5,4},{6,7},{7,6},{8,9},{9,8},{10,11... | collective-permute-start | bytes 3145736 | tf_op jit(solution)/shard_map/ppermute | solution.py:59
  32.2 29.6 %collective-permute-start.3 = (bf16[128,4096]{1,0:T(8,128)(2,1)}, bf16[128,4096]{1,0:T(8,128)(2,1)S(1)}, u32[]{:S(2)}, u32[]{:S(2)}) collective-permute-start(bf16[128,4096]{1,0:T(8,128)(2,1)} %collective-permute-done.2.refs_1_), channel_id=1, source_target_pairs={{0,12},{1,13},{2,14},{3,15},{4,0},{5,1},{6,2},{7,3},{8,4},{9,5},{1... | collective-permute-start | bytes 3145736 | tf_op jit(solution)/shard_map/ppermute | solution.py:59
  35.7 11.5 %collective-permute-start.13 = (bf16[128,4096]{1,0:T(8,128)(2,1)}, bf16[128,4096]{1,0:T(8,128)(2,1)S(1)}, u32[]{:S(2)}, u32[]{:S(2)}) collective-permute-start(bf16[128,4096]{1,0:T(8,128)(2,1)} %collective-permute-done.refs_2_), channel_id=1, source_target_pairs={{0,1},{1,0},{2,3},{3,2},{4,5},{5,4},{6,7},{7,6},{8,9},{9,8},{10,11... | collective-permute-start | bytes 3145736 | tf_op jit(solution)/shard_map/ppermute | solution.py:59
  36.8 28.4 %collective-permute-start.4 = (bf16[128,4096]{1,0:T(8,128)(2,1)}, bf16[128,4096]{1,0:T(8,128)(2,1)S(1)}, u32[]{:S(2)}, u32[]{:S(2)}) collective-permute-start(bf16[128,4096]{1,0:T(8,128)(2,1)} %collective-permute-done.refs_2_), channel_id=1, source_target_pairs={{0,2},{1,3},{2,0},{3,1},{4,6},{5,7},{6,4},{7,5},{8,10},{9,11},{10,... | collective-permute-start | bytes 3145736 | tf_op jit(solution)/shard_map/ppermute | solution.py:59
  40.8 26.7 %collective-permute-start.1 = (bf16[128,4096]{1,0:T(8,128)(2,1)}, bf16[128,4096]{1,0:T(8,128)(2,1)S(1)}, u32[]{:S(2)}, u32[]{:S(2)}) collective-permute-start(bf16[128,4096]{1,0:T(8,128)(2,1)} %collective-permute-done.refs_2_), channel_id=1, source_target_pairs={{0,4},{1,5},{2,6},{3,7},{4,8},{5,9},{6,10},{7,11},{8,12},{9,13},{1... | collective-permute-start | bytes 3145736 | tf_op jit(solution)/shard_map/ppermute | solution.py:59
  40.8 1.6 copy-start.2
  42.4 4.9 %copy-start = (bf16[512,4096]{1,0:T(8,128)(2,1)S(1)}, bf16[512,4096]{1,0:T(8,128)(2,1)}, u32[]{:S(2)}) copy-start(bf16[512,4096]{1,0:T(8,128)(2,1)} %refs_5_.1) | copy-start | bytes 12582916
  42.4 4.9 %copy-start.9 = (bf16[128,4096]{1,0:T(8,128)(2,1)S(1)}, bf16[128,4096]{1,0:T(8,128)(2,1)}, u32[]{:S(2)}) copy-start(bf16[128,4096]{1,0:T(8,128)(2,1)} %refs_0_.2) | copy-start | bytes 3145732
  47.3 24.8 %copy-start.3 = (bf16[512,2048]{1,0:T(8,128)(2,1)}, bf16[512,2048]{1,0:T(8,128)(2,1)S(1)}, u32[]{:S(2)}) copy-start(bf16[512,2048]{1,0:T(8,128)(2,1)S(1)} %hidden.1.refs_8_.refs_6_.refs_4_) | copy-start | bytes 6291460
  60.6 6.9 %copy-start.14 = (f32[16,4096]{1,0:T(8,128)S(1)}, f32[16,4096]{1,0:T(8,128)}, u32[]{:S(2)}) copy-start(f32[16,4096]{1,0:T(8,128)} %get-tuple-element.62) | copy-start | bytes 786436
  61.9 21.7 %collective-permute-start.16 = (bf16[64,4096]{1,0:T(8,128)(2,1)S(1)}, bf16[64,4096]{1,0:T(8,128)(2,1)S(1)}, u32[]{:S(2)}, u32[]{:S(2)}) collective-permute-start(bf16[64,4096]{1,0:T(8,128)(2,1)S(1)} %slice_select_fusion), channel_id=1, source_target_pairs={{0,12},{1,13},{2,14},{3,15},{4,0},{5,1},{6,2},{7,3},{8,4},{9,5},{1... | collective-permute-start | bytes 1572872 | tf_op jit(solution)/shard_map/ppermute | solution.py:59
  65.2 6.9 %collective-permute-start.6 = (bf16[128,4096]{1,0:T(8,128)(2,1)S(1)}, bf16[128,4096]{1,0:T(8,128)(2,1)S(1)}, u32[]{:S(2)}, u32[]{:S(2)}) collective-permute-start(bf16[128,4096]{1,0:T(8,128)(2,1)S(1)} %collective-permute-done.3.refs_1_), channel_id=1, source_target_pairs={{0,1},{1,0},{2,3},{3,2},{4,5},{5,4},{6,7},{7,6},{8,9},{9,8},{10,11... | collective-permute-start | bytes 3145736 | tf_op jit(solution)/shard_map/ppermute | solution.py:59
  65.2 4.2 %collective-permute-start.7 = (bf16[128,4096]{1,0:T(8,128)(2,1)S(1)}, bf16[128,4096]{1,0:T(8,128)(2,1)S(1)}, u32[]{:S(2)}, u32[]{:S(2)}) collective-permute-start(bf16[128,4096]{1,0:T(8,128)(2,1)S(1)} %collective-permute-done.4.refs_2_), channel_id=1, source_target_pairs={{0,1},{1,0},{2,3},{3,2},{4,5},{5,4},{6,7},{7,6},{8,9},{9,8},{10,11... | collective-permute-start | bytes 3145736 | tf_op jit(solution)/shard_map/ppermute | solution.py:59
  67.4 4.7 %collective-permute-start.5 = (bf16[128,4096]{1,0:T(8,128)(2,1)S(1)}, bf16[128,4096]{1,0:T(8,128)(2,1)S(1)}, u32[]{:S(2)}, u32[]{:S(2)}) collective-permute-start(bf16[128,4096]{1,0:T(8,128)(2,1)S(1)} %collective-permute-done.1.refs_0_), channel_id=1, source_target_pairs={{0,1},{1,0},{2,3},{3,2},{4,5},{5,4},{6,7},{7,6},{8,9},{9,8},{10,11... | collective-permute-start | bytes 3145736 | tf_op jit(solution)/shard_map/ppermute | solution.py:59
  67.5 16.3 %collective-permute-start.15 = (bf16[64,4096]{1,0:T(8,128)(2,1)S(1)}, bf16[64,4096]{1,0:T(8,128)(2,1)S(1)}, u32[]{:S(2)}, u32[]{:S(2)}) collective-permute-start(bf16[64,4096]{1,0:T(8,128)(2,1)S(1)} %slice_select_fusion.1), channel_id=1, source_target_pairs={{0,4},{1,5},{2,6},{3,7},{4,8},{5,9},{6,10},{7,11},{8,12},{9,13},{1... | collective-permute-start | bytes 1572872 | tf_op jit(solution)/shard_map/ppermute | solution.py:59
  69.3 23.6 %collective-permute-start.19 = (f32[48,4096]{1,0:T(8,128)S(1)}, f32[48,4096]{1,0:T(8,128)S(1)}, u32[]{:S(2)}, u32[]{:S(2)}) collective-permute-start(f32[48,4096]{1,0:T(8,128)S(1)} %maximum_select_fusion), channel_id=1, source_target_pairs={{16,0},{17,1},{18,2},{19,3},{20,4},{21,5},{22,6},{23,7},{24,8},{25... | collective-permute-start | bytes 2359304 | tf_op jit(solution)/shard_map/ppermute | solution.py:59
  82.3 10.6 %copy-start.4 = (bf16[512,2048]{1,0:T(8,128)(2,1)S(1)}, bf16[512,2048]{1,0:T(8,128)(2,1)}, u32[]{:S(2)}) copy-start(bf16[512,2048]{1,0:T(8,128)(2,1)} %copy-done.3) | copy-start | bytes 6291460
  83.6 9.3 %collective-permute-start.18 = (bf16[64,4096]{1,0:T(8,128)(2,1)S(1)}, bf16[64,4096]{1,0:T(8,128)(2,1)S(1)}, u32[]{:S(2)}, u32[]{:S(2)}) collective-permute-start(bf16[64,4096]{1,0:T(8,128)(2,1)S(1)} %broadcast_select_fusion.1.refs_1_), channel_id=1, source_target_pairs={{0,1},{1,0},{2,3},{3,2},{4,5},{5,4},{6,7},{7,6},{8,9},{9,8},{10,11... | collective-permute-start | bytes 1572872 | tf_op jit(solution)/shard_map/ppermute | solution.py:59
  83.8 9.1 %collective-permute-start.17 = (bf16[64,4096]{1,0:T(8,128)(2,1)S(1)}, bf16[64,4096]{1,0:T(8,128)(2,1)S(1)}, u32[]{:S(2)}, u32[]{:S(2)}) collective-permute-start(bf16[64,4096]{1,0:T(8,128)(2,1)S(1)} %broadcast_select_fusion.2.refs_0_), channel_id=1, source_target_pairs={{0,1},{1,0},{2,3},{3,2},{4,5},{5,4},{6,7},{7,6},{8,9},{9,8},{10,11... | collective-permute-start | bytes 1572872 | tf_op jit(solution)/shard_map/ppermute | solution.py:59
  100.0 27.2 %collective-permute-start.23 = (s16[256,2176]{1,0:T(8,128)(2,1)S(1)}, s16[256,2176]{1,0:T(8,128)(2,1)S(1)}, u32[]{:S(2)}, u32[]{:S(2)}) collective-permute-start(s16[256,2176]{1,0:T(8,128)(2,1)S(1)} %get-tuple-element.40), channel_id=1, source_target_pairs={{0,64},{1,65},{2,66},{3,67},{4,68},{5,69},{6,70},{7,71},{8,72},{9,... | collective-permute-start | bytes 3342344 | tf_op jit(solution)/shard_map/ppermute | solution.py:59
  100.1 25.6 %collective-permute-start.20 = (s16[128,2176]{1,0:T(8,128)(2,1)S(1)}, s16[128,2176]{1,0:T(8,128)(2,1)S(1)}, u32[]{:S(2)}, u32[]{:S(2)}) collective-permute-start(s16[128,2176]{1,0:T(8,128)(2,1)S(1)} %get-tuple-element.37), channel_id=1, source_target_pairs={{0,16},{1,17},{2,18},{3,19},{4,20},{5,21},{6,22},{7,23},{8,24},{9,... | collective-permute-start | bytes 1671176 | tf_op jit(solution)/shard_map/ppermute | solution.py:59
  100.2 27.0 %collective-permute-start.21 = (s16[128,2176]{1,0:T(8,128)(2,1)S(1)}, s16[128,2176]{1,0:T(8,128)(2,1)S(1)}, u32[]{:S(2)}, u32[]{:S(2)}) collective-permute-start(s16[128,2176]{1,0:T(8,128)(2,1)S(1)} %get-tuple-element.38), channel_id=1, source_target_pairs={{0,48},{1,49},{2,50},{3,51},{4,52},{5,53},{6,54},{7,55},{8,56},{9,... | collective-permute-start | bytes 1671176 | tf_op jit(solution)/shard_map/ppermute | solution.py:59
  102.2 25.0 %collective-permute-start.22 = (s16[128,2176]{1,0:T(8,128)(2,1)S(1)}, s16[128,2176]{1,0:T(8,128)(2,1)S(1)}, u32[]{:S(2)}, u32[]{:S(2)}) collective-permute-start(s16[128,2176]{1,0:T(8,128)(2,1)S(1)} %get-tuple-element.39), channel_id=1, source_target_pairs={{0,32},{1,33},{2,34},{3,35},{4,36},{5,37},{6,38},{7,39},{8,40},{9,... | collective-permute-start | bytes 1671176 | tf_op jit(solution)/shard_map/ppermute | solution.py:59
  102.4 7.1 %copy-start.5 = (f32[1,96,4096]{2,1,0:T(8,128)S(1)}, f32[1,96,4096]{2,1,0:T(8,128)}, u32[]{:S(2)}) copy-start(f32[1,96,4096]{2,1,0:T(8,128)} %refs_0_.3) | copy-start | bytes 4718596
  102.4 7.1 %copy-start.6 = (f32[1,96,4096]{2,1,0:T(8,128)S(1)}, f32[1,96,4096]{2,1,0:T(8,128)}, u32[]{:S(2)}) copy-start(f32[1,96,4096]{2,1,0:T(8,128)} %refs_2_.1) | copy-start | bytes 4718596
  102.4 7.1 %copy-start.7 = (f32[1,96,4096]{2,1,0:T(8,128)S(1)}, f32[1,96,4096]{2,1,0:T(8,128)}, u32[]{:S(2)}) copy-start(f32[1,96,4096]{2,1,0:T(8,128)} %refs_1_.1) | copy-start | bytes 4718596
  102.4 7.1 %copy-start.11 = (s32[1,9]{1,0:T(1,128)S(1)}, s32[1,9]{1,0:T(1,128)}, u32[]{:S(2)}) copy-start(s32[1,9]{1,0:T(1,128)} %old_ref.3) | copy-start | bytes 112
  102.5 7.1 %copy-start.12 = (s32[1,9]{1,0:T(1,128)S(1)}, s32[1,9]{1,0:T(1,128)}, u32[]{:S(2)}) copy-start(s32[1,9]{1,0:T(1,128)} %new_ref.3) | copy-start | bytes 112
  106.2 1.3 collective-permute-start.24
  107.4 18.3 %collective-permute-start.25 = (f32[16,1,128]{2,1,0:T(1,128)S(1)}, f32[16,1,128]{2,1,0:T(1,128)S(1)}, u32[]{:S(2)}, u32[]{:S(2)}) collective-permute-start(f32[16,1,128]{2,1,0:T(1,128)S(1)} %add.257), channel_id=1, source_target_pairs={{0,2},{1,3},{2,0},{3,1},{4,6},{5,7},{6,4},{7,5},{8,10},{9,11},{10,... | collective-permute-start | bytes 24584 | tf_op jit(solution)/shard_map/ppermute | solution.py:59
  129.4 13.7 %collective-permute-start.26 = (s16[64,2176]{1,0:T(8,128)(2,1)S(1)}, s16[64,2176]{1,0:T(8,128)(2,1)S(1)}, u32[]{:S(2)}, u32[]{:S(2)}) collective-permute-start(s16[64,2176]{1,0:T(8,128)(2,1)S(1)} %get-tuple-element.45), channel_id=1, source_target_pairs={{0,64},{1,65},{2,66},{3,67},{4,68},{5,69},{6,70},{7,71},{8,72},{9,... | collective-permute-start | bytes 835592 | tf_op jit(solution)/shard_map/ppermute | solution.py:59
  131.0 12.1 %collective-permute-start.27 = (s16[64,2176]{1,0:T(8,128)(2,1)S(1)}, s16[64,2176]{1,0:T(8,128)(2,1)S(1)}, u32[]{:S(2)}, u32[]{:S(2)}) collective-permute-start(s16[64,2176]{1,0:T(8,128)(2,1)S(1)} %get-tuple-element.46), channel_id=1, source_target_pairs={{0,16},{1,17},{2,18},{3,19},{4,20},{5,21},{6,22},{7,23},{8,24},{9,... | collective-permute-start | bytes 835592 | tf_op jit(solution)/shard_map/ppermute | solution.py:59
  132.5 13.3 %collective-permute-start.28 = (s16[64,2176]{1,0:T(8,128)(2,1)S(1)}, s16[64,2176]{1,0:T(8,128)(2,1)S(1)}, u32[]{:S(2)}, u32[]{:S(2)}) collective-permute-start(s16[64,2176]{1,0:T(8,128)(2,1)S(1)} %get-tuple-element.47), channel_id=1, source_target_pairs={{0,48},{1,49},{2,50},{3,51},{4,52},{5,53},{6,54},{7,55},{8,56},{9,... | collective-permute-start | bytes 835592 | tf_op jit(solution)/shard_map/ppermute | solution.py:59
  133.1 12.7 %collective-permute-start.29 = (s16[64,2176]{1,0:T(8,128)(2,1)S(1)}, s16[64,2176]{1,0:T(8,128)(2,1)S(1)}, u32[]{:S(2)}, u32[]{:S(2)}) collective-permute-start(s16[64,2176]{1,0:T(8,128)(2,1)S(1)} %get-tuple-element.48), channel_id=1, source_target_pairs={{0,32},{1,33},{2,34},{3,35},{4,36},{5,37},{6,38},{7,39},{8,40},{9,... | collective-permute-start | bytes 835592 | tf_op jit(solution)/shard_map/ppermute | solution.py:59
  145.8 1.6 copy-start.8
  148.3 8.3 %collective-permute-start.30 = (f32[16,4096]{1,0:T(8,128)S(1)}, f32[16,4096]{1,0:T(8,128)S(1)}, u32[]{:S(2)}, u32[]{:S(2)}) collective-permute-start(f32[16,4096]{1,0:T(8,128)S(1)} %get-tuple-element.53), channel_id=1, source_target_pairs={{0,16},{1,17},{2,18},{3,19},{4,20},{5,21},{6,22},{7,23},{8,24},{9,... | collective-permute-start | bytes 786440 | tf_op jit(solution)/shard_map/ppermute | solution.py:59
  150.6 10.4 %collective-permute-start.31 = (f32[16,4096]{1,0:T(8,128)S(1)}, f32[16,4096]{1,0:T(8,128)S(1)}, u32[]{:S(2)}, u32[]{:S(2)}) collective-permute-start(f32[16,4096]{1,0:T(8,128)S(1)} %get-tuple-element.54), channel_id=1, source_target_pairs={{16,0},{17,1},{18,2},{19,3},{20,4},{21,5},{22,6},{23,7},{24,8},{25... | collective-permute-start | bytes 786440 | tf_op jit(solution)/shard_map/ppermute | solution.py:59
